TPU v7x, 32 devices: a whole 2x2x4 slice. The times are simulated.
32 devices in a mesh: dp: 2 (over core), fsdp: 16 (over z, y, x).
Axes of the slice: x: 2, y: 2, z: 4, core: 2. Of those that a mesh axis runs over, the one named last changes fastest.
Arguments:
- tokens: bfloat16 [64, 392, 768], P(('dp', 'fsdp')), may hold values from -6 to 6
- positions: int32 [64, 392], P(('dp', 'fsdp')), may hold values from 0 to 1567, as said below
- counts: int32 [64], P(('dp', 'fsdp')), may hold values from 78 to 392, as said below
- cotangent: bfloat16 [64, 392, 768], P(('dp', 'fsdp')), may hold values from -6 to 6
- qkv_weight: float32 [768, 2304], P('fsdp'), may hold values from -0.21875 to 0.21875
- out_weight: float32 [768, 768], P('fsdp'), may hold values from -3.5 to 3.5
- up_weight: float32 [768, 3072], P('fsdp'), may hold values from -0.21875 to 0.21875
- down_weight: float32 [3072, 768], P('fsdp'), may hold values from -0.109375 to 0.109375
- small_params: float32 [768, 12], P('fsdp'), may hold values from -2 to 2
- qkv_momentum: float32 [768, 2304], P('fsdp'), may hold values from -256 to 256
- out_momentum: float32 [768, 768], P('fsdp'), may hold values from -48 to 48
- up_momentum: float32 [768, 3072], P('fsdp'), may hold values from -384 to 384
- down_momentum: float32 [3072, 768], P('fsdp'), may hold values from -384 to 384
- small_momentum: float32 [768, 12], P('fsdp'), may hold values from -512 to 512
- qkv_average: float32 [768, 2304], P('fsdp'), may hold values from -0.21875 to 0.21875
- out_average: float32 [768, 768], P('fsdp'), may hold values from -3.5 to 3.5
- up_average: float32 [768, 3072], P('fsdp'), may hold values from -0.21875 to 0.21875
- down_average: float32 [3072, 768], P('fsdp'), may hold values from -0.109375 to 0.109375
- small_average: float32 [768, 12], P('fsdp'), may hold values from -6 to 6
Outputs:
- block_out: bfloat16 [64, 392, 768], P(('dp', 'fsdp'))
- token_grad: float32 [64, 392, 768], P(('dp', 'fsdp'))
- new_qkv_weight: float32 [768, 2304], P('fsdp')
- new_out_weight: float32 [768, 768], P('fsdp')
- new_up_weight: float32 [768, 3072], P('fsdp')
- new_down_weight: float32 [3072, 768], P('fsdp')
- new_small_params: float32 [768, 12], P('fsdp')
- new_qkv_momentum: float32 [768, 2304], P('fsdp')
- new_out_momentum: float32 [768, 768], P('fsdp')
- new_up_momentum: float32 [768, 3072], P('fsdp')
- new_down_momentum: float32 [3072, 768], P('fsdp')
- new_small_momentum: float32 [768, 12], P('fsdp')
- new_qkv_average: float32 [768, 2304], P('fsdp')
- new_out_average: float32 [768, 768], P('fsdp')
- new_up_average: float32 [768, 3072], P('fsdp')
- new_down_average: float32 [3072, 768], P('fsdp')
- new_small_average: float32 [768, 12], P('fsdp')
- norms: float32 [10], replicated
Inputs may be any that keep to these rules, and one draw needn't show every extreme that they name: `counts`: some clip has exactly 392 visible tubelets and some exactly 78. The 392 positions of a clip are distinct; rows at and after a clip's count are padding.
All inputs are finite; a program needn't handle non-finite values.
Results may differ from a plain program's by a relative error of at most 0.012.
The roundings to bfloat16 on the way count: a program that leaves them out, or rounds other values in their place, can miss the bound.
Values may be sent and summed in bfloat16 or wider, within the bound.
No kernel may reach another device: no remote copies, remote signals or barrier semaphores. Data moves between devices by JAX's collectives and lax.ppermute only.
A program may use at most 256 MiB of HBM per device.

v0:
```python
import math

import jax
import jax.numpy as jnp
import numpy as np
from jax import lax
from jax.experimental import pallas as pl
from jax.experimental.pallas import tpu as pltpu
from jax.sharding import PartitionSpec as P

HEAD_DIM = 64
EPS_NORM = 1e-06
MOMENTUM_DECAY = 0.9
WEIGHT_DECAY = 0.0001
TRUST_RATE = 0.2
AVERAGE_DECAY = 0.8
NEG = -1000000000.0
LEAST = 60

BF = jnp.bfloat16
F32 = jnp.float32
AXES = ("dp", "fsdp")
SHORT = pl.CostEstimate(flops=1, bytes_accessed=1, transcendentals=0)
ANY = pl.BlockSpec(memory_space=pl.ANY)
SMEM = pl.BlockSpec(memory_space=pltpu.SMEM)


def params(mib):
    return pltpu.CompilerParams(
        vmem_limit_bytes=max(mib, LEAST) * 1024 * 1024, dimension_semantics=("arbitrary",)
    )


def dot(a, b):
    return lax.dot_general(a, b, (((1,), (0,)), ((), ())), preferred_element_type=F32)


def dot_nt(a, b):
    return lax.dot_general(a, b, (((1,), (1,)), ((), ())), preferred_element_type=F32)


def dot_tn(a, b):
    return lax.dot_general(a, b, (((0,), (0,)), ((), ())), preferred_element_type=F32)


def whole(shape):
    zeros = (0,) * len(shape)
    return pl.BlockSpec(shape, lambda *i: zeros)


class Links:
    def __init__(self, dp, fsdp):
        self.paired = dp == 2 and fsdp == 16
        self.bits = ((4, 4), (8, 8), (1, 2), (2, 1))

    def masks(self):
        table = np.zeros((2, 16), np.int32)
        for core in range(2):
            for p in range(16):
                for bit in range(4):
                    if p >> bit & 1:
                        table[core, p] ^= self.bits[bit][core]
        return table

    def flip(self, x, p):
        table = self.masks()
        pairs = [(c * 16 + f, c * 16 + (f ^ int(table[c, p]))) for c in range(2) for f in range(16)]
        return lax.ppermute(x, AXES, pairs)

    def cross(self, x):
        pairs = [(c * 16 + f, (1 - c) * 16 + f) for c in range(2) for f in range(16)]
        return lax.ppermute(x, AXES, pairs)

    def along_z(self, blocks):
        return [self.flip(block, p) for p, block in zip((1, 2, 3), blocks)]

    def sum_all(self, x):
        x = x + self.cross(x)
        for step in (1, 4):
            one, two, three = [self.flip(x, step * p) for p in (1, 2, 3)]
            x = (x + one) + (two + three)
        return x


def assemble(pieces, order, rows, target, sems, at=0, columns=None):
    copies = []
    n = 0
    for piece in pieces:
        for j in range(piece.shape[0]):
            source = piece.at[j] if columns is None else piece.at[j, :, columns]
            start = pl.multiple_of(order(n) * rows, 16)
            copies.append(
                pltpu.make_async_copy(source, target.at[pl.ds(start, rows)], sems.at[at + n])
            )
            n += 1
    return copies


def deliver(source, order, rows, first, targets, sems, at=0, columns=None):
    copies = []
    n = first
    for target in targets:
        for j in range(target.shape[0]):
            start = pl.multiple_of(order(n) * rows, 16)
            place = target.at[j] if columns is None else target.at[j, :, columns]
            copies.append(
                pltpu.make_async_copy(source.at[pl.ds(start, rows)], place, sems.at[at + n - first])
            )
            n += 1
    return copies


def run_all(copies):
    for copy in copies:
        copy.start()
    for copy in copies:
        copy.wait()


def norm_parts(values):
    center = values - jnp.mean(values, axis=-1, keepdims=True)
    inv = lax.rsqrt(jnp.mean(center * center, axis=-1, keepdims=True) + EPS_NORM)
    return center * inv, inv


def norm_back(u, hat, inv):
    first = jnp.mean(u, axis=-1, keepdims=True)
    second = jnp.mean(u * hat, axis=-1, keepdims=True)
    return inv * (u - first - hat * second)


def embed_kernel(each, n_groups):
    def kernel(table, *refs):
        toks, poss = refs[:n_groups], refs[n_groups : 2 * n_groups]
        embed = refs[-1]
        step = pl.program_id(0)
        p = choose(poss, step, each)
        turns = p * table[0:1, :]
        turns = turns - jnp.round(turns)
        turns = turns + (p * table[1:2, :] + table[2:3, :])
        turns = turns - jnp.round(turns)
        fold = jnp.where(turns > 0.25, 0.5 - turns, jnp.where(turns < -0.25, -0.5 - turns, turns))
        x = fold * (2.0 * math.pi)
        x2 = x * x
        poly = -1.0 / 39916800.0
        for coef in (1.0 / 362880.0, -1.0 / 5040.0, 1.0 / 120.0, -1.0 / 6.0, 1.0):
            poly = poly * x2 + coef
        embed[0] = choose(toks, step, each).astype(F32) + x * poly

    return kernel


def embed_rows(tokens, positions):
    each, length, width = tokens[0].shape
    exact = 10000.0 ** (-2.0 * (np.arange(width) // 2) / width) / (2.0 * math.pi)
    scale = 2.0 ** (11 - np.floor(np.log2(exact)))
    high = np.round(exact * scale) / scale
    table = np.zeros((8, width), np.float32)
    table[0], table[1], table[2] = high, exact - high, 0.25 * (np.arange(width) % 2)
    specs, clips = pair_specs(tokens, (length, width))
    pos_specs, _ = pair_specs(positions, (length, 1))
    size = clips * length * width
    return pl.pallas_call(
        embed_kernel(each, len(tokens)),
        grid=(clips,),
        in_specs=[whole((8, width))] + specs + pos_specs,
        out_specs=pl.BlockSpec((1, length, width), lambda i: (i, 0, 0)),
        out_shape=jax.ShapeDtypeStruct((clips, length, width), F32),
        compiler_params=params(24),
        cost_estimate=SHORT,
        name="embed_rows",
    )(jnp.asarray(table), *tokens, *positions)


def pair_specs(groups, block, column=0):
    specs, first = [], 0
    for array in groups:
        n = array.shape[0]

        def index(*at, first=first, n=n):
            return (jnp.clip(at[-1] - first, 0, n - 1), 0, column)

        specs.append(pl.BlockSpec((1,) + block, index))
        first += n
    return specs, first


def choose(refs, step, each):
    value = refs[0][0]
    for k in range(1, len(refs)):
        value = jnp.where(step >= k * each, refs[k][0], value)
    return value


def attend_forward(
    sources, small, order, core, counts, pieces, rows, each, first, heads, apart, block
):
    length, width = sources[0].shape[1:]
    source_each, n_sources = sources[0].shape[0], len(sources)
    source_specs, clips = pair_specs(sources, (length, width))
    part = heads * HEAD_DIM
    columns = 3 * part
    fresh = sources[0].dtype == F32
    gathered = small is None
    total_columns = columns + (128 if gathered else 0)
    split = clips > each
    n_pieces = len(pieces)
    blocks = sum(piece.shape[0] for piece in pieces)
    smalls = [] if gathered else [small]

    def kernel(order_ref, core_ref, count_ref, *refs):
        source_refs = refs[:n_sources]
        refs = list(refs[n_sources:])
        small_in = None if gathered else refs.pop(0)
        piece_refs = refs[:n_pieces]
        refs = refs[n_pieces:]
        vectors = refs.pop(0) if gathered else small_in
        normed = refs.pop(0) if fresh else None
        qkv, logs, mixes = refs[0], refs[1], refs[2 : 4 if split else 3]
        weight, bias, sems = refs[-3:]
        step = pl.program_id(0)

        @pl.when(step == 0)
        def _():
            cut = slice(columns * block, columns * block + columns)
            target = weight.at[:, :columns]
            copies = assemble(piece_refs, lambda n: order_ref[n], rows, target, sems, 0, cut)
            if gathered:
                last = piece_refs[0].shape[2]
                target = weight.at[:, columns:]
                cut = slice(last - 128, last)
                copies += assemble(
                    piece_refs, lambda n: order_ref[n], rows, target, sems, blocks, cut
                )
            run_all(copies)
            if gathered:
                vectors[...] = weight[:, columns:].astype(F32).T[:16]
            bias[...] = jnp.zeros_like(bias)
            for pair in range(heads // 2):
                head = first + core_ref[0] * apart + 2 * pair
                at = pl.ds(pl.multiple_of(head * HEAD_DIM, 128), 128)
                bias[0:1, 384 * pair : 384 * pair + 128] = vectors[4:5, at]
                bias[0:1, 384 * pair + 256 : 384 * pair + 384] = vectors[5:6, at]

        if fresh:
            hat, _ = norm_parts(choose(source_refs, step, source_each))
            x = (hat * vectors[0:1, :] + vectors[1:2, :]).astype(BF)
            normed[0] = x
        else:
            x = choose(source_refs, step, source_each)
        low = (dot(x, weight[:, :columns]) + bias[0:1, :]).astype(BF)
        qkv[0] = low
        valid = lax.broadcasted_iota(jnp.int32, (length, 1), 0) < count_ref[step]
        lane = lax.broadcasted_iota(jnp.int32, (1, 2 * HEAD_DIM), 1)
        outs, log_rows = [], []
        for pair in range(heads // 2):
            at = 384 * pair
            q = low[:, at : at + 128] * jnp.asarray(HEAD_DIM**-0.5, BF)
            k = low[:, at + 128 : at + 256]
            v = low[:, at + 256 : at + 384]
            mixed_heads = []
            for half in range(2):
                mine = (lane >= HEAD_DIM) if half else (lane < HEAD_DIM)
                s = dot_nt(jnp.where(mine, k, jnp.zeros_like(k)), q)
                s = jnp.where(valid, s, NEG)
                top = jnp.max(s, axis=0, keepdims=True)
                e = jnp.exp(s - top)
                total = jnp.sum(e, axis=0, keepdims=True)
                p = (e * (1.0 / total)).astype(BF)
                mixed_heads.append(dot_tn(p, v))
                log_rows.append(top + jnp.log(total))
            outs.append(jnp.where(lane < HEAD_DIM, mixed_heads[0], mixed_heads[1]))
        mixed = jnp.concatenate(outs, axis=1).astype(BF)
        logs[0] = jnp.concatenate(log_rows, axis=0)
        if split:

            @pl.when(step < each)
            def _():
                mixes[0][0] = mixed

            @pl.when(step >= each)
            def _():
                mixes[1][0] = mixed

        else:
            mixes[0][0] = mixed

    clip = lambda c: pl.BlockSpec((1, length, c), lambda i: (i, 0, 0))
    own = pl.BlockSpec((1, length, part), lambda i: (jnp.minimum(i, each - 1), 0, 0))
    other = pl.BlockSpec((1, length, part), lambda i: (jnp.clip(i - each, 0, each - 1), 0, 0))
    out_specs, out_shapes = [], []
    if gathered:
        out_specs.append(whole((16, width)))
        out_shapes.append(jax.ShapeDtypeStruct((16, width), F32))
    if fresh:
        out_specs.append(clip(width))
        out_shapes.append(jax.ShapeDtypeStruct((clips, length, width), BF))
    out_specs += [clip(columns), pl.BlockSpec((1, heads, length), lambda i: (i, 0, 0)), own]
    out_shapes += [
        jax.ShapeDtypeStruct((clips, length, columns), BF),
        jax.ShapeDtypeStruct((clips, heads, length), F32),
        jax.ShapeDtypeStruct((each, length, part), BF),
    ]
    if split:
        out_specs.append(other)
        out_shapes.append(jax.ShapeDtypeStruct((clips - each, length, part), BF))
    n_rows = clips * length
    return pl.pallas_call(
        kernel,
        grid=(clips,),
        in_specs=[SMEM, SMEM, SMEM]
        + source_specs
        + [whole((16, width))] * len(smalls)
        + [ANY] * n_pieces,
        out_specs=out_specs,
        out_shape=out_shapes,
        scratch_shapes=[
            pltpu.VMEM((width, total_columns), BF),
            pltpu.VMEM((8, columns), F32),
            pltpu.SemaphoreType.DMA((2 * blocks,)),
        ],
        compiler_params=params(48),
        cost_estimate=SHORT,
        name="attend_forward",
    )(order, core, counts, *sources, *smalls, *pieces)


def out_weight_copies(own, other, meta, rows, weight, sems):
    cut = slice(own[0].shape[2] - weight.shape[2], None)
    if other is None:
        return assemble(own, lambda n: meta[1 + n], rows, weight.at[0], sems, 0, cut)
    core = meta[0]
    copies = assemble(own, lambda n: meta[1 + n], rows, weight.at[core], sems, 0, cut)
    return copies + assemble(other, lambda n: meta[17 + n], rows, weight.at[1 - core], sems, 16)


def project_norm(mixes, places, embed, small, meta, pieces, others, rows):
    n, length, width = mixes[0].shape[0], embed.shape[1], embed.shape[2]
    parts = [mix.shape[2] for mix in mixes]
    n_mix, n_p, n_o = len(mixes), len(pieces), len(others)
    halves = 2 if others else 1
    half_width = width // halves

    def kernel(meta_ref, small_ref, embed_ref, *refs):
        mix_refs = refs[:n_mix]
        own_refs = refs[n_mix : n_mix + n_p]
        other_refs = refs[n_mix + n_p : n_mix + n_p + n_o] or None
        resid, mlp_in, weight, sems = refs[n_mix + n_p + n_o :]

        @pl.when(pl.program_id(0) == 0)
        def _():
            run_all(out_weight_copies(own_refs, other_refs, meta_ref, rows, weight, sems))

        outs = []
        for half in range(halves):
            total = 0.0
            for k, mix in enumerate(mix_refs):
                flip, first = places[k]
                at = first
                if halves > 1:
                    at = pl.multiple_of((meta_ref[0] ^ flip) * half_width + first, 128)
                total = total + dot(mix[0], weight[half, pl.ds(at, parts[k]), :])
            outs.append(total)
        total = jnp.concatenate(outs, axis=1) if halves > 1 else outs[0]
        values = embed_ref[0] + total + small_ref[6:7, :]
        resid[0] = values
        hat, _ = norm_parts(values)
        mlp_in[0] = (hat * small_ref[2:3, :] + small_ref[3:4, :]).astype(BF)

    clip = pl.BlockSpec((1, length, width), lambda i: (i, 0, 0))
    mix_specs = [pl.BlockSpec((1, length, c), lambda i: (i, 0, 0)) for c in parts]
    size = n * length * width
    return pl.pallas_call(
        kernel,
        grid=(n,),
        in_specs=[SMEM, whole((16, width)), clip] + mix_specs + [ANY] * (n_p + n_o),
        out_specs=[clip, clip],
        out_shape=[
            jax.ShapeDtypeStruct((n, length, width), F32),
            jax.ShapeDtypeStruct((n, length, width), BF),
        ],
        scratch_shapes=[
            pltpu.VMEM((halves, width, half_width), BF),
            pltpu.SemaphoreType.DMA((32,)),
        ],
        compiler_params=params(24),
        cost_estimate=SHORT,
        name="project_norm",
    )(meta, small, embed, *mixes, *pieces, *others)


def mlp_both(groups, cots, order, counts, bias, pieces, rows, relative):
    each, length, width = groups[0].shape
    hidden = bias.shape[1]
    n_groups, n_pieces = len(groups), len(pieces)
    n_blocks = sum(piece.shape[0] for piece in pieces)
    hidden_rows = hidden // n_blocks
    specs, clips = pair_specs(groups, (length, width))
    if relative:
        half = n_blocks // 2
        grad_shapes = [
            jax.ShapeDtypeStruct((half, rows, 2 * width), F32),
            jax.ShapeDtypeStruct((half, rows, 2 * width), BF),
        ]
    else:
        grad_shapes = [
            jax.ShapeDtypeStruct((1, width, hidden), F32),
            jax.ShapeDtypeStruct((1, hidden, width), F32),
        ]
    own_shape = (each, length, width)
    out_shapes = [jax.ShapeDtypeStruct(own_shape, F32)] * 2
    if n_groups > 1:
        out_shapes += [jax.ShapeDtypeStruct(own_shape, BF)] * 2
    out_shapes += [jax.ShapeDtypeStruct((1, hidden), F32)]

    def kernel(order_ref, count_ref, bias_ref, *refs):
        ins = refs[:n_groups]
        cot_refs = refs[n_groups : 2 * n_groups]
        piece_refs = refs[2 * n_groups : 2 * n_groups + n_pieces]
        outs = refs[2 * n_groups + n_pieces :]
        own_out, own_dm = outs[0], outs[1]
        sent = outs[2:4] if n_groups > 1 else None
        n_out = 4 if n_groups > 1 else 2
        bias_grad = outs[n_out]
        grad_a, grad_b = outs[n_out + 1 : n_out + 3]
        (up, down, g_up, g_down, low_up, low_down, sems) = outs[n_out + 3 :]
        i = pl.program_id(0)
        place = lambda n: order_ref[n]

        @pl.when(i == 0)
        def _():
            copies = assemble(piece_refs, place, rows, up, sems, 0, slice(0, hidden))
            if relative:
                copies += assemble(
                    piece_refs, place, hidden_rows, down, sems, n_blocks, slice(hidden, None)
                )
            else:
                copies = [
                    pltpu.make_async_copy(piece_refs[0].at[0], up, sems.at[0]),
                    pltpu.make_async_copy(piece_refs[1].at[0], down, sems.at[1]),
                ]
            run_all(copies)

        x = choose(ins, i, each)
        valid = lax.broadcasted_iota(jnp.int32, (length, 1), 0) < count_ref[i]
        cot = choose(cot_refs, i, each)
        dd = jnp.where(valid, cot, jnp.zeros_like(cot))
        pre = dot(x, up[...]) + bias_ref[...]
        cdf = 0.5 + 0.5 * lax.erf(pre * 0.7071067811865476)
        pdf = jnp.exp(pre * pre * -0.5) * 0.3989422804014327
        act = (pre * cdf).astype(BF)
        d_pre = (dot_nt(dd, down[...]) * (cdf + pre * pdf)).astype(BF)
        out = dot(act, down[...])
        dm = dot_nt(d_pre, up[...])
        up_part = dot(x.T, d_pre)
        down_part = dot(act.T, dd)
        bias_part = jnp.sum(d_pre.astype(F32), axis=0, keepdims=True)

        @pl.when(i < each)
        def _():
            own_out[0] = out
            own_dm[0] = dm

        if sent is not None:

            @pl.when(i >= each)
            def _():
                sent[0][0] = out.astype(BF)
                sent[1][0] = dm.astype(BF)

        @pl.when(i == 0)
        def _():
            g_up[...] = up_part
            g_down[...] = down_part
            bias_grad[...] = bias_part

        @pl.when((i > 0) & (i < clips - 1))
        def _():
            g_up[...] += up_part
            g_down[...] += down_part
            bias_grad[...] += bias_part

        @pl.when(i == clips - 1)
        def _():
            bias_grad[...] += bias_part
            if relative:
                total_up = g_up[...] + up_part
                g_up[...] = total_up
                low_up[...] = total_up.astype(BF)
                one, two = slice(0, width), slice(width, 2 * width)
                copies = deliver(g_up, place, rows, 0, [grad_a], sems, 0, one)
                copies += deliver(low_up, place, rows, half, [grad_b], sems, half, one)
                for copy in copies:
                    copy.start()
                total_down = g_down[...] + down_part
                g_down[...] = total_down
                low_down[...] = total_down.astype(BF)
                more = deliver(g_down, place, rows, 0, [grad_a], sems, 2 * half, two)
                more += deliver(low_down, place, rows, half, [grad_b], sems, 3 * half, two)
                for copy in more:
                    copy.start()
                for copy in copies + more:
                    copy.wait()
            else:
                g_up[...] += up_part
                g_down[...] += down_part
                copies = [
                    pltpu.make_async_copy(g_up, grad_a.at[0], sems.at[0]),
                    pltpu.make_async_copy(g_down, grad_b.at[0], sems.at[1]),
                ]
                run_all(copies)

    own_index = lambda i: (jnp.minimum(i, each - 1), 0, 0)
    sent_index = lambda i: (jnp.clip(i - each, 0, each - 1), 0, 0)
    out_specs = [pl.BlockSpec((1, length, width), own_index)] * 2
    if n_groups > 1:
        out_specs += [pl.BlockSpec((1, length, width), sent_index)] * 2
    out_specs += [whole((1, hidden)), ANY, ANY]
    low_shape = (width, hidden) if relative else (16, 128)
    low_shape_down = (hidden, width) if relative else (16, 128)
    n_rows = clips * length
    return pl.pallas_call(
        kernel,
        grid=(clips,),
        in_specs=[SMEM, SMEM, whole((1, hidden))] + specs + specs + [ANY] * n_pieces,
        out_specs=out_specs,
        out_shape=out_shapes + grad_shapes,
        scratch_shapes=[
            pltpu.VMEM((width, hidden), BF),
            pltpu.VMEM((hidden, width), BF),
            pltpu.VMEM((width, hidden), F32),
            pltpu.VMEM((hidden, width), F32),
            pltpu.VMEM(low_shape, BF),
            pltpu.VMEM(low_shape_down, BF),
            pltpu.SemaphoreType.DMA((max(2 * n_blocks, 2),)),
        ],
        compiler_params=params(56),
        cost_estimate=SHORT,
        name="mlp_both",
    )(order, counts, bias, *groups, *cots, *pieces)


def norm_two_back(dms, resid, cot, small, meta, counts, pieces, others, rows, part):
    n, length, width = resid.shape
    n_dm, n_p, n_o = len(dms), len(pieces), len(others)
    halves = 2 if others else 1
    half_width = width // halves

    def kernel(meta_ref, count_ref, small_ref, resid_ref, cot_ref, *refs):
        dm_refs = refs[:n_dm]
        own_refs = refs[n_dm : n_dm + n_p]
        other_refs = refs[n_dm + n_p : n_dm + n_p + n_o] or None
        outs = refs[n_dm + n_p + n_o :]
        mixes = outs[: halves]
        proj, d_resid, sums, weight, sems = outs[halves:]
        step = pl.program_id(0)

        @pl.when(step == 0)
        def _():
            run_all(out_weight_copies(own_refs, other_refs, meta_ref, rows, weight, sems))

        valid = lax.broadcasted_iota(jnp.int32, (length, 1), 0) < count_ref[step]
        dy = jnp.where(valid, cot_ref[0].astype(F32), 0.0)
        dm = dm_refs[0][0].astype(F32)
        for ref in dm_refs[1:]:
            dm = dm + ref[0].astype(F32)
        hat, inv = norm_parts(resid_ref[0])
        total = dy + norm_back(dm * small_ref[2:3, :], hat, inv)
        d_resid[0] = total
        low = total.astype(BF)
        proj[0] = low
        row = lambda v: jnp.sum(v, axis=0, keepdims=True)
        parts = jnp.concatenate(
            [row(dm * hat), row(dm), row(low.astype(F32)), row(dy), jnp.zeros((4, width), F32)]
        )
        for k in range(halves):
            at = pl.multiple_of((meta_ref[0] ^ k) * part, 128) if halves > 1 else 0
            value = 0.0
            for half in range(halves):
                cut = low[:, half * half_width : (half + 1) * half_width]
                value = value + dot_nt(cut, weight[half, pl.ds(at, part), :])
            mixes[k][0] = value.astype(BF)

        @pl.when(step == 0)
        def _():
            sums[...] = parts

        @pl.when(step > 0)
        def _():
            sums[...] += parts

    clip = pl.BlockSpec((1, length, width), lambda i: (i, 0, 0))
    mix_spec = pl.BlockSpec((1, length, part), lambda i: (i, 0, 0))
    shape = resid.shape
    mix_shape = jax.ShapeDtypeStruct((n, length, part), BF)
    return pl.pallas_call(
        kernel,
        grid=(n,),
        in_specs=[SMEM, SMEM, whole((16, width)), clip, clip]
        + [clip] * n_dm
        + [ANY] * (n_p + n_o),
        out_specs=[mix_spec] * halves + [clip, clip, whole((8, width))],
        out_shape=[mix_shape] * halves
        + [
            jax.ShapeDtypeStruct(shape, BF),
            jax.ShapeDtypeStruct(shape, F32),
            jax.ShapeDtypeStruct((8, width), F32),
        ],
        scratch_shapes=[
            pltpu.VMEM((halves, width, half_width), BF),
            pltpu.SemaphoreType.DMA((32,)),
        ],
        compiler_params=params(32),
        cost_estimate=SHORT,
        name="norm_two_back",
    )(meta, counts, small, resid, cot, *dms, *pieces, *others)


def out_weight_grad(mixes, places, proj, meta, rows):
    n, length, width = proj.shape
    parts = [mix.shape[2] for mix in mixes]
    n_mix = len(mixes)
    halves = 2 if any(flip for flip, _ in places) else 1
    half_width = width // halves
    blocks = width // rows

    def kernel(meta_ref, proj_ref, *refs):
        mix_refs = refs[:n_mix]
        if halves > 1:
            keep, send, total, low, sems = refs[n_mix:]
        else:
            keep, total, sems = refs[n_mix:]
        step = pl.program_id(0)

        @pl.when(step == 0)
        def _():
            total[...] = jnp.zeros_like(total)

        for k in range(n_mix):
            turned = mix_refs[k][0].T
            flip, at = places[k]
            if halves > 1:
                at = pl.multiple_of((meta_ref[0] ^ flip) * half_width + at, 128)
            for half in range(halves):
                cut = proj_ref[0, :, half * half_width : (half + 1) * half_width]
                total[half, pl.ds(at, parts[k]), :] += dot(turned, cut)

        @pl.when(step == n - 1)
        def _():
            if halves > 1:
                core = meta_ref[0]
                low[...] = total[1 - core].astype(BF)
                copies = deliver(
                    total.at[core], lambda n: meta_ref[1 + n], rows, 0, [keep], sems, 0
                )
                copies += deliver(low, lambda n: meta_ref[17 + n], rows, 0, [send], sems, blocks)
                run_all(copies)
            else:
                run_all([pltpu.make_async_copy(total, keep, sems.at[0])])

    clip = lambda c: pl.BlockSpec((1, length, c), lambda i: (i, 0, 0))
    if halves > 1:
        shapes = [
            jax.ShapeDtypeStruct((blocks, rows, half_width), F32),
            jax.ShapeDtypeStruct((blocks, rows, half_width), BF),
        ]
        scratch = [
            pltpu.VMEM((halves, width, half_width), F32),
            pltpu.VMEM((width, half_width), BF),
            pltpu.SemaphoreType.DMA((2 * blocks,)),
        ]
    else:
        shapes = [jax.ShapeDtypeStruct((1, width, width), F32)]
        scratch = [pltpu.VMEM((1, width, width), F32), pltpu.SemaphoreType.DMA((1,))]
    return pl.pallas_call(
        kernel,
        grid=(n,),
        in_specs=[SMEM, clip(width)] + [clip(c) for c in parts],
        out_specs=[ANY] * len(shapes),
        out_shape=shapes,
        scratch_shapes=scratch,
        compiler_params=params(24),
        cost_estimate=SHORT,
        name="out_weight_grad",
    )(meta, proj, *mixes)


def attend_back(groups, qkv, logs, d_mixes, order, counts, rows, relative, first, at_pair, pairs):
    each, length, width = groups[0].shape
    clips = qkv.shape[0]
    columns, part = 384 * pairs, 128 * pairs
    all_heads = logs.shape[1]
    n_groups = len(groups)
    n_mix = len(d_mixes)
    specs, _ = pair_specs(groups, (length, width))
    mix_each = d_mixes[0].shape[0]
    mix_specs, _ = pair_specs(d_mixes, (length, part), at_pair // pairs)
    blocks = width // rows
    half_blocks = blocks // 2

    def kernel(order_ref, count_ref, qkv_ref, log_ref, *refs):
        ins = refs[:n_groups]
        mix_refs = refs[n_groups : n_groups + n_mix]
        refs = refs[n_groups + n_mix :]
        d_qkv, bias_grad = refs[:2]
        if relative:
            keep, send, total, low, sems = refs[2:]
        else:
            keep, total, sems = refs[2:]
        step = pl.program_id(0)
        valid = lax.broadcasted_iota(jnp.int32, (length, 1), 0) < count_ref[step]
        lane = lax.broadcasted_iota(jnp.int32, (1, 2 * HEAD_DIM), 1)
        d_mix = choose(mix_refs, step, mix_each)
        pieces = []
        scale = HEAD_DIM**-0.5
        for pair in range(pairs):
            at = 384 * pair
            q = qkv_ref[0, :, at : at + 128] * jnp.asarray(scale, BF)
            k = qkv_ref[0, :, at + 128 : at + 256]
            v = qkv_ref[0, :, at + 256 : at + 384]
            do = d_mix[:, 128 * pair : 128 * pair + 128]
            k_t = k.T
            dk = dv = None
            turned_q = []
            for half in range(2):
                mine = (lane >= HEAD_DIM) if half else (lane < HEAD_DIM)
                only = lambda x: jnp.where(mine, x, jnp.zeros_like(x))
                s = dot_nt(only(k), q)
                h = 2 * (first + pair) + half
                p = jnp.exp(jnp.where(valid, s, NEG) - log_ref[0, h : h + 1, :])
                dp = dot_nt(only(v), do)
                inner = jnp.sum(dp * p, axis=0, keepdims=True)
                ds = (p * (dp - inner)).astype(BF)
                dv_half = dot(p.astype(BF), only(do))
                dk_half = dot(ds, only(q))
                dv = dv_half if dv is None else dv + dv_half
                dk = dk_half if dk is None else dk + dk_half
                turned_q.append(dot(k_t[HEAD_DIM * half : HEAD_DIM * half + HEAD_DIM], ds))
            pieces += [(jnp.concatenate(turned_q, axis=0) * scale).T, dk, dv]
        low_rows = jnp.concatenate(pieces, axis=1).astype(BF)
        d_qkv[0] = low_rows
        bias_part = jnp.sum(low_rows.astype(F32), axis=0, keepdims=True)
        weight_part = dot(choose(ins, step, each).T, low_rows)

        @pl.when(step == 0)
        def _():
            total[...] = weight_part
            bias_grad[...] = bias_part

        @pl.when(step > 0)
        def _():
            total[...] += weight_part
            bias_grad[...] += bias_part

        @pl.when(step == clips - 1)
        def _():
            place = lambda n: order_ref[n]
            if relative:
                low[...] = total[...].astype(BF)
                copies = deliver(total, place, rows, 0, [keep], sems, 0)
                copies += deliver(low, place, rows, half_blocks, [send], sems, half_blocks)
                run_all(copies)
            else:
                run_all([pltpu.make_async_copy(total, keep.at[0], sems.at[0])])

    clip = lambda c: pl.BlockSpec((1, length, c), lambda i: (i, 0, 0))
    block_at = first // pairs
    qkv_spec = pl.BlockSpec((1, length, columns), lambda i: (i, 0, block_at))
    if relative:
        shapes = [
            jax.ShapeDtypeStruct((half_blocks, rows, columns), F32),
            jax.ShapeDtypeStruct((half_blocks, rows, columns), BF),
        ]
        scratch = [pltpu.VMEM((width, columns), F32), pltpu.VMEM((width, columns), BF)]
    else:
        shapes = [jax.ShapeDtypeStruct((1, width, columns), F32)]
        scratch = [pltpu.VMEM((width, columns), F32)]
    n_rows = clips * length
    return pl.pallas_call(
        kernel,
        grid=(clips,),
        in_specs=[
            SMEM,
            SMEM,
            qkv_spec,
            pl.BlockSpec((1, all_heads, length), lambda i: (i, 0, 0)),
        ]
        + specs
        + mix_specs,
        out_specs=[clip(columns), whole((1, columns))] + [ANY] * len(shapes),
        out_shape=[
            jax.ShapeDtypeStruct((clips, length, columns), BF),
            jax.ShapeDtypeStruct((1, columns), F32),
        ]
        + shapes,
        scratch_shapes=scratch + [pltpu.SemaphoreType.DMA((blocks,))],
        compiler_params=params(48),
        cost_estimate=SHORT,
        name="attend_back",
    )(order, counts, qkv, logs, *groups, *d_mixes)


def attn_in_grad(d_qkvs, order, pieces, rows, each, width):
    clips, length, _ = d_qkvs[0].shape
    sizes = [d.shape[2] for d in d_qkvs]
    total = sum(sizes)
    n_d = len(d_qkvs)
    flat = [array for arrays, _ in pieces for array in arrays]
    blocks = sum(array.shape[0] for array in flat)
    split = clips > each

    def kernel(order_ref, *refs):
        row_refs = refs[:n_d]
        piece_refs = refs[n_d : n_d + len(flat)]
        outs = refs[n_d + len(flat) :]
        weight, sems = outs[-2:]
        step = pl.program_id(0)

        @pl.when(step == 0)
        def _():
            copies, used, column = [], 0, 0
            for arrays, size in pieces:
                refs_here = piece_refs[used : used + len(arrays)]
                target = weight.at[:, column : column + size]
                copies += assemble(
                    refs_here, lambda n: order_ref[n], rows, target, sems, len(copies), slice(0, size)
                )
                used += len(arrays)
                column += size
            run_all(copies)

        low = jnp.concatenate([ref[0] for ref in row_refs], axis=1) if n_d > 1 else row_refs[0][0]
        value = dot_nt(low, weight[...])
        if split:

            @pl.when(step < each)
            def _():
                outs[0][0] = value

            @pl.when(step >= each)
            def _():
                outs[1][0] = value.astype(BF)
        else:
            outs[0][0] = value

    own = pl.BlockSpec((1, length, width), lambda i: (jnp.minimum(i, each - 1), 0, 0))
    other = pl.BlockSpec((1, length, width), lambda i: (jnp.clip(i - each, 0, each - 1), 0, 0))
    shapes = [jax.ShapeDtypeStruct((each, length, width), F32)]
    if split:
        shapes.append(jax.ShapeDtypeStruct((each, length, width), BF))
    return pl.pallas_call(
        kernel,
        grid=(clips,),
        in_specs=[SMEM]
        + [pl.BlockSpec((1, length, c), lambda i: (i, 0, 0)) for c in sizes]
        + [ANY] * len(flat),
        out_specs=[own, other][: len(shapes)],
        out_shape=shapes,
        scratch_shapes=[pltpu.VMEM((width, total), BF), pltpu.SemaphoreType.DMA((blocks,))],
        compiler_params=params(32),
        cost_estimate=SHORT,
        name="attn_in_grad",
    )(order, *d_qkvs, *flat)


def norm_one_back(das, embed, d_resid, small):
    n, length, width = d_resid.shape
    n_da = len(das)

    def kernel(small_ref, embed_ref, resid_ref, *refs):
        da_refs = refs[:n_da]
        grad, sums = refs[n_da:]
        step = pl.program_id(0)
        da = da_refs[0][0].astype(F32)
        for ref in da_refs[1:]:
            da = da + ref[0].astype(F32)
        hat, inv = norm_parts(embed_ref[0])
        grad[0] = resid_ref[0] + norm_back(da * small_ref[0:1, :], hat, inv)
        row = lambda v: jnp.sum(v, axis=0, keepdims=True)
        parts = jnp.concatenate([row(da * hat), row(da), jnp.zeros((6, width), F32)])

        @pl.when(step == 0)
        def _():
            sums[...] = parts

        @pl.when(step > 0)
        def _():
            sums[...] += parts

    clip = pl.BlockSpec((1, length, width), lambda i: (i, 0, 0))
    return pl.pallas_call(
        kernel,
        grid=(n,),
        in_specs=[whole((16, width)), clip, clip] + [clip] * n_da,
        out_specs=[clip, whole((8, width))],
        out_shape=[
            jax.ShapeDtypeStruct(d_resid.shape, F32),
            jax.ShapeDtypeStruct((8, width), F32),
        ],
        compiler_params=params(24),
        cost_estimate=SHORT,
        name="norm_one_back",
    )(small, embed, d_resid, *das)


def update_group(weight, grad, moment, average, grad_norm, weight_norm):
    effective = grad + WEIGHT_DECAY * weight
    moment_new = MOMENTUM_DECAY * moment + effective
    rate = TRUST_RATE * weight_norm / (grad_norm + WEIGHT_DECAY * weight_norm)
    weight_new = weight - rate * (effective + MOMENTUM_DECAY * moment_new)
    average_new = AVERAGE_DECAY * average + (1.0 - AVERAGE_DECAY) * weight_new
    return (weight_new, moment_new, average_new)


def update_all(state, sums, place, halves_q, halves_r, g_up, g_down, cuts):
    rows, width = state[1].shape
    part = width // 2
    pairs = part // 128
    n_sq = 9

    def kernel(place_ref, sums_ref, q_own, q_other, r_own, r_other, up_ref, down_ref, *refs):
        ins, outs = refs[:15], refs[15:30]
        norms_ref = refs[30]
        core, chip = place_ref[0], place_ref[1]
        small_rows = sums_ref[0:12, :]
        squares = [sums_ref[12:13, k : k + 1] for k in range(n_sq)]
        squares = squares[:4] + [jnp.sum(small_rows * small_rows).reshape(1, 1)] + squares[4:]
        norms = [jnp.sqrt(s) for s in squares]

        def write(group, weight_cols, grad):
            at = (slice(None), weight_cols)
            values = update_group(
                ins[group][at], grad, ins[5 + group][at], ins[10 + group][at],
                norms[group], norms[5 + group],
            )
            for k in range(3):
                outs[5 * k + group][at] = values[k]

        first = core == 0
        for c in range(2):
            pick = lambda own, other: jnp.where(first if c == 0 else ~first, own, other)
            for pair in range(pairs):
                for t in range(3):
                    if pair < 2:
                        cut = slice(384 * pair + 128 * t, 384 * pair + 128 * t + 128)
                        grad = pick(q_own[:, cut], q_other[:, cut])
                    else:
                        cut = slice(128 * t, 128 * t + 128)
                        grad = pick(r_own[:, cut], r_other[:, cut])
                    at = t * width + c * part + 128 * pair
                    write(0, slice(at, at + 128), grad)
            cut = slice(768, 768 + part)
            write(1, slice(c * part, c * part + part), pick(q_own[:, cut], q_other[:, cut]))
        write(2, slice(None), up_ref[...])
        write(3, slice(None), down_ref[...])

        @pl.when(pl.program_id(0) == 0)
        def _():
            lane = lax.broadcasted_iota(jnp.int32, (1, 128), 1)
            row = jnp.zeros((1, 128), F32)
            for k in range(10):
                row = jnp.where(lane == k, norms[k], row)
            norms_ref[...] = row
            shift = lax.rem(width - chip * rows, width)
            mine = pltpu.roll(sums_ref[...], shift, 1)[:, :128]
            grad = mine.T[:rows]
            at = lax.broadcasted_iota(jnp.int32, (rows, 1), 0)
            column = lax.broadcasted_iota(jnp.int32, (1, 16), 1)
            share = rows // 4
            for col in range(4):
                total = jnp.zeros((rows, 128), F32)
                for quarter in range(4):
                    source = (at - share * quarter) * 4 + col
                    inside = (at >= share * quarter) & (at < share * quarter + share)
                    here = inside & (lane == source)
                    total = jnp.where(here, mine[8 + quarter : 9 + quarter, :], total)
                value = jnp.sum(total, axis=1, keepdims=True)
                grad = jnp.where(column == 8 + col, value, grad)
            write(4, slice(None), grad.T[:12])

    tall = lambda x: pl.BlockSpec((x.shape[0] // cuts, x.shape[1]), lambda i: (i, 0))
    state_specs = [whole(x.shape) if k % 5 == 4 else tall(x) for k, x in enumerate(state)]
    return pl.pallas_call(
        kernel,
        grid=(cuts,),
        in_specs=[SMEM, whole(sums.shape)]
        + [tall(x) for x in (*halves_q, *halves_r, g_up, g_down)]
        + state_specs,
        out_specs=state_specs + [whole((1, 128))],
        out_shape=[jax.ShapeDtypeStruct(x.shape, F32) for x in state]
        + [jax.ShapeDtypeStruct((1, 128), F32)],
        compiler_params=params(48),
        cost_estimate=SHORT,
        name="update_all",
    )(place, sums, *halves_q, *halves_r, g_up, g_down, *state)


def weight_squares(state):
    def kernel(*refs):
        lane = lax.broadcasted_iota(jnp.int32, (1, 128), 1)
        row = jnp.zeros((1, 128), F32)
        for k, ref in enumerate(refs[:-1]):
            row = jnp.where(lane == k, 0.5 * jnp.sum(ref[...] * ref[...]), row)
        refs[-1][...] = row

    return pl.pallas_call(
        kernel,
        grid=(1,),
        in_specs=[whole(x.shape) for x in state],
        out_specs=whole((1, 128)),
        out_shape=jax.ShapeDtypeStruct((1, 128), F32),
        compiler_params=params(24),
        cost_estimate=SHORT,
        name="weight_squares",
    )(*state)


def interleave(own, other, place):
    rows, double = own[0].shape
    width = double // 2
    run = rows

    def kernel(place_ref, *refs):
        own_refs, other_refs = refs[:2], refs[2:4]
        up, down, squares = refs[4:]
        first = place_ref[0] == 0
        lane = lax.broadcasted_iota(jnp.int32, (1, 128), 1)
        total_up = sum(jnp.sum(r[:, :width] * r[:, :width]) for r in own_refs)
        total_down = sum(jnp.sum(r[:, width:] * r[:, width:]) for r in own_refs)
        squares[...] = jnp.where(lane == 0, total_up, jnp.where(lane == 1, total_down, 0.0))
        cells = []
        for c in range(2):
            for h in range(2):
                ahead = first if c == 0 else ~first
                cell = jnp.where(ahead, own_refs[h][...], other_refs[h][...])
                cells.append(cell[:, :width])
                at = (2 * c + h) * rows
                down[at : at + rows, :] = cell[:, width:]
        for tile in range(4 * width // 128):
            value = None
            low = 128 * tile
            for k in range(low // run, (low + 127) // run + 1):
                f, ch = k // 4, k % 4
                begin, place_at = f * run, k * run - low
                start = min(begin // 128 * 128, width - 256)
                window = cells[ch][:, start : start + 256]
                moved = pltpu.roll(window, (place_at - (begin - start)) % 256, 1)[:, :128]
                if value is None:
                    value = moved
                else:
                    value = jnp.where(lane >= place_at, moved, value)
            up[:, low : low + 128] = value

    return pl.pallas_call(
        kernel,
        grid=(1,),
        in_specs=[SMEM] + [whole(own[0].shape)] * 4,
        out_specs=[whole((rows, 4 * width)), whole((4 * rows, width)), whole((1, 128))],
        out_shape=[
            jax.ShapeDtypeStruct((rows, 4 * width), F32),
            jax.ShapeDtypeStruct((4 * rows, width), F32),
            jax.ShapeDtypeStruct((1, 128), F32),
        ],
        compiler_params=params(32),
        cost_estimate=SHORT,
        name="interleave",
    )(place, *own, *other)


def gather_sums(place, sums_one, sums_two, bias_grads, bias_ups, squares_mlp, squares_w):
    width = sums_one.shape[1]
    part = width // 2

    def kernel(place_ref, one, two, *refs):
        grads, ups = refs[: len(bias_grads)], refs[len(bias_grads) : len(bias_grads) + 2]
        sq_mlp, sq_w, out = refs[-3:]
        core = place_ref[0]
        out[...] = jnp.zeros_like(out)
        out[0:2, :] = one[0:2, :]
        out[2:4, :] = two[0:2, :]
        out[6:8, :] = two[2:4, :]
        for c in range(2):

            @pl.when(core == c)
            def _():
                for pair, ref in enumerate(grads):
                    at = c * part + 128 * pair
                    out[4:5, at : at + 128] = ref[:, 0:128]
                    out[5:6, at : at + 128] = ref[:, 256:384]
                for h in range(2):
                    out[8 + 2 * c + h : 9 + 2 * c + h, :] = ups[h][...]

        lane = lax.broadcasted_iota(jnp.int32, (1, 128), 1)
        row = jnp.where((lane == 2) | (lane == 3), pltpu.roll(sq_mlp[...], 2, 1), 0.0)
        moved = pltpu.roll(sq_w[...], 4, 1)
        out[12:13, :128] = jnp.where((lane >= 4) & (lane < 9), moved, row)

    ins = [sums_one, sums_two, *bias_grads, *bias_ups, squares_mlp, squares_w]
    return pl.pallas_call(
        kernel,
        grid=(1,),
        in_specs=[SMEM] + [whole(x.shape) for x in ins],
        out_specs=whole((16, width)),
        out_shape=jax.ShapeDtypeStruct((16, width), F32),
        compiler_params=params(16),
        cost_estimate=SHORT,
        name="gather_sums",
    )(place, *ins)


def last_shards(sums, keep_r, recv_r, shard_q):
    _, rows, columns = keep_r.shape
    wide = shard_q.shape[1]

    def kernel(sums_ref, keep, *refs):
        recvs, q, shard, out = refs[:-3], refs[-3], refs[-2], refs[-1]
        total = keep[0]
        for ref in recvs:
            total = total + ref[0].astype(F32)
        shard[...] = total
        out[...] = sums_ref[...]
        inner, outer = q[:, :768], q[:, 768:]
        square = jnp.sum(total * total) + jnp.sum(inner * inner)
        lane = lax.broadcasted_iota(jnp.int32, (1, 128), 1)
        old = sums_ref[12:13, :128]
        new = jnp.where(lane == 0, square, jnp.where(lane == 1, jnp.sum(outer * outer), old))
        out[12:13, :128] = new

    block = pl.BlockSpec((1, rows, columns), lambda i: (0, 0, 0))
    return pl.pallas_call(
        kernel,
        grid=(1,),
        in_specs=[whole(sums.shape), block] + [block] * len(recv_r) + [whole((rows, wide))],
        out_specs=[whole((rows, columns)), whole(sums.shape)],
        out_shape=[
            jax.ShapeDtypeStruct((rows, columns), F32),
            jax.ShapeDtypeStruct(sums.shape, F32),
        ],
        compiler_params=params(16),
        cost_estimate=SHORT,
        name="last_shards",
    )(sums, keep_r, *recv_r, shard_q)


def finish(masters, moments, averages, grads, totals):
    norms = jnp.sqrt(totals)
    results = [
        update_group(masters[i], grads[i], moments[i], averages[i], norms[i], norms[5 + i])
        for i in range(5)
    ]
    return (
        tuple(r[0] for r in results)
        + tuple(r[1] for r in results)
        + tuple(r[2] for r in results)
        + (norms,)
    )


def square_sum(x):
    return jnp.sum(x * x)


def tie(*arrays):
    return lax.optimization_barrier(arrays)


def paired_device(links, tokens, positions, counts, cotangent, *state):
    state = [x.T if k % 5 == 4 else x for k, x in enumerate(state)]
    w_qkv, w_out, w_up, w_down, w_small = state[:5]
    each, length, width = tokens.shape
    rows = w_qkv.shape[0]
    core = lax.axis_index("dp")
    chip = lax.axis_index("fsdp")
    table = jnp.asarray(links.masks())
    mine = lax.dynamic_index_in_dim(table, core, 0, False) ^ chip
    partner = lax.dynamic_index_in_dim(table, 1 - core, 0, False) ^ chip
    core_id = core[None].astype(jnp.int32)
    meta = jnp.concatenate([core_id, mine, partner])
    place = jnp.concatenate([core_id, chip[None].astype(jnp.int32)])
    part = width // 2
    pairs = part // 128
    cross, flip, along_z = links.cross, links.flip, links.along_z
    half_core = lambda x, axis: lax.dynamic_index_in_dim(x, core, axis, False)
    join = lambda *blocks: jnp.concatenate(blocks, axis=0)

    def onward(first, last, keep, *recvs):
        total = keep[first:last]
        for recv in recvs:
            total = total + recv[first:last].astype(F32)
        return total

    cut = half_core(w_qkv.reshape(rows, 3, 2, pairs, 128), 2).astype(BF)
    cut = jnp.swapaxes(cut, 1, 2).reshape(rows, pairs * 384)
    small_cut = jnp.concatenate([w_small[:8], w_small[8:].T.reshape(4, rows)], axis=0)
    small_cut = jnp.pad(small_cut.astype(BF).T, ((0, 0), (0, 116)))
    pack_one = jnp.concatenate([cut[:, :768], small_cut], axis=1)[None]
    pack_one, cut, positions, counts, tokens, w_out, w_up, w_down = tie(
        pack_one, cut, positions, counts, tokens, w_out, w_up, w_down
    )
    one_z = along_z([pack_one] * 3)
    token_other = cross(tokens)
    place_other = cross(jnp.concatenate([positions, counts[:, None]], axis=1))
    out_cut = half_core(w_out.reshape(rows, 2, part), 1).astype(BF)
    pack_two = jnp.concatenate([cut[:, 768:], out_cut], axis=1)[None]
    up_cut = half_core(w_up.reshape(rows, 16, 2, 2, rows), 2).astype(BF)
    down_cut = half_core(w_down.reshape(2, 2, rows, width), 0).astype(BF)
    pack_a, pack_b = [
        jnp.concatenate([up_cut[:, :, h].reshape(rows, 16 * rows), down_cut[h]], axis=1)[None]
        for h in range(2)
    ]
    *one_z, pack_two, pack_a, pack_b = tie(*one_z, pack_two, pack_a, pack_b)
    one_4 = join(pack_one, *one_z)

    column = lambda x: x.astype(F32)[..., None]
    one_4, pack_two, tokens = tie(one_4, pack_two, tokens)
    one_b = flip(one_4, 4)
    two_z = along_z([pack_two] * 3)
    embed = embed_rows([tokens], [column(positions)])
    one_b, *two_z, embed = tie(one_b, *two_z, embed)
    one_8, two_4 = join(one_4, one_b), join(pack_two, *two_z)

    one_8, two_4, pack_a, token_other, cotangent = tie(
        one_8, two_4, pack_a, token_other, cotangent
    )
    one_c = flip(one_8, 8)
    two_b = flip(two_4, 4)
    a_z = along_z([pack_a] * 3)
    cot_other = cross(cotangent)
    embed_other = embed_rows([token_other], [column(place_other[:, :length])])
    squares_w = weight_squares(state[:5])
    one_c, two_b, embed_other, squares_w = tie(one_c, two_b, embed_other, squares_w)
    counts_all = jnp.concatenate([counts, place_other[:, length]])
    two_8 = join(two_4, two_b)

    embed_other, two_8, pack_b = tie(embed_other, two_8, pack_b)
    qkv_one, embeds = [one_8, one_c], [embed, embed_other]
    two_c = flip(two_8, 8)
    b_z = along_z([pack_b] * 3)
    forward = lambda source, small, pieces, pair, at: attend_forward(
        source, small, mine, core_id, counts_all, pieces, rows, each, 2 * pair, 2, 6, at
    )
    small, attn_in, qkv_0, logs_0, mix_own_0, mix_send_0 = forward(embeds, None, qkv_one, 0, 0)
    two_c, mix_send_0, *a_z, attn_in = tie(two_c, mix_send_0, *a_z, attn_in)
    a_4 = join(pack_a, *a_z)
    qkv_two = [two_8, two_c]
    two_8o, two_co = two_8[:, :, part:], two_c[:, :, part:]

    a_4, attn_in_1, mix_send_0, two_8o, two_co = tie(a_4, attn_in, mix_send_0, two_8o, two_co)
    a_b = flip(a_4, 4)
    mix_recv_0 = cross(mix_send_0)
    out_c, out_d = cross(two_8o), cross(two_co)
    qkv_1, logs_1, mix_own_1, mix_send_1 = forward([attn_in_1], small, qkv_one, 1, 1)
    a_b, mix_send_1, *b_z = tie(a_b, mix_send_1, *b_z)
    a_8, b_4 = join(a_4, a_b), join(pack_b, *b_z)

    a_8, b_4, mix_send_1, attn_in_2 = tie(a_8, b_4, mix_send_1, attn_in)
    a_c = flip(a_8, 8)
    mix_recv_1 = cross(mix_send_1)
    qkv_2, logs_2, mix_own_2, mix_send_2 = forward([attn_in_2], small, qkv_two, 2, 0)
    mix_send_2, mix_recv_0, mix_recv_1, b_4 = tie(mix_send_2, mix_recv_0, mix_recv_1, b_4)

    mix_recv_2 = cross(mix_send_2)
    b_b = flip(b_4, 4)
    mixes = [mix_own_0, mix_own_1, mix_own_2, mix_recv_0, mix_recv_1, mix_recv_2]
    places = [(0, 0), (0, 128), (0, 256), (1, 0), (1, 128), (1, 256)]
    out_pieces = ([two_8, two_c], [out_c, out_d])
    resid, mlp_own = project_norm(mixes, places, embed, small, meta, *out_pieces, rows)
    mlp_own, a_c, b_b = tie(mlp_own, a_c, b_b)
    mlp_other = cross(mlp_own)
    b_8 = join(b_4, b_b)

    mlp_own, mlp_other, b_8 = tie(mlp_own, mlp_other, b_8)
    b_c = flip(b_8, 8)
    biases = [lax.dynamic_slice(small, (8 + 2 * core + h, 0), (1, width)) for h in range(2)]
    groups, cots = [mlp_own, mlp_other], [cotangent, cot_other]
    own_out_a, own_dm_a, sent_out_a, sent_dm_a, bias_up_a, keep_a, send_a = mlp_both(
        groups, cots, mine, counts_all, biases[0], [a_8, a_c], rows, True
    )
    mlp_own, mlp_other, send_a, b_c, sent_dm_a, sent_out_a = tie(
        mlp_own, mlp_other, send_a, b_c, sent_dm_a, sent_out_a
    )
    groups = [mlp_own, mlp_other]
    a_r3 = flip(send_a, 8)
    recv_dm_a, recv_out_a = cross(sent_dm_a), cross(sent_out_a)
    own_out_b, own_dm_b, sent_out_b, sent_dm_b, bias_up_b, keep_b, send_b = mlp_both(
        groups, cots, mine, counts_all, biases[1], [b_8, b_c], rows, True
    )
    sent_dm_b, sent_out_b, send_b, a_r3, recv_dm_a, recv_out_a = tie(
        sent_dm_b, sent_out_b, send_b, a_r3, recv_dm_a, recv_out_a
    )
    b_r3 = flip(send_b, 8)
    recv_dm_b = cross(sent_dm_b)
    send_a = onward(4, 8, keep_a, a_r3).astype(BF)
    recv_dm_b, send_a = tie(recv_dm_b, send_a)

    a_r2 = flip(send_a, 4)
    dms = [own_dm_a, own_dm_b, recv_dm_a, recv_dm_b]
    d_mix_own, d_mix_send, proj, d_resid, sums_two = norm_two_back(
        dms, resid, cotangent, small, meta, counts, *out_pieces, rows, part
    )
    d_mix_send, proj, sent_out_b = tie(d_mix_send, proj, sent_out_b)
    d_mix_recv = cross(d_mix_send)
    keep_o, send_o = out_weight_grad(mixes, places, proj, meta, rows)
    d_mix_recv, send_o, b_r3, a_r2 = tie(d_mix_recv, send_o, b_r3, a_r2)
    send_b = onward(4, 8, keep_b, b_r3).astype(BF)
    sends_a = [onward(k, k + 1, keep_a, a_r3, a_r2).astype(BF) for k in (1, 2, 3)]

    d_mix_recv, send_b, send_o, sent_out_b, *sends_a = tie(
        d_mix_recv, send_b, send_o, sent_out_b, *sends_a
    )
    b_r2 = flip(send_b, 4)
    a_rz = along_z(sends_a)
    recv_o = cross(send_o)
    recv_out_b = cross(sent_out_b)
    d_mixes = [d_mix_own, d_mix_recv]
    back = lambda qkv, logs, pair, ins: attend_back(
        [ins], qkv, logs, d_mixes, mine, counts_all, rows, True, 0, pair, 1
    )
    d_qkv_0, bias_grad_0, keep_0, send_0 = back(qkv_0, logs_0, 0, attn_in)
    send_0, b_r2, *a_rz, recv_o, recv_out_b = tie(send_0, b_r2, *a_rz, recv_o, recv_out_b)
    sends_b = [onward(k, k + 1, keep_b, b_r3, b_r2).astype(BF) for k in (1, 2, 3)]
    shard_a = onward(0, 1, keep_a, a_r3, a_r2, *a_rz)[0]

    send_0, shard_a, attn_in_1, *sends_b = tie(send_0, shard_a, attn_in, *sends_b)
    b_rz = along_z(sends_b)
    other_a = cross(shard_a)
    d_qkv_1, bias_grad_1, keep_1, send_1 = back(qkv_1, logs_1, 1, attn_in_1)
    send_1, *b_rz, other_a = tie(send_1, *b_rz, other_a)
    keep_q = jnp.concatenate([keep_0, keep_1, keep_o[:8] + recv_o[:8].astype(F32)], axis=2)
    send_o = keep_o[8:] + recv_o[8:].astype(F32)
    send_q = jnp.concatenate([send_0, send_1, send_o.astype(BF)], axis=2)
    shard_b = onward(0, 1, keep_b, b_r3, b_r2, *b_rz)[0]

    send_q, shard_b, attn_in_2 = tie(send_q, shard_b, attn_in)
    q_r3 = flip(send_q, 8)
    other_b = cross(shard_b)
    d_qkv_2, bias_grad_2, keep_r, send_r = back(qkv_2, logs_2, 2, attn_in_2)
    d_qkv_2, send_r, q_r3, other_b = tie(d_qkv_2, send_r, q_r3, other_b)
    send_q = onward(4, 8, keep_q, q_r3).astype(BF)

    d_qkv_2, send_r, send_q = tie(d_qkv_2, send_r, send_q)
    r_r3 = flip(send_r, 8)
    q_r2 = flip(send_q, 4)
    da_own, da_send = attn_in_grad(
        [d_qkv_0, d_qkv_1, d_qkv_2], mine, [(qkv_one, 768), (qkv_two, 384)], rows, each, width
    )
    da_send, r_r3, q_r2 = tie(da_send, r_r3, q_r2)
    send_r = onward(4, 8, keep_r, r_r3).astype(BF)
    sends_q = [onward(k, k + 1, keep_q, q_r3, q_r2).astype(BF) for k in (1, 2, 3)]

    da_send, send_r, *sends_q = tie(da_send, send_r, *sends_q)
    da_recv = cross(da_send)
    r_r2 = flip(send_r, 4)
    q_rz = along_z(sends_q)
    token_grad, sums_one = norm_one_back([da_own, da_recv], embed, d_resid, small)
    r_r2, sums_one = tie(r_r2, sums_one)
    sends_r = [onward(k, k + 1, keep_r, r_r3, r_r2).astype(BF) for k in (1, 2, 3)]

    resid, *sends_r = tie(resid, *sends_r)
    r_rz = along_z(sends_r)
    g_up, g_down, squares_mlp = interleave((shard_a, shard_b), (other_a, other_b), place)
    bias_grads = [bias_grad_0, bias_grad_1, bias_grad_2]
    sums = gather_sums(
        place, sums_one, sums_two, bias_grads, (bias_up_a, bias_up_b), squares_mlp, squares_w
    )
    block_rows = resid + small[7]
    for value in (own_out_a, own_out_b, recv_out_a, recv_out_b):
        block_rows = block_rows + value.astype(F32)
    block_out = block_rows.astype(BF)
    *q_rz, block_out, sums = tie(*q_rz, block_out, sums)
    shard_q = onward(0, 1, keep_q, q_r3, q_r2, *q_rz)[0]
    *r_rz, shard_q = tie(*r_rz, shard_q)
    other_q = cross(shard_q)
    shard_r, sums = last_shards(sums, keep_r, [r_r3, r_r2, *r_rz], shard_q)
    other_r = cross(shard_r)
    sums = links.sum_all(sums)
    results = update_all(
        state, sums, place, (shard_q, other_q), (shard_r, other_r), g_up, g_down, 3
    )
    outs = [x.T if k % 5 == 4 else x for k, x in enumerate(results[:15])]
    return (block_out, token_grad) + tuple(outs) + (results[15][0, :10],)


def plain_device(tokens, positions, counts, cotangent, *state):
    masters, moments, averages = state[:5], state[5:10], state[10:]
    each, length, width = tokens.shape
    heads = width // HEAD_DIM
    pairs = heads // 2
    full = [
        lax.all_gather(w.astype(BF), "fsdp", axis=0, tiled=True) for w in masters
    ]
    wq, wo, up, down, table = full
    wq = jnp.swapaxes(wq.reshape(width, 3, pairs, 128), 1, 2).reshape(1, width, 3 * width)
    table = table.astype(F32)
    vectors = jnp.concatenate([table[:, :8].T, jnp.zeros((8, width), F32)], axis=0)
    bias_up = table[:, 8:].reshape(1, -1)
    hidden = bias_up.shape[1]
    order = jnp.zeros((33,), jnp.int32)
    embed = embed_rows([tokens], [positions.astype(F32)[..., None]])
    attn_in, qkv, logs, mixed = attend_forward(
        [embed], vectors, order, order, counts, [wq], width, each, 0, heads, 0, 0
    )
    places = [(0, 0)]
    resid, mlp_in = project_norm([mixed], places, embed, vectors, order, [wo[None]], [], width)
    outs, dms, bias_ups, ups, downs = [], [], [], [], []
    parts = 4
    size = hidden // parts
    for h in range(parts):
        cols = slice(h * size, (h + 1) * size)
        out, dm, bias, g_up, g_down = mlp_both(
            [mlp_in],
            [cotangent],
            order,
            counts,
            bias_up[:, cols],
            [up[:, cols][None], down[cols][None]],
            width,
            False,
        )
        outs.append(out)
        dms.append(dm)
        bias_ups.append(bias)
        ups.append(g_up[0])
        downs.append(g_down[0])
    d_mix, proj, d_resid, sums_two = norm_two_back(
        dms, resid, cotangent, vectors, order, counts, [wo[None]], [], width, width
    )
    g_out = out_weight_grad([mixed], places, proj, order, width)[0][0]
    d_qkv, bias_grad, g_qkv = attend_back(
        [attn_in], qkv, logs, [d_mix], order, counts, width, False, 0, 0, pairs
    )
    natural = lambda g: jnp.swapaxes(g.reshape(-1, pairs, 3, 128), 1, 2).reshape(-1, 3 * width)
    g_qkv, bias_grad = natural(g_qkv), natural(bias_grad)
    da = attn_in_grad([d_qkv], order, [([wq], 3 * width)], width, each, width)[0]
    token_grad, sums_one = norm_one_back([da], embed, d_resid, vectors)
    block_rows = resid + vectors[7]
    for value in outs:
        block_rows = block_rows + value
    block_out = block_rows.astype(BF)
    columns = jnp.stack(
        [
            sums_one[0],
            sums_one[1],
            sums_two[0],
            sums_two[1],
            bias_grad[0, :width],
            bias_grad[0, 2 * width :],
            sums_two[2],
            sums_two[3],
        ],
        axis=1,
    )
    small = jnp.concatenate(
        [columns, jnp.concatenate(bias_ups, axis=1).reshape(width, -1)], axis=1
    )
    partial = (
        g_qkv,
        g_out,
        jnp.concatenate(ups, axis=1),
        jnp.concatenate(downs, axis=0),
        small,
    )
    grads = []
    for grad in partial:
        shard = lax.psum_scatter(grad, "fsdp", scatter_dimension=0, tiled=True)
        grads.append(lax.psum(shard, "dp"))
    squares = jnp.stack([square_sum(g) for g in grads] + [square_sum(w) for w in masters])
    totals = lax.psum(squares, "fsdp")
    return (block_out, token_grad) + finish(masters, moments, averages, tuple(grads), totals)


def solution(mesh):
    clips = P(("dp", "fsdp"), None, None)
    in_specs = (clips, P(("dp", "fsdp"), None), P(("dp", "fsdp")), clips) + (P("fsdp", None),) * 15
    out_specs = (clips, clips) + (P("fsdp", None),) * 15 + (P(),)
    links = Links(mesh.shape["dp"], mesh.shape["fsdp"])

    def on_device(*args):
        if links.paired:
            return paired_device(links, *args)
        return plain_device(*args)

    return jax.shard_map(
        on_device, mesh=mesh, in_specs=in_specs, out_specs=out_specs, check_vma=False
    )
```

profile of v0, /device:TPU:0, one launch (start us, length us, event | category | flops | bytes accessed | tf_op | source)
XLA Modules:
  0.0 324.4 jit_solution(6799316655329565607)
XLA Ops:
  3.2 5.1 %collective-permute-start.3 = (bf16[1,48,896]{2,1,0:T(8,128)(2,1)S(1)}, bf16[1,48,896]{2,1,0:T(8,128)(2,1)S(1)}, u32[]{:S(2)}, u32[]{:S(2)}) collective-permute-start(bf16[1,48,896]{2,1,0:T(8,128)(2,1)S(1)} %fusion.16), channel_id=1, source_target_pairs={{0,12},{1,13},{2,14},{3,15},{4,8},{5,9},{6,10},{7,11},{8,4},{9,5},... | collective-permute-start | bytes 258056 | tf_op jit(solution)/shard_map/ppermute | solution.py:68
  12.0 3.5 %collective-permute-done.2 = bf16[1,48,896]{2,1,0:T(8,128)(2,1)S(1)} collective-permute-done((bf16[1,48,896]{2,1,0:T(8,128)(2,1)S(1)}, bf16[1,48,896]{2,1,0:T(8,128)(2,1)S(1)}, u32[]{:S(2)}, u32[]{:S(2)}) %collective-permute-start.2) | collective-permute-done | bytes 86048 | tf_op jit(solution)/shard_map/ppermute | solution.py:68
  17.2 2.6 collective-permute-start.7
  19.8 1.7 collective-permute-start.5
  22.5 6.4 %embed_rows.2.refs_0_.embed_ref = f32[2,392,768]{2,1,0:T(8,128)} custom-call(f32[8,768]{1,0:T(8,128)} %constant.55.clone.table, bf16[2,392,768]{2,1,0:T(8,128)(2,1)} %refs_0_.2, f32[2,392,1]{2,1,0:T(8,128)} %copy.50.refs_1_), custom_call_target="tpu_custom_call" | custom-call | flops 1 | bytes 1 | tf_op jit(solution)/shard_map/embed_rows/pallas_call | solution.py:163
  31.4 2.4 weight_squares.1.refs_6_
  34.8 6.3 %embed_rows.3.refs_1_ = f32[2,392,768]{2,1,0:T(8,128)} custom-call(f32[8,768]{1,0:T(8,128)} %constant.55.clone.table, bf16[2,392,768]{2,1,0:T(8,128)(2,1)} %collective-permute-done.8.refs_0_, f32[2,392,1]{2,1,0:T(8,128)} %copy.51.refs_1_), custom_call_target="tpu_custom_call" | custom-call | flops 1 | bytes 1 | tf_op jit(solution)/shard_map/embed_rows/pallas_call | solution.py:163
  43.0 2.2 collective-permute-start.14
  45.2 2.2 collective-permute-start.12
  48.2 11.5 %attend_forward.3 = (f32[16,768]{1,0:T(8,128)}, bf16[4,392,768]{2,1,0:T(8,128)(2,1)}, bf16[4,392,384]{2,1,0:T(8,128)(2,1)}, f32[4,2,392]{2,1,0:T(2,128)}, bf16[2...) custom-call(s32[16]{0:T(128)} %get-tuple-element.474.order_ref, s32[1]{0:T(128)} %bitcast.8.core_ref, ...), custom_call_target="tpu_custom_call" | custom-call | flops 1 | bytes 1 | tf_op jit(solution)/shard_map/attend_forward/pallas_call | solution.py:308
  62.1 2.6 collective-permute-start.18
  64.8 1.7 collective-permute-start.16
  66.5 9.1 %attend_forward.4 = (bf16[4,392,384]{2,1,0:T(8,128)(2,1)}, f32[4,2,392]{2,1,0:T(2,128)}, bf16[2,392,128]{2,1,0:T(8,128)(2,1)}, bf16[2,392,128]{2,1,0:T(8,128)(2,1)}) custom-call(s32[16]{0:T(128)} %get-tuple-element.474.order_ref, s32[1]{0:T(128)} %bitcast.8.core_ref, s32[4]{0:T(128)} %pad_add_fusion.1.count_ref, ...), custom_call_target="tpu_custom_call" | custom-call | flops 1 | bytes 1 | tf_op jit(solution)/shard_map/attend_forward/pallas_call | solution.py:308
  78.9 9.1 %attend_forward.5 = (bf16[4,392,384]{2,1,0:T(8,128)(2,1)}, f32[4,2,392]{2,1,0:T(2,128)}, bf16[2,392,128]{2,1,0:T(8,128)(2,1)}, bf16[2,392,128]{2,1,0:T(8,128)(2,1)}) custom-call(s32[16]{0:T(128)} %get-tuple-element.474.order_ref, s32[1]{0:T(128)} %bitcast.8.core_ref, s32[4]{0:T(128)} %pad_add_fusion.1.count_ref, ...), custom_call_target="tpu_custom_call" | custom-call | flops 1 | bytes 1 | tf_op jit(solution)/shard_map/attend_forward/pallas_call | solution.py:308
  92.1 7.9 %project_norm.1 = (f32[2,392,768]{2,1,0:T(8,128)}, bf16[2,392,768]{2,1,0:T(8,128)(2,1)}) custom-call(s32[33]{0:T(128)} %pad_add_fusion.2.meta_ref, f32[16,768]{1,0:T(8,128)} %get-tuple-element.271.refs_1_.small_ref, f32[2,392,768]{2,1,0:T(8,128)} %embed_rows.2.refs_0_.embed_ref, bf16[2,392,128]{2,1,0:T(8,128)(2,1)} %get-tuple-element.272.refs_0_, ...), custom_call_target="tpu_custom_call" | custom-call | flops 1 | bytes 1 | tf_op jit(solution)/shard_map/project_norm/pallas_call | solution.py:373
  100.6 2.4 pad_maximum_fusion.2.refs_4_
  104.2 2.0 slice_reduce_fusion
  106.2 23.9 %mlp_both.2 = (f32[2,392,768]{2,1,0:T(8,128)}, f32[2,392,768]{2,1,0:T(8,128)}, bf16[2,392,768]{2,1,0:T(8,128)(2,1)}, bf16[2,392,768]{2,1,0:T(8,128)(2,1)}, f32[1...) custom-call(s32[16]{0:T(128)} %get-tuple-element.474.order_ref, s32[4]{0:T(128)} %pad_add_fusion.1.count_ref, ...), custom_call_target="tpu_custom_call" | custom-call | flops 1 | bytes 1 | tf_op jit(solution)/shard_map/mlp_both/pallas_call | solution.py:522
  132.1 24.4 %mlp_both.3 = (f32[2,392,768]{2,1,0:T(8,128)}, f32[2,392,768]{2,1,0:T(8,128)}, bf16[2,392,768]{2,1,0:T(8,128)(2,1)}, bf16[2,392,768]{2,1,0:T(8,128)(2,1)}, f32[1...) custom-call(s32[16]{0:T(128)} %get-tuple-element.474.order_ref, s32[4]{0:T(128)} %pad_add_fusion.1.count_ref, ...), custom_call_target="tpu_custom_call" | custom-call | flops 1 | bytes 1 | tf_op jit(solution)/shard_map/mlp_both/pallas_call | solution.py:522
  157.7 2.0 add_convert_fusion.2
  159.8 10.7 %norm_two_back.1 = (bf16[2,392,384]{2,1,0:T(8,128)(2,1)}, bf16[2,392,384]{2,1,0:T(8,128)(2,1)}, bf16[2,392,768]{2,1,0:T(8,128)(2,1)}, f32[2,392,768]{2,1,0:T(8,128)}, f32[8,768]{1,0:T(8,128)}) custom-call(s32[33]{0:T(128)} %pad_add_fusion.2.meta_ref, s32[2]{0:T(128)} %count_ref, f32[16,768]{1,0:T(8,128)} %get-tuple-element.271.refs_1_.small_ref, ...), custom_call_target="tpu_custom_call" | custom-call | flops 1 | bytes 1 | tf_op jit(solution)/shard_map/norm_two_back/pallas_call | solution.py:596
  172.1 5.2 %out_weight_grad.1 = (f32[16,48,384]{2,1,0:T(8,128)}, bf16[16,48,384]{2,1,0:T(8,128)(2,1)}) custom-call(s32[33]{0:T(128)} %pad_add_fusion.2.meta_ref, bf16[2,392,768]{2,1,0:T(8,128)(2,1)} %get-tuple-element.334.proj_ref, bf16[2,392,128]{2,1,0:T(8,128)(2,1)} %get-tuple-element.272.refs_0_, bf16[2,392,128]{2,1,0:T(8,128)(2,1)} %get-tuple-element.279.refs_1_, ...), custom_call_target="tpu_custom_call" | custom-call | flops 1 | bytes 1 | tf_op jit(solution)/shard_map/out_weight_grad/pallas_call | solution.py:675
  177.3 3.7 %collective-permute-done.35 = bf16[4,48,1536]{2,1,0:T(8,128)(2,1)} collective-permute-done((bf16[4,48,1536]{2,1,0:T(8,128)(2,1)S(1)}, bf16[4,48,1536]{2,1,0:T(8,128)(2,1)}, u32[]{:S(2)}, u32[]{:S(2)}) %collective-permute-start.35) | collective-permute-done | bytes 589856 | tf_op jit(solution)/shard_map/ppermute | solution.py:68
  180.9 1.8 add_convert_fusion.8
  182.8 2.0 add_convert_fusion.1
  185.9 2.9 collective-permute-start.38
  188.8 6.3 %collective-permute-done.37 = bf16[1,48,1536]{2,1,0:T(8,128)(2,1)S(1)} collective-permute-done((bf16[1,48,1536]{2,1,0:T(8,128)(2,1)S(1)}, bf16[1,48,1536]{2,1,0:T(8,128)(2,1)S(1)}, u32[]{:S(2)}, u32[]{:S(2)}) %collective-permute-start.37) | collective-permute-done | bytes 147488 | tf_op jit(solution)/shard_map/ppermute | solution.py:68
  196.6 12.0 %attend_back.3 = (bf16[4,392,384]{2,1,0:T(8,128)(2,1)}, f32[1,384]{1,0:T(1,128)}, f32[8,48,384]{2,1,0:T(8,128)}, bf16[8,48,384]{2,1,0:T(8,128)(2,1)}) custom-call(s32[16]{0:T(128)} %get-tuple-element.474.order_ref, s32[4]{0:T(128)} %pad_add_fusion.1.count_ref, bf16[4,392,384]{2,1,0:T(8,128)(2,1)} %get-tuple-element.264.qkv_ref, ...), custom_call_target="tpu_custom_call" | custom-call | flops 1 | bytes 1 | tf_op jit(solution)/shard_map/attend_back/pallas_call | solution.py:779
  208.6 2.3 add_convert_fusion.5
  210.9 2.0 add_bitcast_fusion.1.refs_0_
  213.1 2.9 collective-permute-start.43
  217.4 11.9 %attend_back.4 = (bf16[4,392,384]{2,1,0:T(8,128)(2,1)}, f32[1,384]{1,0:T(1,128)}, f32[8,48,384]{2,1,0:T(8,128)}, bf16[8,48,384]{2,1,0:T(8,128)(2,1)}) custom-call(s32[16]{0:T(128)} %get-tuple-element.474.order_ref, s32[4]{0:T(128)} %pad_add_fusion.1.count_ref, bf16[4,392,384]{2,1,0:T(8,128)(2,1)} %get-tuple-element.346.qkv_ref, ...), custom_call_target="tpu_custom_call" | custom-call | flops 1 | bytes 1 | tf_op jit(solution)/shard_map/attend_back/pallas_call | solution.py:779
  234.0 11.9 %attend_back.5 = (bf16[4,392,384]{2,1,0:T(8,128)(2,1)}, f32[1,384]{1,0:T(1,128)}, f32[8,48,384]{2,1,0:T(8,128)}, bf16[8,48,384]{2,1,0:T(8,128)(2,1)}) custom-call(s32[16]{0:T(128)} %get-tuple-element.474.order_ref, s32[4]{0:T(128)} %pad_add_fusion.1.count_ref, bf16[4,392,384]{2,1,0:T(8,128)(2,1)} %get-tuple-element.362.qkv_ref, ...), custom_call_target="tpu_custom_call" | custom-call | flops 1 | bytes 1 | tf_op jit(solution)/shard_map/attend_back/pallas_call | solution.py:779
  246.4 1.9 fusion
  250.0 8.9 %attn_in_grad.1 = (f32[2,392,768]{2,1,0:T(8,128)}, bf16[2,392,768]{2,1,0:T(8,128)(2,1)}) custom-call(s32[16]{0:T(128)} %get-tuple-element.474.order_ref, bf16[4,392,384]{2,1,0:T(8,128)(2,1)} %get-tuple-element.345.refs_0_, bf16[4,392,384]{2,1,0:T(8,128)(2,1)} %get-tuple-element.361.refs_1_, bf16[4,392,384]{2,1,0:T(8,128)(2,1)} %get-tuple-element.386.refs_2_, ...), custom_call_target="tpu_custom_call" | custom-call | flops 1 | bytes 1 | tf_op jit(solution)/shard_map/attn_in_grad/pallas_call | solution.py:851
  259.9 2.0 fusion.8
  264.1 3.1 interleave.1
  267.2 2.9 collective-permute-start.51
  272.6 5.7 %norm_one_back.1 = (f32[2,392,768]{2,1,0:T(8,128)}, f32[8,768]{1,0:T(8,128)}) custom-call(f32[16,768]{1,0:T(8,128)} %get-tuple-element.271.refs_1_.small_ref, f32[2,392,768]{2,1,0:T(8,128)} %embed_rows.2.refs_0_.embed_ref, f32[2,392,768]{2,1,0:T(8,128)} %get-tuple-element.398.resid_ref, f32[2,392,768]{2,1,0:T(8,128)} %get-tuple-element.399.refs_0_, ...), custom_call_target="tpu_custom_call" | custom-call | flops 1 | bytes 1 | tf_op jit(solution)/shard_map/norm_one_back/pallas_call | solution.py:891
  278.4 1.7 add_convert_fusion.11
  280.0 4.8 %add_convert_fusion = bf16[2,392,768]{2,1,0:T(8,128)(2,1)} fusion(bf16[2,392,768]{2,1,0:T(8,128)(2,1)} %collective-permute-done.41, bf16[2,392,768]{2,1,0:T(8,128)(2,1)} %copy-done.18, f32[2,392,768]{2,1,0:T(8,128)} %get-tuple-element.405, f32[2,392,768]{2,1,0:T(8,128)} %get-tuple-element.404, f32[2,392,768]{2,1,0:T(8,128)S(1)} %copy-done.4, f32[768]{0:T(1024)S(1)} %copy-done.46), kind=kLoop, calls=%fused_computation | loop fusion | flops 4816896 | bytes 10841088 | tf_op jit(solution)/shard_map/convert_element_type | solution.py:1369
  286.5 2.9 collective-permute-start.56
  290.9 1.9 fusion.6.refs_5_.q_own
  292.8 2.4 collective-permute-done.57.refs_4_
  295.8 1.9 last_shards.1
  301.4 2.9 collective-permute-start.59
  304.3 1.9 collective-permute-done.61
  315.8 7.3 %update_all.1 = (f32[48,2304]{1,0:T(8,128)}, f32[48,768]{1,0:T(8,128)}, f32[48,3072]{1,0:T(8,128)}, f32[192,768]{1,0:T(8,128)}, f32[12,48]{1,0:T(8,128)}, /*inde...) custom-call(s32[2]{0:T(128)} %pad_add_fusion.3.place_ref, ...), custom_call_target="tpu_custom_call" | custom-call | flops 1 | bytes 1 | tf_op jit(solution)/shard_map/update_all/pallas_call | solution.py:983
  (279 shorter events, 65.4 us)
Async XLA Ops:
  3.2 8.8 %collective-permute-start.3 = (bf16[1,48,896]{2,1,0:T(8,128)(2,1)S(1)}, bf16[1,48,896]{2,1,0:T(8,128)(2,1)S(1)}, u32[]{:S(2)}, u32[]{:S(2)}) collective-permute-start(bf16[1,48,896]{2,1,0:T(8,128)(2,1)S(1)} %fusion.16), channel_id=1, source_target_pairs={{0,12},{1,13},{2,14},{3,15},{4,8},{5,9},{6,10},{7,11},{8,4},{9,5},... | collective-permute-start | bytes 258056 | tf_op jit(solution)/shard_map/ppermute | solution.py:68
  8.3 7.2 %collective-permute-start.2 = (bf16[1,48,896]{2,1,0:T(8,128)(2,1)S(1)}, bf16[1,48,896]{2,1,0:T(8,128)(2,1)S(1)}, u32[]{:S(2)}, u32[]{:S(2)}) collective-permute-start(bf16[1,48,896]{2,1,0:T(8,128)(2,1)S(1)} %fusion.16), channel_id=1, source_target_pairs={{0,8},{1,9},{2,10},{3,11},{4,12},{5,13},{6,14},{7,15},{8,0},{9,1},... | collective-permute-start | bytes 258056 | tf_op jit(solution)/shard_map/ppermute | solution.py:68
  8.3 7.2 %collective-permute-start.1 = (bf16[1,48,896]{2,1,0:T(8,128)(2,1)S(1)}, bf16[1,48,896]{2,1,0:T(8,128)(2,1)S(1)}, u32[]{:S(2)}, u32[]{:S(2)}) collective-permute-start(bf16[1,48,896]{2,1,0:T(8,128)(2,1)S(1)} %fusion.16), channel_id=1, source_target_pairs={{0,4},{1,5},{2,6},{3,7},{4,0},{5,1},{6,2},{7,3},{8,12},{9,13},{10,... | collective-permute-start | bytes 258056 | tf_op jit(solution)/shard_map/ppermute | solution.py:68
  9.0 20.2 %collective-permute-start.8 = (bf16[2,392,768]{2,1,0:T(8,128)(2,1)}, bf16[2,392,768]{2,1,0:T(8,128)(2,1)}, u32[]{:S(2)}, u32[]{:S(2)}) collective-permute-start(bf16[2,392,768]{2,1,0:T(8,128)(2,1)} %refs_0_.2), channel_id=1, source_target_pairs={{0,16},{1,17},{2,18},{3,19},{4,20},{5,21},{6,22},{7,23},{8,24},{9,... | collective-permute-start | bytes 3612680 | tf_op jit(solution)/shard_map/ppermute | solution.py:72
  15.6 13.4 %collective-permute-start.4 = (bf16[4,48,896]{2,1,0:T(8,128)(2,1)S(1)}, bf16[4,48,896]{2,1,0:T(8,128)(2,1)S(1)}, u32[]{:S(2)}, u32[]{:S(2)}) collective-permute-start(bf16[4,48,896]{2,1,0:T(8,128)(2,1)S(1)} %pad_maximum_fusion.8), channel_id=1, source_target_pairs={{0,1},{1,0},{2,3},{3,2},{4,5},{5,4},{6,7},{7,6},{8,9},{9,8},{10,11... | collective-permute-start | bytes 1032200 | tf_op jit(solution)/shard_map/ppermute | solution.py:68
  17.2 11.8 %collective-permute-start.7 = (bf16[1,48,768]{2,1,0:T(8,128)(2,1)S(1)}, bf16[1,48,768]{2,1,0:T(8,128)(2,1)S(1)}, u32[]{:S(2)}, u32[]{:S(2)}) collective-permute-start(bf16[1,48,768]{2,1,0:T(8,128)(2,1)S(1)} %maximum_bitcast_fusion.2), channel_id=1, source_target_pairs={{0,12},{1,13},{2,14},{3,15},{4,8},{5,9},{6,10},{7,11},{8,4},{9,5},... | collective-permute-start | bytes 221192 | tf_op jit(solution)/shard_map/ppermute | solution.py:68
  19.8 9.2 %collective-permute-start.6 = (bf16[1,48,768]{2,1,0:T(8,128)(2,1)S(1)}, bf16[1,48,768]{2,1,0:T(8,128)(2,1)S(1)}, u32[]{:S(2)}, u32[]{:S(2)}) collective-permute-start(bf16[1,48,768]{2,1,0:T(8,128)(2,1)S(1)} %maximum_bitcast_fusion.2), channel_id=1, source_target_pairs={{0,8},{1,9},{2,10},{3,11},{4,12},{5,13},{6,14},{7,15},{8,0},{9,1},... | collective-permute-start | bytes 221192 | tf_op jit(solution)/shard_map/ppermute | solution.py:68
  19.8 9.2 %collective-permute-start.5 = (bf16[1,48,768]{2,1,0:T(8,128)(2,1)S(1)}, bf16[1,48,768]{2,1,0:T(8,128)(2,1)S(1)}, u32[]{:S(2)}, u32[]{:S(2)}) collective-permute-start(bf16[1,48,768]{2,1,0:T(8,128)(2,1)S(1)} %maximum_bitcast_fusion.2), channel_id=1, source_target_pairs={{0,4},{1,5},{2,6},{3,7},{4,0},{5,1},{6,2},{7,3},{8,12},{9,13},{10,... | collective-permute-start | bytes 221192 | tf_op jit(solution)/shard_map/ppermute | solution.py:68
  29.1 12.7 %collective-permute-start.9 = (bf16[8,48,896]{2,1,0:T(8,128)(2,1)S(1)}, bf16[8,48,896]{2,1,0:T(8,128)(2,1)S(1)}, u32[]{:S(2)}, u32[]{:S(2)}) collective-permute-start(bf16[8,48,896]{2,1,0:T(8,128)(2,1)S(1)} %pad_maximum_fusion.4.refs_2_.refs_3_), channel_id=1, source_target_pairs={{0,2},{1,3},{2,0},{3,1},{4,6},{5,7},{6,4},{7,5},{8,10},{9,11},{10,... | collective-permute-start | bytes 2064392 | tf_op jit(solution)/shard_map/ppermute | solution.py:68
  30.8 10.2 %collective-permute-start.10 = (bf16[4,48,768]{2,1,0:T(8,128)(2,1)S(1)}, bf16[4,48,768]{2,1,0:T(8,128)(2,1)S(1)}, u32[]{:S(2)}, u32[]{:S(2)}) collective-permute-start(bf16[4,48,768]{2,1,0:T(8,128)(2,1)S(1)} %pad_maximum_fusion.9), channel_id=1, source_target_pairs={{0,1},{1,0},{2,3},{3,2},{4,5},{5,4},{6,7},{7,6},{8,9},{9,8},{10,11... | collective-permute-start | bytes 884744 | tf_op jit(solution)/shard_map/ppermute | solution.py:68
  41.9 18.6 %collective-permute-start.11 = (bf16[8,48,768]{2,1,0:T(8,128)(2,1)S(1)}, bf16[8,48,768]{2,1,0:T(8,128)(2,1)S(1)}, u32[]{:S(2)}, u32[]{:S(2)}) collective-permute-start(bf16[8,48,768]{2,1,0:T(8,128)(2,1)S(1)} %pad_maximum_fusion.5.refs_2_.refs_6_.refs_4_.refs_5_), channel_id=1, source_target_pairs={{0,2},{1,3},{2,0},{3,1},{4,6},{5,7},{6,4},{7,5},{8,10},{9,11},{10,... | collective-permute-start | bytes 1769480 | tf_op jit(solution)/shard_map/ppermute | solution.py:68
  43.0 17.4 %collective-permute-start.14 = (bf16[1,48,1536]{2,1,0:T(8,128)(2,1)S(1)}, bf16[1,48,1536]{2,1,0:T(8,128)(2,1)S(1)}, u32[]{:S(2)}, u32[]{:S(2)}) collective-permute-start(bf16[1,48,1536]{2,1,0:T(8,128)(2,1)S(1)} %get-tuple-element.268), channel_id=1, source_target_pairs={{0,12},{1,13},{2,14},{3,15},{4,8},{5,9},{6,10},{7,11},{8,4},{9,5},... | collective-permute-start | bytes 442376 | tf_op jit(solution)/shard_map/ppermute | solution.py:68
  45.2 15.3 %collective-permute-start.13 = (bf16[1,48,1536]{2,1,0:T(8,128)(2,1)S(1)}, bf16[1,48,1536]{2,1,0:T(8,128)(2,1)S(1)}, u32[]{:S(2)}, u32[]{:S(2)}) collective-permute-start(bf16[1,48,1536]{2,1,0:T(8,128)(2,1)S(1)} %get-tuple-element.268), channel_id=1, source_target_pairs={{0,8},{1,9},{2,10},{3,11},{4,12},{5,13},{6,14},{7,15},{8,0},{9,1},... | collective-permute-start | bytes 442376 | tf_op jit(solution)/shard_map/ppermute | solution.py:68
  45.2 15.3 %collective-permute-start.12 = (bf16[1,48,1536]{2,1,0:T(8,128)(2,1)S(1)}, bf16[1,48,1536]{2,1,0:T(8,128)(2,1)S(1)}, u32[]{:S(2)}, u32[]{:S(2)}) collective-permute-start(bf16[1,48,1536]{2,1,0:T(8,128)(2,1)S(1)} %get-tuple-element.268), channel_id=1, source_target_pairs={{0,4},{1,5},{2,6},{3,7},{4,0},{5,1},{6,2},{7,3},{8,12},{9,13},{10,... | collective-permute-start | bytes 442376 | tf_op jit(solution)/shard_map/ppermute | solution.py:68
  61.4 15.1 %collective-permute-start.15 = (bf16[4,48,1536]{2,1,0:T(8,128)(2,1)S(1)}, bf16[4,48,1536]{2,1,0:T(8,128)(2,1)S(1)}, u32[]{:S(2)}, u32[]{:S(2)}) collective-permute-start(bf16[4,48,1536]{2,1,0:T(8,128)(2,1)S(1)} %pad_maximum_fusion.6), channel_id=1, source_target_pairs={{0,1},{1,0},{2,3},{3,2},{4,5},{5,4},{6,7},{7,6},{8,9},{9,8},{10,11... | collective-permute-start | bytes 1769480 | tf_op jit(solution)/shard_map/ppermute | solution.py:68
  62.1 13.5 %collective-permute-start.18 = (bf16[1,48,1536]{2,1,0:T(8,128)(2,1)S(1)}, bf16[1,48,1536]{2,1,0:T(8,128)(2,1)S(1)}, u32[]{:S(2)}, u32[]{:S(2)}) collective-permute-start(bf16[1,48,1536]{2,1,0:T(8,128)(2,1)S(1)} %get-tuple-element.282), channel_id=1, source_target_pairs={{0,12},{1,13},{2,14},{3,15},{4,8},{5,9},{6,10},{7,11},{8,4},{9,5},... | collective-permute-start | bytes 442376 | tf_op jit(solution)/shard_map/ppermute | solution.py:68
  64.8 11.7 %collective-permute-start.17 = (bf16[1,48,1536]{2,1,0:T(8,128)(2,1)S(1)}, bf16[1,48,1536]{2,1,0:T(8,128)(2,1)S(1)}, u32[]{:S(2)}, u32[]{:S(2)}) collective-permute-start(bf16[1,48,1536]{2,1,0:T(8,128)(2,1)S(1)} %get-tuple-element.282), channel_id=1, source_target_pairs={{0,8},{1,9},{2,10},{3,11},{4,12},{5,13},{6,14},{7,15},{8,0},{9,1},... | collective-permute-start | bytes 442376 | tf_op jit(solution)/shard_map/ppermute | solution.py:68
  64.8 11.7 %collective-permute-start.16 = (bf16[1,48,1536]{2,1,0:T(8,128)(2,1)S(1)}, bf16[1,48,1536]{2,1,0:T(8,128)(2,1)S(1)}, u32[]{:S(2)}, u32[]{:S(2)}) collective-permute-start(bf16[1,48,1536]{2,1,0:T(8,128)(2,1)S(1)} %get-tuple-element.282), channel_id=1, source_target_pairs={{0,4},{1,5},{2,6},{3,7},{4,0},{5,1},{6,2},{7,3},{8,12},{9,13},{10,... | collective-permute-start | bytes 442376 | tf_op jit(solution)/shard_map/ppermute | solution.py:68
  76.8 23.3 %collective-permute-start.24 = (bf16[8,48,1536]{2,1,0:T(8,128)(2,1)S(1)}, bf16[8,48,1536]{2,1,0:T(8,128)(2,1)}, u32[]{:S(2)}, u32[]{:S(2)}) collective-permute-start(bf16[8,48,1536]{2,1,0:T(8,128)(2,1)S(1)} %pad_maximum_fusion.1.refs_4_), channel_id=1, source_target_pairs={{0,2},{1,3},{2,0},{3,1},{4,6},{5,7},{6,4},{7,5},{8,10},{9,11},{10,... | collective-permute-start | bytes 3538952 | tf_op jit(solution)/shard_map/ppermute | solution.py:68
  78.4 9.6 %collective-permute-start.19 = (bf16[2,392,128]{2,1,0:T(8,128)(2,1)S(1)}, bf16[2,392,128]{2,1,0:T(8,128)(2,1)S(1)}, u32[]{:S(2)}, u32[]{:S(2)}) collective-permute-start(bf16[2,392,128]{2,1,0:T(8,128)(2,1)S(1)} %copy-done.51), channel_id=1, source_target_pairs={{0,16},{1,17},{2,18},{3,19},{4,20},{5,21},{6,22},{7,23},{8,24},{9,... | collective-permute-start | bytes 602120 | tf_op jit(solution)/shard_map/ppermute | solution.py:72
  78.4 9.7 %collective-permute-start.20 = (bf16[2,392,128]{2,1,0:T(8,128)(2,1)}, bf16[2,392,128]{2,1,0:T(8,128)(2,1)S(1)}, u32[]{:S(2)}, u32[]{:S(2)}) collective-permute-start(bf16[2,392,128]{2,1,0:T(8,128)(2,1)} %get-tuple-element.292), channel_id=1, source_target_pairs={{0,16},{1,17},{2,18},{3,19},{4,20},{5,21},{6,22},{7,23},{8,24},{9,... | collective-permute-start | bytes 602120 | tf_op jit(solution)/shard_map/ppermute | solution.py:72
  88.0 12.0 %collective-permute-start.25 = (bf16[4,48,1536]{2,1,0:T(8,128)(2,1)S(1)}, bf16[4,48,1536]{2,1,0:T(8,128)(2,1)}, u32[]{:S(2)}, u32[]{:S(2)}) collective-permute-start(bf16[4,48,1536]{2,1,0:T(8,128)(2,1)S(1)} %pad_maximum_fusion.7), channel_id=1, source_target_pairs={{0,1},{1,0},{2,3},{3,2},{4,5},{5,4},{6,7},{7,6},{8,9},{9,8},{10,11... | collective-permute-start | bytes 1769480 | tf_op jit(solution)/shard_map/ppermute | solution.py:68
  103.5 26.6 %collective-permute-start.28 = (bf16[8,48,1536]{2,1,0:T(8,128)(2,1)}, bf16[8,48,1536]{2,1,0:T(8,128)(2,1)}, u32[]{:S(2)}, u32[]{:S(2)}) collective-permute-start(bf16[8,48,1536]{2,1,0:T(8,128)(2,1)} %pad_maximum_fusion.2.refs_4_), channel_id=1, source_target_pairs={{0,2},{1,3},{2,0},{3,1},{4,6},{5,7},{6,4},{7,5},{8,10},{9,11},{10,... | collective-permute-start | bytes 3538952 | tf_op jit(solution)/shard_map/ppermute | solution.py:68
  130.1 26.4 %collective-permute-start.30 = (bf16[2,392,768]{2,1,0:T(8,128)(2,1)}, bf16[2,392,768]{2,1,0:T(8,128)(2,1)}, u32[]{:S(2)}, u32[]{:S(2)}) collective-permute-start(bf16[2,392,768]{2,1,0:T(8,128)(2,1)} %get-tuple-element.322), channel_id=1, source_target_pairs={{0,16},{1,17},{2,18},{3,19},{4,20},{5,21},{6,22},{7,23},{8,24},{9,... | collective-permute-start | bytes 3612680 | tf_op jit(solution)/shard_map/ppermute | solution.py:72
  130.7 25.8 %collective-permute-start.31 = (bf16[2,392,768]{2,1,0:T(8,128)(2,1)}, bf16[2,392,768]{2,1,0:T(8,128)(2,1)S(1)}, u32[]{:S(2)}, u32[]{:S(2)}) collective-permute-start(bf16[2,392,768]{2,1,0:T(8,128)(2,1)} %get-tuple-element.323), channel_id=1, source_target_pairs={{0,16},{1,17},{2,18},{3,19},{4,20},{5,21},{6,22},{7,23},{8,24},{9,... | collective-permute-start | bytes 3612680 | tf_op jit(solution)/shard_map/ppermute | solution.py:72
  130.8 25.7 %collective-permute-start.29 = (bf16[8,48,1536]{2,1,0:T(8,128)(2,1)}, bf16[8,48,1536]{2,1,0:T(8,128)(2,1)}, u32[]{:S(2)}, u32[]{:S(2)}) collective-permute-start(bf16[8,48,1536]{2,1,0:T(8,128)(2,1)} %get-tuple-element.321), channel_id=1, source_target_pairs={{0,2},{1,3},{2,0},{3,1},{4,6},{5,7},{6,4},{7,5},{8,10},{9,11},{10,... | collective-permute-start | bytes 3538952 | tf_op jit(solution)/shard_map/ppermute | solution.py:68
  156.6 20.6 %collective-permute-start.34 = (bf16[8,48,1536]{2,1,0:T(8,128)(2,1)}, bf16[8,48,1536]{2,1,0:T(8,128)(2,1)}, u32[]{:S(2)}, u32[]{:S(2)}) collective-permute-start(bf16[8,48,1536]{2,1,0:T(8,128)(2,1)} %get-tuple-element.336), channel_id=1, source_target_pairs={{0,2},{1,3},{2,0},{3,1},{4,6},{5,7},{6,4},{7,5},{8,10},{9,11},{10,... | collective-permute-start | bytes 3538952 | tf_op jit(solution)/shard_map/ppermute | solution.py:68
  170.6 10.4 %collective-permute-start.33 = (bf16[2,392,384]{2,1,0:T(8,128)(2,1)}, bf16[2,392,384]{2,1,0:T(8,128)(2,1)S(1)}, u32[]{:S(2)}, u32[]{:S(2)}) collective-permute-start(bf16[2,392,384]{2,1,0:T(8,128)(2,1)} %get-tuple-element.333), channel_id=1, source_target_pairs={{0,16},{1,17},{2,18},{3,19},{4,20},{5,21},{6,22},{7,23},{8,24},{9,... | collective-permute-start | bytes 1806344 | tf_op jit(solution)/shard_map/ppermute | solution.py:72
  171.0 10.0 %collective-permute-start.35 = (bf16[4,48,1536]{2,1,0:T(8,128)(2,1)S(1)}, bf16[4,48,1536]{2,1,0:T(8,128)(2,1)}, u32[]{:S(2)}, u32[]{:S(2)}) collective-permute-start(bf16[4,48,1536]{2,1,0:T(8,128)(2,1)S(1)} %copy-done.29), channel_id=1, source_target_pairs={{0,1},{1,0},{2,3},{3,2},{4,5},{5,4},{6,7},{7,6},{8,9},{9,8},{10,11... | collective-permute-start | bytes 1769480 | tf_op jit(solution)/shard_map/ppermute | solution.py:68
  184.8 23.9 %collective-permute-start.41 = (bf16[2,392,768]{2,1,0:T(8,128)(2,1)}, bf16[2,392,768]{2,1,0:T(8,128)(2,1)}, u32[]{:S(2)}, u32[]{:S(2)}) collective-permute-start(bf16[2,392,768]{2,1,0:T(8,128)(2,1)} %get-tuple-element.354), channel_id=1, source_target_pairs={{0,16},{1,17},{2,18},{3,19},{4,20},{5,21},{6,22},{7,23},{8,24},{9,... | collective-permute-start | bytes 3612680 | tf_op jit(solution)/shard_map/ppermute | solution.py:72
  184.8 23.8 %collective-permute-start.36 = (bf16[4,48,1536]{2,1,0:T(8,128)(2,1)}, bf16[4,48,1536]{2,1,0:T(8,128)(2,1)S(1)}, u32[]{:S(2)}, u32[]{:S(2)}) collective-permute-start(bf16[4,48,1536]{2,1,0:T(8,128)(2,1)} %add_convert_fusion.1), channel_id=1, source_target_pairs={{0,1},{1,0},{2,3},{3,2},{4,5},{5,4},{6,7},{7,6},{8,9},{9,8},{10,11... | collective-permute-start | bytes 1769480 | tf_op jit(solution)/shard_map/ppermute | solution.py:68
  185.9 22.7 %collective-permute-start.40 = (bf16[16,48,384]{2,1,0:T(8,128)(2,1)}, bf16[16,48,384]{2,1,0:T(8,128)(2,1)S(1)}, u32[]{:S(2)}, u32[]{:S(2)}) collective-permute-start(bf16[16,48,384]{2,1,0:T(8,128)(2,1)} %get-tuple-element.353), channel_id=1, source_target_pairs={{0,16},{1,17},{2,18},{3,19},{4,20},{5,21},{6,22},{7,23},{8,24},{9,... | collective-permute-start | bytes 1769480 | tf_op jit(solution)/shard_map/ppermute | solution.py:72
  185.9 9.2 %collective-permute-start.37 = (bf16[1,48,1536]{2,1,0:T(8,128)(2,1)S(1)}, bf16[1,48,1536]{2,1,0:T(8,128)(2,1)S(1)}, u32[]{:S(2)}, u32[]{:S(2)}) collective-permute-start(bf16[1,48,1536]{2,1,0:T(8,128)(2,1)S(1)} %get-tuple-element.350), channel_id=1, source_target_pairs={{0,4},{1,5},{2,6},{3,7},{4,0},{5,1},{6,2},{7,3},{8,12},{9,13},{10,... | collective-permute-start | bytes 442376 | tf_op jit(solution)/shard_map/ppermute | solution.py:68
  185.9 22.7 %collective-permute-start.38 = (bf16[1,48,1536]{2,1,0:T(8,128)(2,1)S(1)}, bf16[1,48,1536]{2,1,0:T(8,128)(2,1)}, u32[]{:S(2)}, u32[]{:S(2)}) collective-permute-start(bf16[1,48,1536]{2,1,0:T(8,128)(2,1)S(1)} %get-tuple-element.351), channel_id=1, source_target_pairs={{0,8},{1,9},{2,10},{3,11},{4,12},{5,13},{6,14},{7,15},{8,0},{9,1},... | collective-permute-start | bytes 442376 | tf_op jit(solution)/shard_map/ppermute | solution.py:68
  195.1 13.5 %collective-permute-start.39 = (bf16[1,48,1536]{2,1,0:T(8,128)(2,1)S(1)}, bf16[1,48,1536]{2,1,0:T(8,128)(2,1)}, u32[]{:S(2)}, u32[]{:S(2)}) collective-permute-start(bf16[1,48,1536]{2,1,0:T(8,128)(2,1)S(1)} %get-tuple-element.352), channel_id=1, source_target_pairs={{0,12},{1,13},{2,14},{3,15},{4,8},{5,9},{6,10},{7,11},{8,4},{9,5},... | collective-permute-start | bytes 442376 | tf_op jit(solution)/shard_map/ppermute | solution.py:68
  213.0 17.6 %collective-permute-start.45 = (f32[48,1536]{1,0:T(8,128)}, f32[48,1536]{1,0:T(8,128)}, u32[]{:S(2)}, u32[]{:S(2)}) collective-permute-start(f32[48,1536]{1,0:T(8,128)} %add_bitcast_fusion.1.refs_0_), channel_id=1, source_target_pairs={{0,16},{1,17},{2,18},{3,19},{4,20},{5,21},{6,22},{7,23},{8,24},{9,... | collective-permute-start | bytes 884744 | tf_op jit(solution)/shard_map/ppermute | solution.py:72
  213.0 17.6 %collective-permute-start.42 = (bf16[1,48,1536]{2,1,0:T(8,128)(2,1)}, bf16[1,48,1536]{2,1,0:T(8,128)(2,1)}, u32[]{:S(2)}, u32[]{:S(2)}) collective-permute-start(bf16[1,48,1536]{2,1,0:T(8,128)(2,1)} %get-tuple-element.366), channel_id=1, source_target_pairs={{0,4},{1,5},{2,6},{3,7},{4,0},{5,1},{6,2},{7,3},{8,12},{9,13},{10,... | collective-permute-start | bytes 442376 | tf_op jit(solution)/shard_map/ppermute | solution.py:68
  213.1 17.5 %collective-permute-start.43 = (bf16[1,48,1536]{2,1,0:T(8,128)(2,1)}, bf16[1,48,1536]{2,1,0:T(8,128)(2,1)}, u32[]{:S(2)}, u32[]{:S(2)}) collective-permute-start(bf16[1,48,1536]{2,1,0:T(8,128)(2,1)} %get-tuple-element.367), channel_id=1, source_target_pairs={{0,8},{1,9},{2,10},{3,11},{4,12},{5,13},{6,14},{7,15},{8,0},{9,1},... | collective-permute-start | bytes 442376 | tf_op jit(solution)/shard_map/ppermute | solution.py:68
  216.0 14.6 %collective-permute-start.44 = (bf16[1,48,1536]{2,1,0:T(8,128)(2,1)}, bf16[1,48,1536]{2,1,0:T(8,128)(2,1)}, u32[]{:S(2)}, u32[]{:S(2)}) collective-permute-start(bf16[1,48,1536]{2,1,0:T(8,128)(2,1)} %get-tuple-element.368), channel_id=1, source_target_pairs={{0,12},{1,13},{2,14},{3,15},{4,8},{5,9},{6,10},{7,11},{8,4},{9,5},... | collective-permute-start | bytes 442376 | tf_op jit(solution)/shard_map/ppermute | solution.py:68
  233.0 13.4 %collective-permute-start.46 = (bf16[8,48,1152]{2,1,0:T(8,128)(2,1)}, bf16[8,48,1152]{2,1,0:T(8,128)(2,1)}, u32[]{:S(2)}, u32[]{:S(2)}) collective-permute-start(bf16[8,48,1152]{2,1,0:T(8,128)(2,1)} %pad_maximum_fusion.3), channel_id=1, source_target_pairs={{0,2},{1,3},{2,0},{3,1},{4,6},{5,7},{6,4},{7,5},{8,10},{9,11},{10,... | collective-permute-start | bytes 2654216 | tf_op jit(solution)/shard_map/ppermute | solution.py:68
  233.8 12.0 %collective-permute-start.47 = (f32[48,1536]{1,0:T(8,128)S(1)}, f32[48,1536]{1,0:T(8,128)S(1)}, u32[]{:S(2)}, u32[]{:S(2)}) collective-permute-start(f32[48,1536]{1,0:T(8,128)S(1)} %add_bitcast_fusion.refs_1_), channel_id=1, source_target_pairs={{0,16},{1,17},{2,18},{3,19},{4,20},{5,21},{6,22},{7,23},{8,24},{9,... | collective-permute-start | bytes 884744 | tf_op jit(solution)/shard_map/ppermute | solution.py:72
  248.2 11.7 %collective-permute-start.49 = (bf16[4,48,1152]{2,1,0:T(8,128)(2,1)}, bf16[4,48,1152]{2,1,0:T(8,128)(2,1)S(1)}, u32[]{:S(2)}, u32[]{:S(2)}) collective-permute-start(bf16[4,48,1152]{2,1,0:T(8,128)(2,1)} %fusion), channel_id=1, source_target_pairs={{0,1},{1,0},{2,3},{3,2},{4,5},{5,4},{6,7},{7,6},{8,9},{9,8},{10,11... | collective-permute-start | bytes 1327112 | tf_op jit(solution)/shard_map/ppermute | solution.py:68
  249.1 9.9 %collective-permute-start.48 = (bf16[8,48,384]{2,1,0:T(8,128)(2,1)}, bf16[8,48,384]{2,1,0:T(8,128)(2,1)S(1)}, u32[]{:S(2)}, u32[]{:S(2)}) collective-permute-start(bf16[8,48,384]{2,1,0:T(8,128)(2,1)} %get-tuple-element.388), channel_id=1, source_target_pairs={{0,2},{1,3},{2,0},{3,1},{4,6},{5,7},{6,4},{7,5},{8,10},{9,11},{10,... | collective-permute-start | bytes 884744 | tf_op jit(solution)/shard_map/ppermute | solution.py:68
  262.6 9.0 %collective-permute-start.54 = (bf16[2,392,768]{2,1,0:T(8,128)(2,1)S(1)}, bf16[2,392,768]{2,1,0:T(8,128)(2,1)S(1)}, u32[]{:S(2)}, u32[]{:S(2)}) collective-permute-start(bf16[2,392,768]{2,1,0:T(8,128)(2,1)S(1)} %copy-done.50), channel_id=1, source_target_pairs={{0,16},{1,17},{2,18},{3,19},{4,20},{5,21},{6,22},{7,23},{8,24},{9,... | collective-permute-start | bytes 3612680 | tf_op jit(solution)/shard_map/ppermute | solution.py:72
  262.6 15.7 %collective-permute-start.53 = (bf16[4,48,384]{2,1,0:T(8,128)(2,1)}, bf16[4,48,384]{2,1,0:T(8,128)(2,1)S(1)}, u32[]{:S(2)}, u32[]{:S(2)}) collective-permute-start(bf16[4,48,384]{2,1,0:T(8,128)(2,1)} %add_convert_fusion.4), channel_id=1, source_target_pairs={{0,1},{1,0},{2,3},{3,2},{4,5},{5,4},{6,7},{7,6},{8,9},{9,8},{10,11... | collective-permute-start | bytes 442376 | tf_op jit(solution)/shard_map/ppermute | solution.py:68
  267.2 19.2 %collective-permute-start.50 = (bf16[1,48,1152]{2,1,0:T(8,128)(2,1)}, bf16[1,48,1152]{2,1,0:T(8,128)(2,1)}, u32[]{:S(2)}, u32[]{:S(2)}) collective-permute-start(bf16[1,48,1152]{2,1,0:T(8,128)(2,1)} %get-tuple-element.394), channel_id=1, source_target_pairs={{0,4},{1,5},{2,6},{3,7},{4,0},{5,1},{6,2},{7,3},{8,12},{9,13},{10,... | collective-permute-start | bytes 331784 | tf_op jit(solution)/shard_map/ppermute | solution.py:68
  267.2 19.2 %collective-permute-start.51 = (bf16[1,48,1152]{2,1,0:T(8,128)(2,1)}, bf16[1,48,1152]{2,1,0:T(8,128)(2,1)}, u32[]{:S(2)}, u32[]{:S(2)}) collective-permute-start(bf16[1,48,1152]{2,1,0:T(8,128)(2,1)} %get-tuple-element.395), channel_id=1, source_target_pairs={{0,8},{1,9},{2,10},{3,11},{4,12},{5,13},{6,14},{7,15},{8,0},{9,1},... | collective-permute-start | bytes 331784 | tf_op jit(solution)/shard_map/ppermute | solution.py:68
  270.1 16.3 %collective-permute-start.52 = (bf16[1,48,1152]{2,1,0:T(8,128)(2,1)}, bf16[1,48,1152]{2,1,0:T(8,128)(2,1)}, u32[]{:S(2)}, u32[]{:S(2)}) collective-permute-start(bf16[1,48,1152]{2,1,0:T(8,128)(2,1)} %get-tuple-element.396), channel_id=1, source_target_pairs={{0,12},{1,13},{2,14},{3,15},{4,8},{5,9},{6,10},{7,11},{8,4},{9,5},... | collective-permute-start | bytes 331784 | tf_op jit(solution)/shard_map/ppermute | solution.py:68
  (72 other events, 438.2 us)
where the time goes:
time: 329 us; the launch traced here: 324 us
  Pallas kernels  181 us (55%)
  starting transfers between devices  64 us (19%)
  other arithmetic  34.2 us (10%)
  waiting for transfers between devices  28.4 us (9%)
  local copies, waits for them, and re-layouts  14.7 us (4%)
    ppermute x46, starting transfers between devices, flip(): return lax.ppermute(x, AXES, pairs)  60.7 us
    pallas_call x2, Pallas kernels, mlp_both(): pl.pallas_call(kernel, grid=(clips,), in_specs=[SMEM, SMEM, whole((1, hid...  48.3 us
    pallas_call x3, Pallas kernels, attend_back(): pl.pallas_call(kernel, grid=(clips,), in_specs=[SMEM, SMEM, qkv_spec, pl....  35.8 us
    pallas_call x3, Pallas kernels, attend_forward(): pl.pallas_call(kernel, grid=(clips,), in_specs=[SMEM, SMEM, SMEM] + sourc...  29.7 us
    ppermute x46, waiting for transfers between devices, flip(): return lax.ppermute(x, AXES, pairs)  25 us
    pallas_call x2, Pallas kernels, embed_rows(): pl.pallas_call(embed_kernel(each, len(tokens)), grid=(clips,), in_specs=[...  12.7 us
    pallas_call x1, Pallas kernels, norm_two_back(): pl.pallas_call(kernel, grid=(n,), in_specs=[SMEM, SMEM, whole((16, width)...  10.7 us
    pallas_call x1, Pallas kernels, attn_in_grad(): pl.pallas_call(kernel, grid=(clips,), in_specs=[SMEM] + [pl.BlockSpec((1,...  8.93 us
  transfers between devices with their start and end apart: 67, of which 20 were waited for; matrix products, arithmetic and copies ran while one was open for 8% of the time, Pallas kernels for 53%

commit v1 on v0

--- a/solution.py
+++ b/solution.py
@@ -15,12 +15,16 @@
 TRUST_RATE = 0.2
 AVERAGE_DECAY = 0.8
 NEG = -1000000000.0
-LEAST = 60
+LEAST = 0
 
 BF = jnp.bfloat16
 F32 = jnp.float32
 AXES = ("dp", "fsdp")
 SHORT = pl.CostEstimate(flops=1, bytes_accessed=1, transcendentals=0)
+def lasting(us):
+    return pl.CostEstimate(flops=us * 10**9, bytes_accessed=us * 3 * 10**6, transcendentals=0)
+
+
 ANY = pl.BlockSpec(memory_space=pl.ANY)
 SMEM = pl.BlockSpec(memory_space=pltpu.SMEM)
 
@@ -167,7 +171,7 @@
         out_specs=pl.BlockSpec((1, length, width), lambda i: (i, 0, 0)),
         out_shape=jax.ShapeDtypeStruct((clips, length, width), F32),
         compiler_params=params(24),
-        cost_estimate=SHORT,
+        cost_estimate=lasting(4),
         name="embed_rows",
     )(jnp.asarray(table), *tokens, *positions)
 
@@ -320,7 +324,7 @@
             pltpu.SemaphoreType.DMA((2 * blocks,)),
         ],
         compiler_params=params(48),
-        cost_estimate=SHORT,
+        cost_estimate=lasting(8),
         name="attend_forward",
     )(order, core, counts, *sources, *smalls, *pieces)
 
@@ -384,7 +388,7 @@
             pltpu.SemaphoreType.DMA((32,)),
         ],
         compiler_params=params(24),
-        cost_estimate=SHORT,
+        cost_estimate=lasting(6),
         name="project_norm",
     )(meta, small, embed, *mixes, *pieces, *others)
 
@@ -535,7 +539,7 @@
             pltpu.SemaphoreType.DMA((max(2 * n_blocks, 2),)),
         ],
         compiler_params=params(56),
-        cost_estimate=SHORT,
+        cost_estimate=lasting(23),
         name="mlp_both",
     )(order, counts, bias, *groups, *cots, *pieces)
 
@@ -611,7 +615,7 @@
             pltpu.SemaphoreType.DMA((32,)),
         ],
         compiler_params=params(32),
-        cost_estimate=SHORT,
+        cost_estimate=lasting(7),
         name="norm_two_back",
     )(meta, counts, small, resid, cot, *dms, *pieces, *others)
 
@@ -680,7 +684,7 @@
         out_shape=shapes,
         scratch_shapes=scratch,
         compiler_params=params(24),
-        cost_estimate=SHORT,
+        cost_estimate=lasting(5),
         name="out_weight_grad",
     )(meta, proj, *mixes)
 
@@ -795,7 +799,7 @@
         + shapes,
         scratch_shapes=scratch + [pltpu.SemaphoreType.DMA((blocks,))],
         compiler_params=params(48),
-        cost_estimate=SHORT,
+        cost_estimate=lasting(12),
         name="attend_back",
     )(order, counts, qkv, logs, *groups, *d_mixes)
 
@@ -858,7 +862,7 @@
         out_shape=shapes,
         scratch_shapes=[pltpu.VMEM((width, total), BF), pltpu.SemaphoreType.DMA((blocks,))],
         compiler_params=params(32),
-        cost_estimate=SHORT,
+        cost_estimate=lasting(7),
         name="attn_in_grad",
     )(order, *d_qkvs, *flat)
 
@@ -898,7 +902,7 @@
             jax.ShapeDtypeStruct((8, width), F32),
         ],
         compiler_params=params(24),
-        cost_estimate=SHORT,
+        cost_estimate=lasting(4),
         name="norm_one_back",
     )(small, embed, d_resid, *das)
 
@@ -990,7 +994,7 @@
         out_shape=[jax.ShapeDtypeStruct(x.shape, F32) for x in state]
         + [jax.ShapeDtypeStruct((1, 128), F32)],
         compiler_params=params(48),
-        cost_estimate=SHORT,
+        cost_estimate=lasting(6),
         name="update_all",
     )(place, sums, *halves_q, *halves_r, g_up, g_down, *state)
 
@@ -1010,7 +1014,7 @@
         out_specs=whole((1, 128)),
         out_shape=jax.ShapeDtypeStruct((1, 128), F32),
         compiler_params=params(24),
-        cost_estimate=SHORT,
+        cost_estimate=lasting(2),
         name="weight_squares",
     )(*state)
 
@@ -1062,7 +1066,7 @@
             jax.ShapeDtypeStruct((1, 128), F32),
         ],
         compiler_params=params(32),
-        cost_estimate=SHORT,
+        cost_estimate=lasting(3),
         name="interleave",
     )(place, *own, *other)
 
@@ -1103,7 +1107,7 @@
         out_specs=whole((16, width)),
         out_shape=jax.ShapeDtypeStruct((16, width), F32),
         compiler_params=params(16),
-        cost_estimate=SHORT,
+        cost_estimate=lasting(1),
         name="gather_sums",
     )(place, *ins)
 
@@ -1137,7 +1141,7 @@
             jax.ShapeDtypeStruct(sums.shape, F32),
         ],
         compiler_params=params(16),
-        cost_estimate=SHORT,
+        cost_estimate=lasting(2),
         name="last_shards",
     )(sums, keep_r, *recv_r, shard_q)
 

time: 329 us -> 292 us (0.89)
  Pallas kernels: 181 us -> 153 us
  other arithmetic: 34.2 us -> 19.8 us
    unnamed x107 -> x171, local copies, waits for them, and re-layouts: 3.43 us -> 11.4 us
    pallas_call x3, Pallas kernels: 29.7 us -> 23.2 us  [attend_forward(): pl.pallas_call(kernel, grid=(clips,), in_specs=[SMEM, SMEM, SMEM] + sourc...]
    pallas_call x1, Pallas kernels: 10.7 us -> 7.09 us  [norm_two_back(): pl.pallas_call(kernel, grid=(n,), in_specs=[SMEM, SMEM, whole((16, width)...]
  transfers between devices with their start and end apart: 67 -> 67, of which waited for: 20 -> 19; matrix products, arithmetic and copies ran while one was open for 8% -> 4% of each run, Pallas kernels for 53% -> 51%
where the time goes in v1:
time: 292 us; the launch traced here: 288 us
  Pallas kernels  153 us (52%)
  starting transfers between devices  66 us (23%)
  waiting for transfers between devices  31 us (11%)
  other arithmetic  19.8 us (7%)
  local copies, waits for them, and re-layouts  16.6 us (6%)
    ppermute x46, starting transfers between devices, flip(): return lax.ppermute(x, AXES, pairs)  60.7 us
    pallas_call x2, Pallas kernels, mlp_both(): pl.pallas_call(kernel, grid=(clips,), in_specs=[SMEM, SMEM, whole((1, hid...  48.5 us
    pallas_call x3, Pallas kernels, attend_back(): pl.pallas_call(kernel, grid=(clips,), in_specs=[SMEM, SMEM, qkv_spec, pl....  34.9 us
    ppermute x46, waiting for transfers between devices, flip(): return lax.ppermute(x, AXES, pairs)  27.2 us
    pallas_call x3, Pallas kernels, attend_forward(): pl.pallas_call(kernel, grid=(clips,), in_specs=[SMEM, SMEM, SMEM] + sourc...  23.2 us
    unnamed x171, local copies, waits for them, and re-layouts  11.4 us
    pallas_call x2, Pallas kernels, embed_rows(): pl.pallas_call(embed_kernel(each, len(tokens)), grid=(clips,), in_specs=[...  9.57 us
    pallas_call x1, Pallas kernels, norm_two_back(): pl.pallas_call(kernel, grid=(n,), in_specs=[SMEM, SMEM, whole((16, width)...  7.09 us
  transfers between devices with their start and end apart: 67, of which 19 were waited for; matrix products, arithmetic and copies ran while one was open for 4% of the time, Pallas kernels for 51%

profile of v1, /device:TPU:0, one launch (start us, length us, event | category | flops | bytes accessed | tf_op | source)
XLA Modules:
  0.0 288.4 jit_solution(12056279788775612702)
XLA Ops:
  3.3 5.1 %collective-permute-start.3 = (bf16[1,48,896]{2,1,0:T(8,128)(2,1)S(1)}, bf16[1,48,896]{2,1,0:T(8,128)(2,1)S(1)}, u32[]{:S(2)}, u32[]{:S(2)}) collective-permute-start(bf16[1,48,896]{2,1,0:T(8,128)(2,1)S(1)} %fusion.16), channel_id=1, source_target_pairs={{0,12},{1,13},{2,14},{3,15},{4,8},{5,9},{6,10},{7,11},{8,4},{9,5},... | collective-permute-start | bytes 258056 | tf_op jit(solution)/shard_map/ppermute | solution.py:72
  12.9 2.7 collective-permute-done.2
  15.7 2.7 collective-permute-start.7
  18.4 1.7 collective-permute-start.5
  21.6 4.3 %embed_rows.2.refs_0_.embed_ref = f32[2,392,768]{2,1,0:T(8,128)S(1)} custom-call(f32[8,768]{1,0:T(8,128)S(1)} %copy-done.34, bf16[2,392,768]{2,1,0:T(8,128)(2,1)S(1)} %copy-done.16, f32[2,392,1]{2,1,0:T(8,128)S(1)} %copy.50.refs_1_), custom_call_target="tpu_custom_call" | custom-call | flops 4000000000 | bytes 12000000 | tf_op jit(solution)/shard_map/embed_rows/pallas_call | solution.py:167
  27.6 1.6 collective-permute-start.9
  29.6 2.7 collective-permute-start.14
  32.3 1.7 collective-permute-start.12
  35.5 5.2 %embed_rows.3.refs_1_ = f32[2,392,768]{2,1,0:T(8,128)S(1)} custom-call(f32[8,768]{1,0:T(8,128)S(1)} %copy-done.34, bf16[2,392,768]{2,1,0:T(8,128)(2,1)} %collective-permute-done.8.refs_0_, f32[2,392,1]{2,1,0:T(8,128)S(1)} %copy.51.refs_1_), custom_call_target="tpu_custom_call" | custom-call | flops 4000000000 | bytes 12000000 | tf_op jit(solution)/shard_map/embed_rows/pallas_call | solution.py:167
  43.4 2.6 collective-permute-start.18
  46.1 9.5 %attend_forward.3 = (f32[16,768]{1,0:T(8,128)S(1)}, bf16[4,392,768]{2,1,0:T(8,128)(2,1)S(1)}, bf16[4,392,384]{2,1,0:T(8,128)(2,1)S(1)}, f32[4,2,392]{2,1,0:T(2,1...) custom-call(s32[16]{0:T(128)S(1)} %get-tuple-element.474.order_ref, s32[1]{0:T(128)} %bitcast.8.core_ref, ...), custom_call_target="tpu_custom_call" | custom-call | flops 8000000000 | bytes 24000000 | tf_op jit(solution)/shard_map/attend_forward/pallas_call | solution.py:312
  56.3 1.7 collective-permute-start.16
  58.2 1.5 collective-permute-start.15
  59.7 6.9 %attend_forward.4 = (bf16[4,392,384]{2,1,0:T(8,128)(2,1)S(1)}, f32[4,2,392]{2,1,0:T(2,128)S(1)}, bf16[2,392,128]{2,1,0:T(8,128)(2,1)S(1)}, bf16[2,392,128]{2,1,0:T(8,128)(2,1)S(1)}) custom-call(s32[16]{0:T(128)S(1)} %get-tuple-element.474.order_ref, s32[1]{0:T(128)} %bitcast.8.core_ref, s32[4]{0:T(128)S(1)} %pad_add_fusion.1.count_ref, ...), custom_call_target="tpu_custom_call" | custom-call | flops 8000000000 | bytes 24000000 | tf_op jit(solution)/shard_map/attend_forward/pallas_call | solution.py:312
  70.6 6.8 %attend_forward.5 = (bf16[4,392,384]{2,1,0:T(8,128)(2,1)S(1)}, f32[4,2,392]{2,1,0:T(2,128)S(1)}, bf16[2,392,128]{2,1,0:T(8,128)(2,1)S(1)}, bf16[2,392,128]{2,1,0:T(8,128)(2,1)S(1)}) custom-call(s32[16]{0:T(128)S(1)} %get-tuple-element.474.order_ref, s32[1]{0:T(128)} %bitcast.8.core_ref, s32[4]{0:T(128)S(1)} %pad_add_fusion.1.count_ref, ...), custom_call_target="tpu_custom_call" | custom-call | flops 8000000000 | bytes 24000000 | tf_op jit(solution)/shard_map/attend_forward/pallas_call | solution.py:312
  80.9 6.8 %project_norm.1 = (f32[2,392,768]{2,1,0:T(8,128)S(1)}, bf16[2,392,768]{2,1,0:T(8,128)(2,1)}) custom-call(s32[33]{0:T(128)S(1)} %pad_add_fusion.2.meta_ref, f32[16,768]{1,0:T(8,128)S(1)} %get-tuple-element.271.refs_1_.small_ref, f32[2,392,768]{2,1,0:T(8,128)S(1)} %copy-done.38, bf16[2,392,128]{2,1,0:T(8,128)(2,1)S(1)} %get-tuple-element.272.refs_0_, ...), custom_call_target="tpu_custom_call" | custom-call | flops 6000000000 | bytes 18000000 | tf_op jit(solution)/shard_map/project_norm/pallas_call | solution.py:377
  87.7 4.0 %collective-permute-done.25 = bf16[4,48,1536]{2,1,0:T(8,128)(2,1)} collective-permute-done((bf16[4,48,1536]{2,1,0:T(8,128)(2,1)S(1)}, bf16[4,48,1536]{2,1,0:T(8,128)(2,1)}, u32[]{:S(2)}, u32[]{:S(2)}) %collective-permute-start.25) | collective-permute-done | bytes 589856 | tf_op jit(solution)/shard_map/ppermute | solution.py:72
  97.7 23.9 %mlp_both.2 = (f32[2,392,768]{2,1,0:T(8,128)}, f32[2,392,768]{2,1,0:T(8,128)}, bf16[2,392,768]{2,1,0:T(8,128)(2,1)}, bf16[2,392,768]{2,1,0:T(8,128)(2,1)}, f32[1...) custom-call(s32[16]{0:T(128)} %copy-done.14, s32[4]{0:T(128)} %copy-done.35, ...), custom_call_target="tpu_custom_call" | custom-call | flops 23000000512 | bytes 69000000 | tf_op jit(solution)/shard_map/mlp_both/pallas_call | solution.py:526
  124.2 24.6 %mlp_both.3 = (f32[2,392,768]{2,1,0:T(8,128)}, f32[2,392,768]{2,1,0:T(8,128)}, bf16[2,392,768]{2,1,0:T(8,128)(2,1)}, bf16[2,392,768]{2,1,0:T(8,128)(2,1)}, f32[1...) custom-call(s32[16]{0:T(128)} %copy-done.14, s32[4]{0:T(128)} %copy-done.35, ...), custom_call_target="tpu_custom_call" | custom-call | flops 23000000512 | bytes 69000000 | tf_op jit(solution)/shard_map/mlp_both/pallas_call | solution.py:526
  150.0 1.5 add_convert_fusion.2
  152.2 1.7 copy-done.44
  153.9 7.1 %norm_two_back.1 = (bf16[2,392,384]{2,1,0:T(8,128)(2,1)S(1)}, bf16[2,392,384]{2,1,0:T(8,128)(2,1)S(1)}, bf16[2,392,768]{2,1,0:T(8,128)(2,1)S(1)}, f32[2,392,768]{2,1,0:T(8,128)S(1)}, f32[8,768]{1,0:T(8,128)S(1)}) custom-call(s32[33]{0:T(128)S(1)} %pad_add_fusion.2.meta_ref, s32[2]{0:T(128)S(1)} %copy-done.33, ...), custom_call_target="tpu_custom_call" | custom-call | flops 7000000000 | bytes 21000000 | tf_op jit(solution)/shard_map/norm_two_back/pallas_call | solution.py:600
  162.1 5.8 %out_weight_grad.1 = (f32[16,48,384]{2,1,0:T(8,128)S(1)}, bf16[16,48,384]{2,1,0:T(8,128)(2,1)S(1)}) custom-call(s32[33]{0:T(128)S(1)} %pad_add_fusion.2.meta_ref, bf16[2,392,768]{2,1,0:T(8,128)(2,1)S(1)} %get-tuple-element.334.proj_ref, bf16[2,392,128]{2,1,0:T(8,128)(2,1)S(1)} %copy-done.53, bf16[2,392,128]{2,1,0:T(8,128)(2,1)S(1)} %copy-done.55, ...), custom_call_target="tpu_custom_call" | custom-call | flops 5000000000 | bytes 15000000 | tf_op jit(solution)/shard_map/out_weight_grad/pallas_call | solution.py:679
  167.9 3.4 %collective-permute-done.35 = bf16[4,48,1536]{2,1,0:T(8,128)(2,1)S(1)} collective-permute-done((bf16[4,48,1536]{2,1,0:T(8,128)(2,1)S(1)}, bf16[4,48,1536]{2,1,0:T(8,128)(2,1)S(1)}, u32[]{:S(2)}, u32[]{:S(2)}) %collective-permute-start.35) | collective-permute-done | bytes 589856 | tf_op jit(solution)/shard_map/ppermute | solution.py:72
  171.3 1.6 add_convert_fusion.8
  174.0 2.8 collective-permute-start.38
  178.6 3.7 %collective-permute-done.37 = bf16[1,48,1536]{2,1,0:T(8,128)(2,1)S(1)} collective-permute-done((bf16[1,48,1536]{2,1,0:T(8,128)(2,1)S(1)}, bf16[1,48,1536]{2,1,0:T(8,128)(2,1)S(1)}, u32[]{:S(2)}, u32[]{:S(2)}) %collective-permute-start.37) | collective-permute-done | bytes 147488 | tf_op jit(solution)/shard_map/ppermute | solution.py:72
  182.4 11.8 %attend_back.3 = (bf16[4,392,384]{2,1,0:T(8,128)(2,1)S(1)}, f32[1,384]{1,0:T(1,128)S(1)}, f32[8,48,384]{2,1,0:T(8,128)S(1)}, bf16[8,48,384]{2,1,0:T(8,128)(2,1)S(1)}) custom-call(s32[16]{0:T(128)S(1)} %copy-done.15, s32[4]{0:T(128)S(1)} %copy-done.36, bf16[4,392,384]{2,1,0:T(8,128)(2,1)S(1)} %copy-done.47, f32[4,2,392]{2,1,0:T(2,128)S(1)} %copy-done.63, ...), custom_call_target="tpu_custom_call" | custom-call | flops 12000000000 | bytes 36000000 | tf_op jit(solution)/shard_map/attend_back/pallas_call | solution.py:783
  194.3 1.7 add_convert_fusion.5
  197.3 2.2 collective-permute-start.43
  199.5 2.2 collective-permute-start.44
  202.9 11.5 %attend_back.4 = (bf16[4,392,384]{2,1,0:T(8,128)(2,1)S(1)}, f32[1,384]{1,0:T(1,128)S(1)}, f32[8,48,384]{2,1,0:T(8,128)S(1)}, bf16[8,48,384]{2,1,0:T(8,128)(2,1)S(1)}) custom-call(s32[16]{0:T(128)S(1)} %copy-done.15, s32[4]{0:T(128)S(1)} %copy-done.36, bf16[4,392,384]{2,1,0:T(8,128)(2,1)S(1)} %copy-done.49, f32[4,2,392]{2,1,0:T(2,128)S(1)} %copy-done.65, ...), custom_call_target="tpu_custom_call" | custom-call | flops 12000000000 | bytes 36000000 | tf_op jit(solution)/shard_map/attend_back/pallas_call | solution.py:783
  217.7 11.5 %attend_back.5 = (bf16[4,392,384]{2,1,0:T(8,128)(2,1)S(1)}, f32[1,384]{1,0:T(1,128)S(1)}, f32[8,48,384]{2,1,0:T(8,128)S(1)}, bf16[8,48,384]{2,1,0:T(8,128)(2,1)S(1)}) custom-call(s32[16]{0:T(128)S(1)} %copy-done.15, s32[4]{0:T(128)S(1)} %copy-done.36, bf16[4,392,384]{2,1,0:T(8,128)(2,1)S(1)} %copy-done.51, f32[4,2,392]{2,1,0:T(2,128)S(1)} %copy-done.67, ...), custom_call_target="tpu_custom_call" | custom-call | flops 12000000000 | bytes 36000000 | tf_op jit(solution)/shard_map/attend_back/pallas_call | solution.py:783
  233.7 5.7 %attn_in_grad.1 = (f32[2,392,768]{2,1,0:T(8,128)S(1)}, bf16[2,392,768]{2,1,0:T(8,128)(2,1)S(1)}) custom-call(s32[16]{0:T(128)S(1)} %copy-done.15, bf16[4,392,384]{2,1,0:T(8,128)(2,1)S(1)} %get-tuple-element.345.refs_0_, bf16[4,392,384]{2,1,0:T(8,128)(2,1)S(1)} %get-tuple-element.361.refs_1_, bf16[4,392,384]{2,1,0:T(8,128)(2,1)S(1)} %get-tuple-element.386.refs_2_, ...), custom_call_target="tpu_custom_call" | custom-call | flops 7000000000 | bytes 21000000 | tf_op jit(solution)/shard_map/attn_in_grad/pallas_call | solution.py:855
  239.4 2.3 collective-permute-done.48.refs_0_
  244.7 2.2 collective-permute-start.51
  246.9 2.2 collective-permute-start.52
  250.3 3.2 %norm_one_back.1 = (f32[2,392,768]{2,1,0:T(8,128)}, f32[8,768]{1,0:T(8,128)S(1)}) custom-call(f32[16,768]{1,0:T(8,128)S(1)} %get-tuple-element.271.refs_1_.small_ref, f32[2,392,768]{2,1,0:T(8,128)S(1)} %copy-done.39, f32[2,392,768]{2,1,0:T(8,128)S(1)} %copy-done.41, f32[2,392,768]{2,1,0:T(8,128)S(1)} %get-tuple-element.399.refs_0_, ...), custom_call_target="tpu_custom_call" | custom-call | flops 4000000000 | bytes 12000000 | tf_op jit(solution)/shard_map/norm_one_back/pallas_call | solution.py:895
  254.4 3.2 %add_convert_fusion = bf16[2,392,768]{2,1,0:T(8,128)(2,1)} fusion(bf16[2,392,768]{2,1,0:T(8,128)(2,1)S(1)} %copy-done.73, bf16[2,392,768]{2,1,0:T(8,128)(2,1)} %collective-permute-done.31, f32[2,392,768]{2,1,0:T(8,128)S(1)} %copy-done.69, f32[2,392,768]{2,1,0:T(8,128)S(1)} %copy-done.68, f32[2,392,768]{2,1,0:T(8,128)S(1)} %get-tuple-element.403.resid_ref, ...), kind=kLoop, calls=%fused_computation | loop fusion | flops 4816896 | bytes 10841088 | tf_op jit(solution)/shard_map/convert_element_type | solution.py:1373
  258.7 1.8 collective-permute-start.56
  260.5 2.2 collective-permute-start.57
  263.8 2.4 collective-permute-done.57.refs_4_
  267.7 2.2 collective-permute-start.61
  270.0 2.2 collective-permute-start.59
  272.2 1.8 collective-permute-done.61
  273.9 1.5 collective-permute-done.60
  279.5 1.5 collective-permute-done.64
  282.4 5.3 %update_all.1 = (f32[48,2304]{1,0:T(8,128)}, f32[48,768]{1,0:T(8,128)}, f32[48,3072]{1,0:T(8,128)}, f32[192,768]{1,0:T(8,128)}, f32[12,48]{1,0:T(8,128)}, /*inde...) custom-call(s32[2]{0:T(128)S(1)} %pad_add_fusion.3.place_ref, ...), custom_call_target="tpu_custom_call" | custom-call | flops 6000000000 | bytes 18000000 | tf_op jit(solution)/shard_map/update_all/pallas_call | solution.py:987
  (343 shorter events, 61.5 us)
Async XLA Ops:
  3.3 9.6 %collective-permute-start.3 = (bf16[1,48,896]{2,1,0:T(8,128)(2,1)S(1)}, bf16[1,48,896]{2,1,0:T(8,128)(2,1)S(1)}, u32[]{:S(2)}, u32[]{:S(2)}) collective-permute-start(bf16[1,48,896]{2,1,0:T(8,128)(2,1)S(1)} %fusion.16), channel_id=1, source_target_pairs={{0,12},{1,13},{2,14},{3,15},{4,8},{5,9},{6,10},{7,11},{8,4},{9,5},... | collective-permute-start | bytes 258056 | tf_op jit(solution)/shard_map/ppermute | solution.py:72
  8.4 7.2 %collective-permute-start.2 = (bf16[1,48,896]{2,1,0:T(8,128)(2,1)S(1)}, bf16[1,48,896]{2,1,0:T(8,128)(2,1)S(1)}, u32[]{:S(2)}, u32[]{:S(2)}) collective-permute-start(bf16[1,48,896]{2,1,0:T(8,128)(2,1)S(1)} %fusion.16), channel_id=1, source_target_pairs={{0,8},{1,9},{2,10},{3,11},{4,12},{5,13},{6,14},{7,15},{8,0},{9,1},... | collective-permute-start | bytes 258056 | tf_op jit(solution)/shard_map/ppermute | solution.py:72
  9.0 18.5 %collective-permute-start.8 = (bf16[2,392,768]{2,1,0:T(8,128)(2,1)}, bf16[2,392,768]{2,1,0:T(8,128)(2,1)}, u32[]{:S(2)}, u32[]{:S(2)}) collective-permute-start(bf16[2,392,768]{2,1,0:T(8,128)(2,1)} %refs_0_.2), channel_id=1, source_target_pairs={{0,16},{1,17},{2,18},{3,19},{4,20},{5,21},{6,22},{7,23},{8,24},{9,... | collective-permute-start | bytes 3612680 | tf_op jit(solution)/shard_map/ppermute | solution.py:76
  15.7 11.7 %collective-permute-start.7 = (bf16[1,48,768]{2,1,0:T(8,128)(2,1)S(1)}, bf16[1,48,768]{2,1,0:T(8,128)(2,1)S(1)}, u32[]{:S(2)}, u32[]{:S(2)}) collective-permute-start(bf16[1,48,768]{2,1,0:T(8,128)(2,1)S(1)} %maximum_bitcast_fusion.2), channel_id=1, source_target_pairs={{0,12},{1,13},{2,14},{3,15},{4,8},{5,9},{6,10},{7,11},{8,4},{9,5},... | collective-permute-start | bytes 221192 | tf_op jit(solution)/shard_map/ppermute | solution.py:72
  18.4 9.0 %collective-permute-start.6 = (bf16[1,48,768]{2,1,0:T(8,128)(2,1)S(1)}, bf16[1,48,768]{2,1,0:T(8,128)(2,1)S(1)}, u32[]{:S(2)}, u32[]{:S(2)}) collective-permute-start(bf16[1,48,768]{2,1,0:T(8,128)(2,1)S(1)} %maximum_bitcast_fusion.2), channel_id=1, source_target_pairs={{0,8},{1,9},{2,10},{3,11},{4,12},{5,13},{6,14},{7,15},{8,0},{9,1},... | collective-permute-start | bytes 221192 | tf_op jit(solution)/shard_map/ppermute | solution.py:72
  18.4 9.0 %collective-permute-start.5 = (bf16[1,48,768]{2,1,0:T(8,128)(2,1)S(1)}, bf16[1,48,768]{2,1,0:T(8,128)(2,1)S(1)}, u32[]{:S(2)}, u32[]{:S(2)}) collective-permute-start(bf16[1,48,768]{2,1,0:T(8,128)(2,1)S(1)} %maximum_bitcast_fusion.2), channel_id=1, source_target_pairs={{0,4},{1,5},{2,6},{3,7},{4,0},{5,1},{6,2},{7,3},{8,12},{9,13},{10,... | collective-permute-start | bytes 221192 | tf_op jit(solution)/shard_map/ppermute | solution.py:72
  20.1 7.3 %collective-permute-start.4 = (bf16[4,48,896]{2,1,0:T(8,128)(2,1)S(1)}, bf16[4,48,896]{2,1,0:T(8,128)(2,1)S(1)}, u32[]{:S(2)}, u32[]{:S(2)}) collective-permute-start(bf16[4,48,896]{2,1,0:T(8,128)(2,1)S(1)} %pad_maximum_fusion.8), channel_id=1, source_target_pairs={{0,1},{1,0},{2,3},{3,2},{4,5},{5,4},{6,7},{7,6},{8,9},{9,8},{10,11... | collective-permute-start | bytes 1032200 | tf_op jit(solution)/shard_map/ppermute | solution.py:72
  27.6 14.6 %collective-permute-start.9 = (bf16[8,48,896]{2,1,0:T(8,128)(2,1)S(1)}, bf16[8,48,896]{2,1,0:T(8,128)(2,1)S(1)}, u32[]{:S(2)}, u32[]{:S(2)}) collective-permute-start(bf16[8,48,896]{2,1,0:T(8,128)(2,1)S(1)} %pad_maximum_fusion.4.refs_2_.refs_3_), channel_id=1, source_target_pairs={{0,2},{1,3},{2,0},{3,1},{4,6},{5,7},{6,4},{7,5},{8,10},{9,11},{10,... | collective-permute-start | bytes 2064392 | tf_op jit(solution)/shard_map/ppermute | solution.py:72
  29.6 26.6 %collective-permute-start.14 = (bf16[1,48,1536]{2,1,0:T(8,128)(2,1)S(1)}, bf16[1,48,1536]{2,1,0:T(8,128)(2,1)S(1)}, u32[]{:S(2)}, u32[]{:S(2)}) collective-permute-start(bf16[1,48,1536]{2,1,0:T(8,128)(2,1)S(1)} %get-tuple-element.268), channel_id=1, source_target_pairs={{0,12},{1,13},{2,14},{3,15},{4,8},{5,9},{6,10},{7,11},{8,4},{9,5},... | collective-permute-start | bytes 442376 | tf_op jit(solution)/shard_map/ppermute | solution.py:72
  32.3 24.0 %collective-permute-start.13 = (bf16[1,48,1536]{2,1,0:T(8,128)(2,1)S(1)}, bf16[1,48,1536]{2,1,0:T(8,128)(2,1)S(1)}, u32[]{:S(2)}, u32[]{:S(2)}) collective-permute-start(bf16[1,48,1536]{2,1,0:T(8,128)(2,1)S(1)} %get-tuple-element.268), channel_id=1, source_target_pairs={{0,8},{1,9},{2,10},{3,11},{4,12},{5,13},{6,14},{7,15},{8,0},{9,1},... | collective-permute-start | bytes 442376 | tf_op jit(solution)/shard_map/ppermute | solution.py:72
  32.3 25.7 %collective-permute-start.12 = (bf16[1,48,1536]{2,1,0:T(8,128)(2,1)S(1)}, bf16[1,48,1536]{2,1,0:T(8,128)(2,1)S(1)}, u32[]{:S(2)}, u32[]{:S(2)}) collective-permute-start(bf16[1,48,1536]{2,1,0:T(8,128)(2,1)S(1)} %get-tuple-element.268), channel_id=1, source_target_pairs={{0,4},{1,5},{2,6},{3,7},{4,0},{5,1},{6,2},{7,3},{8,12},{9,13},{10,... | collective-permute-start | bytes 442376 | tf_op jit(solution)/shard_map/ppermute | solution.py:72
  34.0 8.1 %collective-permute-start.10 = (bf16[4,48,768]{2,1,0:T(8,128)(2,1)S(1)}, bf16[4,48,768]{2,1,0:T(8,128)(2,1)S(1)}, u32[]{:S(2)}, u32[]{:S(2)}) collective-permute-start(bf16[4,48,768]{2,1,0:T(8,128)(2,1)S(1)} %pad_maximum_fusion.9), channel_id=1, source_target_pairs={{0,1},{1,0},{2,3},{3,2},{4,5},{5,4},{6,7},{7,6},{8,9},{9,8},{10,11... | collective-permute-start | bytes 884744 | tf_op jit(solution)/shard_map/ppermute | solution.py:72
  42.3 15.8 %collective-permute-start.11 = (bf16[8,48,768]{2,1,0:T(8,128)(2,1)S(1)}, bf16[8,48,768]{2,1,0:T(8,128)(2,1)S(1)}, u32[]{:S(2)}, u32[]{:S(2)}) collective-permute-start(bf16[8,48,768]{2,1,0:T(8,128)(2,1)S(1)} %pad_maximum_fusion.5.refs_2_.refs_6_.refs_4_.refs_5_), channel_id=1, source_target_pairs={{0,2},{1,3},{2,0},{3,1},{4,6},{5,7},{6,4},{7,5},{8,10},{9,11},{10,... | collective-permute-start | bytes 1769480 | tf_op jit(solution)/shard_map/ppermute | solution.py:72
  43.4 23.8 %collective-permute-start.18 = (bf16[1,48,1536]{2,1,0:T(8,128)(2,1)}, bf16[1,48,1536]{2,1,0:T(8,128)(2,1)S(1)}, u32[]{:S(2)}, u32[]{:S(2)}) collective-permute-start(bf16[1,48,1536]{2,1,0:T(8,128)(2,1)} %get-tuple-element.282), channel_id=1, source_target_pairs={{0,12},{1,13},{2,14},{3,15},{4,8},{5,9},{6,10},{7,11},{8,4},{9,5},... | collective-permute-start | bytes 442376 | tf_op jit(solution)/shard_map/ppermute | solution.py:72
  56.2 11.0 %collective-permute-start.17 = (bf16[1,48,1536]{2,1,0:T(8,128)(2,1)}, bf16[1,48,1536]{2,1,0:T(8,128)(2,1)S(1)}, u32[]{:S(2)}, u32[]{:S(2)}) collective-permute-start(bf16[1,48,1536]{2,1,0:T(8,128)(2,1)} %get-tuple-element.282), channel_id=1, source_target_pairs={{0,8},{1,9},{2,10},{3,11},{4,12},{5,13},{6,14},{7,15},{8,0},{9,1},... | collective-permute-start | bytes 442376 | tf_op jit(solution)/shard_map/ppermute | solution.py:72
  56.3 11.4 %collective-permute-start.16 = (bf16[1,48,1536]{2,1,0:T(8,128)(2,1)}, bf16[1,48,1536]{2,1,0:T(8,128)(2,1)S(1)}, u32[]{:S(2)}, u32[]{:S(2)}) collective-permute-start(bf16[1,48,1536]{2,1,0:T(8,128)(2,1)} %get-tuple-element.282), channel_id=1, source_target_pairs={{0,4},{1,5},{2,6},{3,7},{4,0},{5,1},{6,2},{7,3},{8,12},{9,13},{10,... | collective-permute-start | bytes 442376 | tf_op jit(solution)/shard_map/ppermute | solution.py:72
  58.2 20.9 %collective-permute-start.19 = (bf16[2,392,128]{2,1,0:T(8,128)(2,1)S(1)}, bf16[2,392,128]{2,1,0:T(8,128)(2,1)S(1)}, u32[]{:S(2)}, u32[]{:S(2)}) collective-permute-start(bf16[2,392,128]{2,1,0:T(8,128)(2,1)S(1)} %get-tuple-element.291), channel_id=1, source_target_pairs={{0,16},{1,17},{2,18},{3,19},{4,20},{5,21},{6,22},{7,23},{8,24},{9,... | collective-permute-start | bytes 602120 | tf_op jit(solution)/shard_map/ppermute | solution.py:76
  58.2 9.9 %collective-permute-start.15 = (bf16[4,48,1536]{2,1,0:T(8,128)(2,1)S(1)}, bf16[4,48,1536]{2,1,0:T(8,128)(2,1)S(1)}, u32[]{:S(2)}, u32[]{:S(2)}) collective-permute-start(bf16[4,48,1536]{2,1,0:T(8,128)(2,1)S(1)} %pad_maximum_fusion.6), channel_id=1, source_target_pairs={{0,1},{1,0},{2,3},{3,2},{4,5},{5,4},{6,7},{7,6},{8,9},{9,8},{10,11... | collective-permute-start | bytes 1769480 | tf_op jit(solution)/shard_map/ppermute | solution.py:72
  67.2 13.2 %collective-permute-start.22 = (bf16[8,48,384]{2,1,0:T(8,128)(2,1)S(1)}, bf16[8,48,384]{2,1,0:T(8,128)(2,1)S(1)}, u32[]{:S(2)}, u32[]{:S(2)}) collective-permute-start(bf16[8,48,384]{2,1,0:T(8,128)(2,1)S(1)} %slice.227), channel_id=1, source_target_pairs={{0,16},{1,17},{2,18},{3,19},{4,20},{5,21},{6,22},{7,23},{8,24},{9,... | collective-permute-start | bytes 884744 | tf_op jit(solution)/shard_map/ppermute | solution.py:76
  67.2 13.2 %collective-permute-start.23 = (bf16[8,48,384]{2,1,0:T(8,128)(2,1)S(1)}, bf16[8,48,384]{2,1,0:T(8,128)(2,1)S(1)}, u32[]{:S(2)}, u32[]{:S(2)}) collective-permute-start(bf16[8,48,384]{2,1,0:T(8,128)(2,1)S(1)} %slice.228), channel_id=1, source_target_pairs={{0,16},{1,17},{2,18},{3,19},{4,20},{5,21},{6,22},{7,23},{8,24},{9,... | collective-permute-start | bytes 884744 | tf_op jit(solution)/shard_map/ppermute | solution.py:76
  69.5 9.6 %collective-permute-start.20 = (bf16[2,392,128]{2,1,0:T(8,128)(2,1)S(1)}, bf16[2,392,128]{2,1,0:T(8,128)(2,1)S(1)}, u32[]{:S(2)}, u32[]{:S(2)}) collective-permute-start(bf16[2,392,128]{2,1,0:T(8,128)(2,1)S(1)} %get-tuple-element.292), channel_id=1, source_target_pairs={{0,16},{1,17},{2,18},{3,19},{4,20},{5,21},{6,22},{7,23},{8,24},{9,... | collective-permute-start | bytes 602120 | tf_op jit(solution)/shard_map/ppermute | solution.py:76
  69.6 22.2 %collective-permute-start.24 = (bf16[8,48,1536]{2,1,0:T(8,128)(2,1)S(1)}, bf16[8,48,1536]{2,1,0:T(8,128)(2,1)S(1)}, u32[]{:S(2)}, u32[]{:S(2)}) collective-permute-start(bf16[8,48,1536]{2,1,0:T(8,128)(2,1)S(1)} %pad_maximum_fusion.1.refs_4_), channel_id=1, source_target_pairs={{0,2},{1,3},{2,0},{3,1},{4,6},{5,7},{6,4},{7,5},{8,10},{9,11},{10,... | collective-permute-start | bytes 3538952 | tf_op jit(solution)/shard_map/ppermute | solution.py:72
  79.8 11.9 %collective-permute-start.25 = (bf16[4,48,1536]{2,1,0:T(8,128)(2,1)S(1)}, bf16[4,48,1536]{2,1,0:T(8,128)(2,1)}, u32[]{:S(2)}, u32[]{:S(2)}) collective-permute-start(bf16[4,48,1536]{2,1,0:T(8,128)(2,1)S(1)} %pad_maximum_fusion.7), channel_id=1, source_target_pairs={{0,1},{1,0},{2,3},{3,2},{4,5},{5,4},{6,7},{7,6},{8,9},{9,8},{10,11... | collective-permute-start | bytes 1769480 | tf_op jit(solution)/shard_map/ppermute | solution.py:72
  96.0 25.7 %collective-permute-start.28 = (bf16[8,48,1536]{2,1,0:T(8,128)(2,1)S(1)}, bf16[8,48,1536]{2,1,0:T(8,128)(2,1)S(1)}, u32[]{:S(2)}, u32[]{:S(2)}) collective-permute-start(bf16[8,48,1536]{2,1,0:T(8,128)(2,1)S(1)} %pad_maximum_fusion.2.refs_4_), channel_id=1, source_target_pairs={{0,2},{1,3},{2,0},{3,1},{4,6},{5,7},{6,4},{7,5},{8,10},{9,11},{10,... | collective-permute-start | bytes 3538952 | tf_op jit(solution)/shard_map/ppermute | solution.py:72
  122.7 26.1 %collective-permute-start.29 = (bf16[8,48,1536]{2,1,0:T(8,128)(2,1)}, bf16[8,48,1536]{2,1,0:T(8,128)(2,1)}, u32[]{:S(2)}, u32[]{:S(2)}) collective-permute-start(bf16[8,48,1536]{2,1,0:T(8,128)(2,1)} %get-tuple-element.321), channel_id=1, source_target_pairs={{0,2},{1,3},{2,0},{3,1},{4,6},{5,7},{6,4},{7,5},{8,10},{9,11},{10,... | collective-permute-start | bytes 3538952 | tf_op jit(solution)/shard_map/ppermute | solution.py:72
  123.6 25.2 %collective-permute-start.30 = (bf16[2,392,768]{2,1,0:T(8,128)(2,1)}, bf16[2,392,768]{2,1,0:T(8,128)(2,1)S(1)}, u32[]{:S(2)}, u32[]{:S(2)}) collective-permute-start(bf16[2,392,768]{2,1,0:T(8,128)(2,1)} %get-tuple-element.322), channel_id=1, source_target_pairs={{0,16},{1,17},{2,18},{3,19},{4,20},{5,21},{6,22},{7,23},{8,24},{9,... | collective-permute-start | bytes 3612680 | tf_op jit(solution)/shard_map/ppermute | solution.py:76
  124.2 24.6 %collective-permute-start.31 = (bf16[2,392,768]{2,1,0:T(8,128)(2,1)}, bf16[2,392,768]{2,1,0:T(8,128)(2,1)}, u32[]{:S(2)}, u32[]{:S(2)}) collective-permute-start(bf16[2,392,768]{2,1,0:T(8,128)(2,1)} %get-tuple-element.323), channel_id=1, source_target_pairs={{0,16},{1,17},{2,18},{3,19},{4,20},{5,21},{6,22},{7,23},{8,24},{9,... | collective-permute-start | bytes 3612680 | tf_op jit(solution)/shard_map/ppermute | solution.py:76
  149.4 18.5 %collective-permute-start.34 = (bf16[8,48,1536]{2,1,0:T(8,128)(2,1)}, bf16[8,48,1536]{2,1,0:T(8,128)(2,1)S(1)}, u32[]{:S(2)}, u32[]{:S(2)}) collective-permute-start(bf16[8,48,1536]{2,1,0:T(8,128)(2,1)} %get-tuple-element.336), channel_id=1, source_target_pairs={{0,2},{1,3},{2,0},{3,1},{4,6},{5,7},{6,4},{7,5},{8,10},{9,11},{10,... | collective-permute-start | bytes 3538952 | tf_op jit(solution)/shard_map/ppermute | solution.py:72
  161.0 10.3 %collective-permute-start.33 = (bf16[2,392,384]{2,1,0:T(8,128)(2,1)S(1)}, bf16[2,392,384]{2,1,0:T(8,128)(2,1)S(1)}, u32[]{:S(2)}, u32[]{:S(2)}) collective-permute-start(bf16[2,392,384]{2,1,0:T(8,128)(2,1)S(1)} %get-tuple-element.333), channel_id=1, source_target_pairs={{0,16},{1,17},{2,18},{3,19},{4,20},{5,21},{6,22},{7,23},{8,24},{9,... | collective-permute-start | bytes 1806344 | tf_op jit(solution)/shard_map/ppermute | solution.py:76
  161.4 9.9 %collective-permute-start.35 = (bf16[4,48,1536]{2,1,0:T(8,128)(2,1)S(1)}, bf16[4,48,1536]{2,1,0:T(8,128)(2,1)S(1)}, u32[]{:S(2)}, u32[]{:S(2)}) collective-permute-start(bf16[4,48,1536]{2,1,0:T(8,128)(2,1)S(1)} %add_convert_fusion.2), channel_id=1, source_target_pairs={{0,1},{1,0},{2,3},{3,2},{4,5},{5,4},{6,7},{7,6},{8,9},{9,8},{10,11... | collective-permute-start | bytes 1769480 | tf_op jit(solution)/shard_map/ppermute | solution.py:72
  173.1 9.2 %collective-permute-start.37 = (bf16[1,48,1536]{2,1,0:T(8,128)(2,1)S(1)}, bf16[1,48,1536]{2,1,0:T(8,128)(2,1)S(1)}, u32[]{:S(2)}, u32[]{:S(2)}) collective-permute-start(bf16[1,48,1536]{2,1,0:T(8,128)(2,1)S(1)} %get-tuple-element.350), channel_id=1, source_target_pairs={{0,4},{1,5},{2,6},{3,7},{4,0},{5,1},{6,2},{7,3},{8,12},{9,13},{10,... | collective-permute-start | bytes 442376 | tf_op jit(solution)/shard_map/ppermute | solution.py:72
  173.6 20.7 %collective-permute-start.41 = (bf16[2,392,768]{2,1,0:T(8,128)(2,1)}, bf16[2,392,768]{2,1,0:T(8,128)(2,1)S(1)}, u32[]{:S(2)}, u32[]{:S(2)}) collective-permute-start(bf16[2,392,768]{2,1,0:T(8,128)(2,1)} %get-tuple-element.354), channel_id=1, source_target_pairs={{0,16},{1,17},{2,18},{3,19},{4,20},{5,21},{6,22},{7,23},{8,24},{9,... | collective-permute-start | bytes 3612680 | tf_op jit(solution)/shard_map/ppermute | solution.py:76
  174.0 20.2 %collective-permute-start.38 = (bf16[1,48,1536]{2,1,0:T(8,128)(2,1)S(1)}, bf16[1,48,1536]{2,1,0:T(8,128)(2,1)S(1)}, u32[]{:S(2)}, u32[]{:S(2)}) collective-permute-start(bf16[1,48,1536]{2,1,0:T(8,128)(2,1)S(1)} %get-tuple-element.351), channel_id=1, source_target_pairs={{0,8},{1,9},{2,10},{3,11},{4,12},{5,13},{6,14},{7,15},{8,0},{9,1},... | collective-permute-start | bytes 442376 | tf_op jit(solution)/shard_map/ppermute | solution.py:72
  176.8 17.4 %collective-permute-start.39 = (bf16[1,48,1536]{2,1,0:T(8,128)(2,1)S(1)}, bf16[1,48,1536]{2,1,0:T(8,128)(2,1)}, u32[]{:S(2)}, u32[]{:S(2)}) collective-permute-start(bf16[1,48,1536]{2,1,0:T(8,128)(2,1)S(1)} %get-tuple-element.352), channel_id=1, source_target_pairs={{0,12},{1,13},{2,14},{3,15},{4,8},{5,9},{6,10},{7,11},{8,4},{9,5},... | collective-permute-start | bytes 442376 | tf_op jit(solution)/shard_map/ppermute | solution.py:72
  178.0 16.2 %collective-permute-start.36 = (bf16[4,48,1536]{2,1,0:T(8,128)(2,1)S(1)}, bf16[4,48,1536]{2,1,0:T(8,128)(2,1)}, u32[]{:S(2)}, u32[]{:S(2)}) collective-permute-start(bf16[4,48,1536]{2,1,0:T(8,128)(2,1)S(1)} %add_convert_fusion.1), channel_id=1, source_target_pairs={{0,1},{1,0},{2,3},{3,2},{4,5},{5,4},{6,7},{7,6},{8,9},{9,8},{10,11... | collective-permute-start | bytes 1769480 | tf_op jit(solution)/shard_map/ppermute | solution.py:72
  182.3 11.9 %collective-permute-start.40 = (bf16[16,48,384]{2,1,0:T(8,128)(2,1)S(1)}, bf16[16,48,384]{2,1,0:T(8,128)(2,1)S(1)}, u32[]{:S(2)}, u32[]{:S(2)}) collective-permute-start(bf16[16,48,384]{2,1,0:T(8,128)(2,1)S(1)} %get-tuple-element.353), channel_id=1, source_target_pairs={{0,16},{1,17},{2,18},{3,19},{4,20},{5,21},{6,22},{7,23},{8,24},{9,... | collective-permute-start | bytes 1769480 | tf_op jit(solution)/shard_map/ppermute | solution.py:76
  197.2 17.4 %collective-permute-start.42 = (bf16[1,48,1536]{2,1,0:T(8,128)(2,1)S(1)}, bf16[1,48,1536]{2,1,0:T(8,128)(2,1)S(1)}, u32[]{:S(2)}, u32[]{:S(2)}) collective-permute-start(bf16[1,48,1536]{2,1,0:T(8,128)(2,1)S(1)} %get-tuple-element.366), channel_id=1, source_target_pairs={{0,4},{1,5},{2,6},{3,7},{4,0},{5,1},{6,2},{7,3},{8,12},{9,13},{10,... | collective-permute-start | bytes 442376 | tf_op jit(solution)/shard_map/ppermute | solution.py:72
  197.3 17.3 %collective-permute-start.43 = (bf16[1,48,1536]{2,1,0:T(8,128)(2,1)S(1)}, bf16[1,48,1536]{2,1,0:T(8,128)(2,1)S(1)}, u32[]{:S(2)}, u32[]{:S(2)}) collective-permute-start(bf16[1,48,1536]{2,1,0:T(8,128)(2,1)S(1)} %get-tuple-element.367), channel_id=1, source_target_pairs={{0,8},{1,9},{2,10},{3,11},{4,12},{5,13},{6,14},{7,15},{8,0},{9,1},... | collective-permute-start | bytes 442376 | tf_op jit(solution)/shard_map/ppermute | solution.py:72
  199.5 15.1 %collective-permute-start.44 = (bf16[1,48,1536]{2,1,0:T(8,128)(2,1)S(1)}, bf16[1,48,1536]{2,1,0:T(8,128)(2,1)S(1)}, u32[]{:S(2)}, u32[]{:S(2)}) collective-permute-start(bf16[1,48,1536]{2,1,0:T(8,128)(2,1)S(1)} %get-tuple-element.368), channel_id=1, source_target_pairs={{0,12},{1,13},{2,14},{3,15},{4,8},{5,9},{6,10},{7,11},{8,4},{9,5},... | collective-permute-start | bytes 442376 | tf_op jit(solution)/shard_map/ppermute | solution.py:72
  201.7 13.0 %collective-permute-start.45 = (f32[48,1536]{1,0:T(8,128)S(1)}, f32[48,1536]{1,0:T(8,128)S(1)}, u32[]{:S(2)}, u32[]{:S(2)}) collective-permute-start(f32[48,1536]{1,0:T(8,128)S(1)} %add_bitcast_fusion.1.refs_0_), channel_id=1, source_target_pairs={{0,16},{1,17},{2,18},{3,19},{4,20},{5,21},{6,22},{7,23},{8,24},{9,... | collective-permute-start | bytes 884744 | tf_op jit(solution)/shard_map/ppermute | solution.py:76
  216.8 12.5 %collective-permute-start.47 = (f32[48,1536]{1,0:T(8,128)S(1)}, f32[48,1536]{1,0:T(8,128)S(1)}, u32[]{:S(2)}, u32[]{:S(2)}) collective-permute-start(f32[48,1536]{1,0:T(8,128)S(1)} %add_bitcast_fusion.refs_1_), channel_id=1, source_target_pairs={{0,16},{1,17},{2,18},{3,19},{4,20},{5,21},{6,22},{7,23},{8,24},{9,... | collective-permute-start | bytes 884744 | tf_op jit(solution)/shard_map/ppermute | solution.py:76
  217.3 13.4 %collective-permute-start.46 = (bf16[8,48,1152]{2,1,0:T(8,128)(2,1)}, bf16[8,48,1152]{2,1,0:T(8,128)(2,1)}, u32[]{:S(2)}, u32[]{:S(2)}) collective-permute-start(bf16[8,48,1152]{2,1,0:T(8,128)(2,1)} %pad_maximum_fusion.3), channel_id=1, source_target_pairs={{0,2},{1,3},{2,0},{3,1},{4,6},{5,7},{6,4},{7,5},{8,10},{9,11},{10,... | collective-permute-start | bytes 2654216 | tf_op jit(solution)/shard_map/ppermute | solution.py:72
  231.8 10.0 %collective-permute-start.48 = (bf16[8,48,384]{2,1,0:T(8,128)(2,1)S(1)}, bf16[8,48,384]{2,1,0:T(8,128)(2,1)S(1)}, u32[]{:S(2)}, u32[]{:S(2)}) collective-permute-start(bf16[8,48,384]{2,1,0:T(8,128)(2,1)S(1)} %get-tuple-element.388), channel_id=1, source_target_pairs={{0,2},{1,3},{2,0},{3,1},{4,6},{5,7},{6,4},{7,5},{8,10},{9,11},{10,... | collective-permute-start | bytes 884744 | tf_op jit(solution)/shard_map/ppermute | solution.py:72
  232.4 9.4 %collective-permute-start.49 = (bf16[4,48,1152]{2,1,0:T(8,128)(2,1)S(1)}, bf16[4,48,1152]{2,1,0:T(8,128)(2,1)S(1)}, u32[]{:S(2)}, u32[]{:S(2)}) collective-permute-start(bf16[4,48,1152]{2,1,0:T(8,128)(2,1)S(1)} %fusion), channel_id=1, source_target_pairs={{0,1},{1,0},{2,3},{3,2},{4,5},{5,4},{6,7},{7,6},{8,9},{9,8},{10,11... | collective-permute-start | bytes 1327112 | tf_op jit(solution)/shard_map/ppermute | solution.py:72
  242.9 7.3 %collective-permute-start.54 = (bf16[2,392,768]{2,1,0:T(8,128)(2,1)S(1)}, bf16[2,392,768]{2,1,0:T(8,128)(2,1)S(1)}, u32[]{:S(2)}, u32[]{:S(2)}) collective-permute-start(bf16[2,392,768]{2,1,0:T(8,128)(2,1)S(1)} %get-tuple-element.400), channel_id=1, source_target_pairs={{0,16},{1,17},{2,18},{3,19},{4,20},{5,21},{6,22},{7,23},{8,24},{9,... | collective-permute-start | bytes 3612680 | tf_op jit(solution)/shard_map/ppermute | solution.py:76
  244.7 13.5 %collective-permute-start.50 = (bf16[1,48,1152]{2,1,0:T(8,128)(2,1)S(1)}, bf16[1,48,1152]{2,1,0:T(8,128)(2,1)S(1)}, u32[]{:S(2)}, u32[]{:S(2)}) collective-permute-start(bf16[1,48,1152]{2,1,0:T(8,128)(2,1)S(1)} %get-tuple-element.394), channel_id=1, source_target_pairs={{0,4},{1,5},{2,6},{3,7},{4,0},{5,1},{6,2},{7,3},{8,12},{9,13},{10,... | collective-permute-start | bytes 331784 | tf_op jit(solution)/shard_map/ppermute | solution.py:72
  244.7 13.5 %collective-permute-start.51 = (bf16[1,48,1152]{2,1,0:T(8,128)(2,1)S(1)}, bf16[1,48,1152]{2,1,0:T(8,128)(2,1)S(1)}, u32[]{:S(2)}, u32[]{:S(2)}) collective-permute-start(bf16[1,48,1152]{2,1,0:T(8,128)(2,1)S(1)} %get-tuple-element.395), channel_id=1, source_target_pairs={{0,8},{1,9},{2,10},{3,11},{4,12},{5,13},{6,14},{7,15},{8,0},{9,1},... | collective-permute-start | bytes 331784 | tf_op jit(solution)/shard_map/ppermute | solution.py:72
  246.9 11.3 %collective-permute-start.52 = (bf16[1,48,1152]{2,1,0:T(8,128)(2,1)S(1)}, bf16[1,48,1152]{2,1,0:T(8,128)(2,1)S(1)}, u32[]{:S(2)}, u32[]{:S(2)}) collective-permute-start(bf16[1,48,1152]{2,1,0:T(8,128)(2,1)S(1)} %get-tuple-element.396), channel_id=1, source_target_pairs={{0,12},{1,13},{2,14},{3,15},{4,8},{5,9},{6,10},{7,11},{8,4},{9,5},... | collective-permute-start | bytes 331784 | tf_op jit(solution)/shard_map/ppermute | solution.py:72
  (104 other events, 945.7 us)

commit v2 on v1

--- a/solution.py
+++ b/solution.py
@@ -33,6 +33,31 @@
     return pltpu.CompilerParams(
         vmem_limit_bytes=max(mib, LEAST) * 1024 * 1024, dimension_semantics=("arbitrary",)
     )
+
+
+def call(kernel, token, in_specs, out_specs, out_shape, **rest):
+    many = isinstance(out_shape, (list, tuple))
+    shapes = list(out_shape) if many else [out_shape]
+    specs = list(out_specs) if many else [out_specs]
+    n_in = len(in_specs)
+
+    def body(token_ref, *refs):
+        kernel(*refs[:n_in], *refs[n_in + 1 :])
+
+    run = pl.pallas_call(
+        body,
+        in_specs=[ANY] + list(in_specs),
+        out_specs=[ANY] + specs,
+        out_shape=[jax.ShapeDtypeStruct(token.shape, token.dtype)] + shapes,
+        input_output_aliases={0: 0},
+        **rest,
+    )
+
+    def apply(*args):
+        token_out, *outs = run(token, *args)
+        return (token_out, *outs)
+
+    return apply
 
 
 def dot(a, b):
@@ -133,39 +158,49 @@
     return inv * (u - first - hat * second)
 
 
+def sine_terms(count):
+    x = 0.25 * np.cos(np.pi * (np.arange(400) + 0.5) / 800)
+    powers = x[:, None] ** (2 * np.arange(count)[None, :] + 1)
+    scale = powers.max(axis=0)
+    found = np.linalg.lstsq(powers / scale, np.sin(2 * np.pi * x), rcond=None)[0]
+    return [float(c) for c in found / scale]
+
+
+SINE = sine_terms(6)
+TO_WHOLE = 1.5 * 2.0**23
+
+
 def embed_kernel(each, n_groups):
     def kernel(table, *refs):
         toks, poss = refs[:n_groups], refs[n_groups : 2 * n_groups]
         embed = refs[-1]
         step = pl.program_id(0)
         p = choose(poss, step, each)
-        turns = p * table[0:1, :]
-        turns = turns - jnp.round(turns)
-        turns = turns + (p * table[1:2, :] + table[2:3, :])
-        turns = turns - jnp.round(turns)
-        fold = jnp.where(turns > 0.25, 0.5 - turns, jnp.where(turns < -0.25, -0.5 - turns, turns))
-        x = fold * (2.0 * math.pi)
+        turns = p * table[0:1, :] + table[2:3, :]
+        turns = turns - ((turns + TO_WHOLE) - TO_WHOLE) + p * table[1:2, :]
+        x = 0.25 - jnp.abs(turns)
         x2 = x * x
-        poly = -1.0 / 39916800.0
-        for coef in (1.0 / 362880.0, -1.0 / 5040.0, 1.0 / 120.0, -1.0 / 6.0, 1.0):
+        poly = SINE[-1]
+        for coef in SINE[-2::-1]:
             poly = poly * x2 + coef
         embed[0] = choose(toks, step, each).astype(F32) + x * poly
 
     return kernel
 
 
-def embed_rows(tokens, positions):
+def embed_rows(token, tokens, positions):
     each, length, width = tokens[0].shape
     exact = 10000.0 ** (-2.0 * (np.arange(width) // 2) / width) / (2.0 * math.pi)
     scale = 2.0 ** (11 - np.floor(np.log2(exact)))
     high = np.round(exact * scale) / scale
     table = np.zeros((8, width), np.float32)
-    table[0], table[1], table[2] = high, exact - high, 0.25 * (np.arange(width) % 2)
+    table[0], table[1], table[2] = high, exact - high, -0.25 * (np.arange(width) % 2 == 0)
     specs, clips = pair_specs(tokens, (length, width))
     pos_specs, _ = pair_specs(positions, (length, 1))
     size = clips * length * width
-    return pl.pallas_call(
+    return call(
         embed_kernel(each, len(tokens)),
+        token,
         grid=(clips,),
         in_specs=[whole((8, width))] + specs + pos_specs,
         out_specs=pl.BlockSpec((1, length, width), lambda i: (i, 0, 0)),
@@ -197,7 +232,7 @@
 
 
 def attend_forward(
-    sources, small, order, core, counts, pieces, rows, each, first, heads, apart, block
+    token, sources, small, order, core, counts, pieces, rows, each, first, heads, apart, block
 ):
     length, width = sources[0].shape[1:]
     source_each, n_sources = sources[0].shape[0], len(sources)
@@ -309,8 +344,9 @@
         out_specs.append(other)
         out_shapes.append(jax.ShapeDtypeStruct((clips - each, length, part), BF))
     n_rows = clips * length
-    return pl.pallas_call(
+    return call(
         kernel,
+        token,
         grid=(clips,),
         in_specs=[SMEM, SMEM, SMEM]
         + source_specs
@@ -335,10 +371,11 @@
         return assemble(own, lambda n: meta[1 + n], rows, weight.at[0], sems, 0, cut)
     core = meta[0]
     copies = assemble(own, lambda n: meta[1 + n], rows, weight.at[core], sems, 0, cut)
-    return copies + assemble(other, lambda n: meta[17 + n], rows, weight.at[1 - core], sems, 16)
-
-
-def project_norm(mixes, places, embed, small, meta, pieces, others, rows):
+    far = weight.at[1 - core]
+    return copies + assemble(other, lambda n: meta[17 + n], rows, far, sems, 16, cut)
+
+
+def project_norm(token, mixes, places, embed, small, meta, pieces, others, rows):
     n, length, width = mixes[0].shape[0], embed.shape[1], embed.shape[2]
     parts = [mix.shape[2] for mix in mixes]
     n_mix, n_p, n_o = len(mixes), len(pieces), len(others)
@@ -374,8 +411,9 @@
     clip = pl.BlockSpec((1, length, width), lambda i: (i, 0, 0))
     mix_specs = [pl.BlockSpec((1, length, c), lambda i: (i, 0, 0)) for c in parts]
     size = n * length * width
-    return pl.pallas_call(
+    return call(
         kernel,
+        token,
         grid=(n,),
         in_specs=[SMEM, whole((16, width)), clip] + mix_specs + [ANY] * (n_p + n_o),
         out_specs=[clip, clip],
@@ -393,26 +431,28 @@
     )(meta, small, embed, *mixes, *pieces, *others)
 
 
-def mlp_both(groups, cots, order, counts, bias, pieces, rows, relative):
+def mlp_both(
+    token, groups, cots, order, counts, bias, bias_row, pieces, rows, relative
+):
     each, length, width = groups[0].shape
     hidden = bias.shape[1]
     n_groups, n_pieces = len(groups), len(pieces)
     n_blocks = sum(piece.shape[0] for piece in pieces)
     hidden_rows = hidden // n_blocks
     specs, clips = pair_specs(groups, (length, width))
+    n_places = width // rows
+    half = n_places // 2
     if relative:
-        half = n_blocks // 2
-        grad_shapes = [
-            jax.ShapeDtypeStruct((half, rows, 2 * width), F32),
-            jax.ShapeDtypeStruct((half, rows, 2 * width), BF),
-        ]
+        grad_shapes = [jax.ShapeDtypeStruct((half, rows, 2 * width), BF)]
+        grad_shapes += [jax.ShapeDtypeStruct((half // 2, rows, 2 * width), BF)] * 2
     else:
         grad_shapes = [
             jax.ShapeDtypeStruct((1, width, hidden), F32),
             jax.ShapeDtypeStruct((1, hidden, width), F32),
         ]
     own_shape = (each, length, width)
-    out_shapes = [jax.ShapeDtypeStruct(own_shape, F32)] * 2
+    own_type = BF if n_groups > 1 else F32
+    out_shapes = [jax.ShapeDtypeStruct(own_shape, own_type)] * 2
     if n_groups > 1:
         out_shapes += [jax.ShapeDtypeStruct(own_shape, BF)] * 2
     out_shapes += [jax.ShapeDtypeStruct((1, hidden), F32)]
@@ -426,30 +466,34 @@
         sent = outs[2:4] if n_groups > 1 else None
         n_out = 4 if n_groups > 1 else 2
         bias_grad = outs[n_out]
-        grad_a, grad_b = outs[n_out + 1 : n_out + 3]
-        (up, down, g_up, g_down, low_up, low_down, sems) = outs[n_out + 3 :]
+        grads = outs[n_out + 1 : -7]
+        (up, down, g_up, g_down, low_up, low_down, sems) = outs[-7:]
         i = pl.program_id(0)
         place = lambda n: order_ref[n]
 
+        def weights_in():
+            if not relative:
+                return [
+                    [pltpu.make_async_copy(piece_refs[0].at[0], up, sems.at[0])],
+                    [pltpu.make_async_copy(piece_refs[1].at[0], down, sems.at[1])],
+                ]
+            cut = slice(hidden, None)
+            return [
+                assemble(piece_refs, place, rows, up, sems, 0, slice(0, hidden)),
+                assemble(piece_refs, place, hidden_rows, down, sems, n_blocks, cut),
+            ]
+
         @pl.when(i == 0)
         def _():
-            copies = assemble(piece_refs, place, rows, up, sems, 0, slice(0, hidden))
-            if relative:
-                copies += assemble(
-                    piece_refs, place, hidden_rows, down, sems, n_blocks, slice(hidden, None)
-                )
-            else:
-                copies = [
-                    pltpu.make_async_copy(piece_refs[0].at[0], up, sems.at[0]),
-                    pltpu.make_async_copy(piece_refs[1].at[0], down, sems.at[1]),
-                ]
-            run_all(copies)
+            first, second = weights_in()
+            run_all(first + second)
 
         x = choose(ins, i, each)
         valid = lax.broadcasted_iota(jnp.int32, (length, 1), 0) < count_ref[i]
         cot = choose(cot_refs, i, each)
         dd = jnp.where(valid, cot, jnp.zeros_like(cot))
-        pre = dot(x, up[...]) + bias_ref[...]
+        at_row = bias_row + 2 * order_ref[16] if relative else bias_row
+        pre = dot(x, up[...]) + bias_ref[pl.ds(at_row, 1), :]
         cdf = 0.5 + 0.5 * lax.erf(pre * 0.7071067811865476)
         pdf = jnp.exp(pre * pre * -0.5) * 0.3989422804014327
         act = (pre * cdf).astype(BF)
@@ -462,8 +506,8 @@
 
         @pl.when(i < each)
         def _():
-            own_out[0] = out
-            own_dm[0] = dm
+            own_out[0] = out.astype(own_type)
+            own_dm[0] = dm.astype(own_type)
 
         if sent is not None:
 
@@ -487,20 +531,14 @@
         @pl.when(i == clips - 1)
         def _():
             bias_grad[...] += bias_part
+            one, two = slice(0, width), slice(width, 2 * width)
             if relative:
-                total_up = g_up[...] + up_part
-                g_up[...] = total_up
-                low_up[...] = total_up.astype(BF)
-                one, two = slice(0, width), slice(width, 2 * width)
-                copies = deliver(g_up, place, rows, 0, [grad_a], sems, 0, one)
-                copies += deliver(low_up, place, rows, half, [grad_b], sems, half, one)
+                low_up[...] = (g_up[...] + up_part).astype(BF)
+                copies = deliver(low_up, place, rows, 0, grads, sems, 0, one)
                 for copy in copies:
                     copy.start()
-                total_down = g_down[...] + down_part
-                g_down[...] = total_down
-                low_down[...] = total_down.astype(BF)
-                more = deliver(g_down, place, rows, 0, [grad_a], sems, 2 * half, two)
-                more += deliver(low_down, place, rows, half, [grad_b], sems, 3 * half, two)
+                low_down[...] = (g_down[...] + down_part).astype(BF)
+                more = deliver(low_down, place, rows, 0, grads, sems, 2 * half, two)
                 for copy in more:
                     copy.start()
                 for copy in copies + more:
@@ -509,8 +547,8 @@
                 g_up[...] += up_part
                 g_down[...] += down_part
                 copies = [
-                    pltpu.make_async_copy(g_up, grad_a.at[0], sems.at[0]),
-                    pltpu.make_async_copy(g_down, grad_b.at[0], sems.at[1]),
+                    pltpu.make_async_copy(g_up, grads[0].at[0], sems.at[0]),
+                    pltpu.make_async_copy(g_down, grads[1].at[0], sems.at[1]),
                 ]
                 run_all(copies)
 
@@ -519,14 +557,15 @@
     out_specs = [pl.BlockSpec((1, length, width), own_index)] * 2
     if n_groups > 1:
         out_specs += [pl.BlockSpec((1, length, width), sent_index)] * 2
-    out_specs += [whole((1, hidden)), ANY, ANY]
+    out_specs += [whole((1, hidden))] + [ANY] * len(grad_shapes)
     low_shape = (width, hidden) if relative else (16, 128)
     low_shape_down = (hidden, width) if relative else (16, 128)
     n_rows = clips * length
-    return pl.pallas_call(
+    return call(
         kernel,
+        token,
         grid=(clips,),
-        in_specs=[SMEM, SMEM, whole((1, hidden))] + specs + specs + [ANY] * n_pieces,
+        in_specs=[SMEM, SMEM, whole(bias.shape)] + specs + specs + [ANY] * n_pieces,
         out_specs=out_specs,
         out_shape=out_shapes + grad_shapes,
         scratch_shapes=[
@@ -536,7 +575,7 @@
             pltpu.VMEM((hidden, width), F32),
             pltpu.VMEM(low_shape, BF),
             pltpu.VMEM(low_shape_down, BF),
-            pltpu.SemaphoreType.DMA((max(2 * n_blocks, 2),)),
+            pltpu.SemaphoreType.DMA((max(2 * n_blocks, 2 * n_places, 2),)),
         ],
         compiler_params=params(56),
         cost_estimate=lasting(23),
@@ -544,7 +583,7 @@
     )(order, counts, bias, *groups, *cots, *pieces)
 
 
-def norm_two_back(dms, resid, cot, small, meta, counts, pieces, others, rows, part):
+def norm_two_back(token, dms, resid, cot, small, meta, counts, pieces, others, rows, part):
     n, length, width = resid.shape
     n_dm, n_p, n_o = len(dms), len(pieces), len(others)
     halves = 2 if others else 1
@@ -597,8 +636,9 @@
     mix_spec = pl.BlockSpec((1, length, part), lambda i: (i, 0, 0))
     shape = resid.shape
     mix_shape = jax.ShapeDtypeStruct((n, length, part), BF)
-    return pl.pallas_call(
+    return call(
         kernel,
+        token,
         grid=(n,),
         in_specs=[SMEM, SMEM, whole((16, width)), clip, clip]
         + [clip] * n_dm
@@ -620,7 +660,7 @@
     )(meta, counts, small, resid, cot, *dms, *pieces, *others)
 
 
-def out_weight_grad(mixes, places, proj, meta, rows):
+def out_weight_grad(token, mixes, places, proj, meta, rows):
     n, length, width = proj.shape
     parts = [mix.shape[2] for mix in mixes]
     n_mix = len(mixes)
@@ -653,11 +693,10 @@
         def _():
             if halves > 1:
                 core = meta_ref[0]
-                low[...] = total[1 - core].astype(BF)
-                copies = deliver(
-                    total.at[core], lambda n: meta_ref[1 + n], rows, 0, [keep], sems, 0
-                )
-                copies += deliver(low, lambda n: meta_ref[17 + n], rows, 0, [send], sems, blocks)
+                low[...] = total[...].astype(BF)
+                here, there = low.at[core], low.at[1 - core]
+                copies = deliver(here, lambda n: meta_ref[1 + n], rows, 0, [keep], sems, 0)
+                copies += deliver(there, lambda n: meta_ref[17 + n], rows, 0, [send], sems, blocks)
                 run_all(copies)
             else:
                 run_all([pltpu.make_async_copy(total, keep, sems.at[0])])
@@ -665,19 +704,20 @@
     clip = lambda c: pl.BlockSpec((1, length, c), lambda i: (i, 0, 0))
     if halves > 1:
         shapes = [
-            jax.ShapeDtypeStruct((blocks, rows, half_width), F32),
+            jax.ShapeDtypeStruct((blocks, rows, half_width), BF),
             jax.ShapeDtypeStruct((blocks, rows, half_width), BF),
         ]
         scratch = [
             pltpu.VMEM((halves, width, half_width), F32),
-            pltpu.VMEM((width, half_width), BF),
+            pltpu.VMEM((halves, width, half_width), BF),
             pltpu.SemaphoreType.DMA((2 * blocks,)),
         ]
     else:
         shapes = [jax.ShapeDtypeStruct((1, width, width), F32)]
         scratch = [pltpu.VMEM((1, width, width), F32), pltpu.SemaphoreType.DMA((1,))]
-    return pl.pallas_call(
+    return call(
         kernel,
+        token,
         grid=(n,),
         in_specs=[SMEM, clip(width)] + [clip(c) for c in parts],
         out_specs=[ANY] * len(shapes),
@@ -689,7 +729,7 @@
     )(meta, proj, *mixes)
 
 
-def attend_back(groups, qkv, logs, d_mixes, order, counts, rows, relative, first, at_pair, pairs):
+def attend_back(token, groups, qkv, logs, d_mixes, order, counts, rows, relative, first, at_pair, pairs):
     each, length, width = groups[0].shape
     clips = qkv.shape[0]
     columns, part = 384 * pairs, 128 * pairs
@@ -761,9 +801,7 @@
             place = lambda n: order_ref[n]
             if relative:
                 low[...] = total[...].astype(BF)
-                copies = deliver(total, place, rows, 0, [keep], sems, 0)
-                copies += deliver(low, place, rows, half_blocks, [send], sems, half_blocks)
-                run_all(copies)
+                run_all(deliver(low, place, rows, 0, [keep, send], sems))
             else:
                 run_all([pltpu.make_async_copy(total, keep.at[0], sems.at[0])])
 
@@ -772,7 +810,7 @@
     qkv_spec = pl.BlockSpec((1, length, columns), lambda i: (i, 0, block_at))
     if relative:
         shapes = [
-            jax.ShapeDtypeStruct((half_blocks, rows, columns), F32),
+            jax.ShapeDtypeStruct((half_blocks, rows, columns), BF),
             jax.ShapeDtypeStruct((half_blocks, rows, columns), BF),
         ]
         scratch = [pltpu.VMEM((width, columns), F32), pltpu.VMEM((width, columns), BF)]
@@ -780,8 +818,9 @@
         shapes = [jax.ShapeDtypeStruct((1, width, columns), F32)]
         scratch = [pltpu.VMEM((width, columns), F32)]
     n_rows = clips * length
-    return pl.pallas_call(
+    return call(
         kernel,
+        token,
         grid=(clips,),
         in_specs=[
             SMEM,
@@ -804,7 +843,7 @@
     )(order, counts, qkv, logs, *groups, *d_mixes)
 
 
-def attn_in_grad(d_qkvs, order, pieces, rows, each, width):
+def attn_in_grad(token, d_qkvs, order, pieces, rows, each, width):
     clips, length, _ = d_qkvs[0].shape
     sizes = [d.shape[2] for d in d_qkvs]
     total = sum(sizes)
@@ -852,8 +891,9 @@
     shapes = [jax.ShapeDtypeStruct((each, length, width), F32)]
     if split:
         shapes.append(jax.ShapeDtypeStruct((each, length, width), BF))
-    return pl.pallas_call(
+    return call(
         kernel,
+        token,
         grid=(clips,),
         in_specs=[SMEM]
         + [pl.BlockSpec((1, length, c), lambda i: (i, 0, 0)) for c in sizes]
@@ -867,7 +907,7 @@
     )(order, *d_qkvs, *flat)
 
 
-def norm_one_back(das, embed, d_resid, small):
+def norm_one_back(token, das, embed, d_resid, small):
     n, length, width = d_resid.shape
     n_da = len(das)
 
@@ -892,8 +932,9 @@
             sums[...] += parts
 
     clip = pl.BlockSpec((1, length, width), lambda i: (i, 0, 0))
-    return pl.pallas_call(
+    return call(
         kernel,
+        token,
         grid=(n,),
         in_specs=[whole((16, width)), clip, clip] + [clip] * n_da,
         out_specs=[clip, whole((8, width))],
@@ -916,13 +957,13 @@
     return (weight_new, moment_new, average_new)
 
 
-def update_all(state, sums, place, halves_q, halves_r, g_up, g_down, cuts):
+def update_all(token, state, sums, place, halves, g_up, g_down, cuts):
     rows, width = state[1].shape
     part = width // 2
     pairs = part // 128
     n_sq = 9
 
-    def kernel(place_ref, sums_ref, q_own, q_other, r_own, r_other, up_ref, down_ref, *refs):
+    def kernel(place_ref, sums_ref, own_ref, other_ref, up_ref, down_ref, *refs):
         ins, outs = refs[:15], refs[15:30]
         norms_ref = refs[30]
         core, chip = place_ref[0], place_ref[1]
@@ -945,16 +986,11 @@
             pick = lambda own, other: jnp.where(first if c == 0 else ~first, own, other)
             for pair in range(pairs):
                 for t in range(3):
-                    if pair < 2:
-                        cut = slice(384 * pair + 128 * t, 384 * pair + 128 * t + 128)
-                        grad = pick(q_own[:, cut], q_other[:, cut])
-                    else:
-                        cut = slice(128 * t, 128 * t + 128)
-                        grad = pick(r_own[:, cut], r_other[:, cut])
+                    cut = slice(384 * pair + 128 * t, 384 * pair + 128 * t + 128)
                     at = t * width + c * part + 128 * pair
-                    write(0, slice(at, at + 128), grad)
-            cut = slice(768, 768 + part)
-            write(1, slice(c * part, c * part + part), pick(q_own[:, cut], q_other[:, cut]))
+                    write(0, slice(at, at + 128), pick(own_ref[:, cut], other_ref[:, cut]))
+            cut = slice(384 * pairs, 384 * pairs + part)
+            write(1, slice(c * part, c * part + part), pick(own_ref[:, cut], other_ref[:, cut]))
         write(2, slice(None), up_ref[...])
         write(3, slice(None), down_ref[...])
 
@@ -984,11 +1020,12 @@
 
     tall = lambda x: pl.BlockSpec((x.shape[0] // cuts, x.shape[1]), lambda i: (i, 0))
     state_specs = [whole(x.shape) if k % 5 == 4 else tall(x) for k, x in enumerate(state)]
-    return pl.pallas_call(
+    return call(
         kernel,
+        token,
         grid=(cuts,),
         in_specs=[SMEM, whole(sums.shape)]
-        + [tall(x) for x in (*halves_q, *halves_r, g_up, g_down)]
+        + [tall(x) for x in (*halves, g_up, g_down)]
         + state_specs,
         out_specs=state_specs + [whole((1, 128))],
         out_shape=[jax.ShapeDtypeStruct(x.shape, F32) for x in state]
@@ -996,10 +1033,10 @@
         compiler_params=params(48),
         cost_estimate=lasting(6),
         name="update_all",
-    )(place, sums, *halves_q, *halves_r, g_up, g_down, *state)
-
-
-def weight_squares(state):
+    )(place, sums, *halves, g_up, g_down, *state)
+
+
+def weight_squares(token, state):
     def kernel(*refs):
         lane = lax.broadcasted_iota(jnp.int32, (1, 128), 1)
         row = jnp.zeros((1, 128), F32)
@@ -1007,8 +1044,9 @@
             row = jnp.where(lane == k, 0.5 * jnp.sum(ref[...] * ref[...]), row)
         refs[-1][...] = row
 
-    return pl.pallas_call(
+    return call(
         kernel,
+        token,
         grid=(1,),
         in_specs=[whole(x.shape) for x in state],
         out_specs=whole((1, 128)),
@@ -1019,14 +1057,15 @@
     )(*state)
 
 
-def interleave(own, other, place):
-    rows, double = own[0].shape
-    width = double // 2
+def interleave(token, own, other, place):
+    rows, total = own.shape
+    width = total // 4
     run = rows
 
-    def kernel(place_ref, *refs):
-        own_refs, other_refs = refs[:2], refs[2:4]
-        up, down, squares = refs[4:]
+    def kernel(place_ref, own_ref, other_ref, up, down, squares):
+        both = [slice(2 * width * h, 2 * width * (h + 1)) for h in range(2)]
+        own_refs = [own_ref[:, cut] for cut in both]
+        other_refs = [other_ref[:, cut] for cut in both]
         first = place_ref[0] == 0
         lane = lax.broadcasted_iota(jnp.int32, (1, 128), 1)
         total_up = sum(jnp.sum(r[:, :width] * r[:, :width]) for r in own_refs)
@@ -1036,7 +1075,7 @@
         for c in range(2):
             for h in range(2):
                 ahead = first if c == 0 else ~first
-                cell = jnp.where(ahead, own_refs[h][...], other_refs[h][...])
+                cell = jnp.where(ahead, own_refs[h], other_refs[h])
                 cells.append(cell[:, :width])
                 at = (2 * c + h) * rows
                 down[at : at + rows, :] = cell[:, width:]
@@ -1055,10 +1094,11 @@
                     value = jnp.where(lane >= place_at, moved, value)
             up[:, low : low + 128] = value
 
-    return pl.pallas_call(
+    return call(
         kernel,
+        token,
         grid=(1,),
-        in_specs=[SMEM] + [whole(own[0].shape)] * 4,
+        in_specs=[SMEM] + [whole(own.shape)] * 2,
         out_specs=[whole((rows, 4 * width)), whole((4 * rows, width)), whole((1, 128))],
         out_shape=[
             jax.ShapeDtypeStruct((rows, 4 * width), F32),
@@ -1068,10 +1108,10 @@
         compiler_params=params(32),
         cost_estimate=lasting(3),
         name="interleave",
-    )(place, *own, *other)
-
-
-def gather_sums(place, sums_one, sums_two, bias_grads, bias_ups, squares_mlp, squares_w):
+    )(place, own, other)
+
+
+def gather_sums(token, place, sums_one, sums_two, bias_grads, bias_ups, squares_mlp, squares_w):
     width = sums_one.shape[1]
     part = width // 2
 
@@ -1087,10 +1127,12 @@
 
             @pl.when(core == c)
             def _():
-                for pair, ref in enumerate(grads):
-                    at = c * part + 128 * pair
-                    out[4:5, at : at + 128] = ref[:, 0:128]
-                    out[5:6, at : at + 128] = ref[:, 256:384]
+                at = c * part
+                for ref in grads:
+                    for cut in range(0, ref.shape[1], 384):
+                        out[4:5, at : at + 128] = ref[:, cut : cut + 128]
+                        out[5:6, at : at + 128] = ref[:, cut + 256 : cut + 384]
+                        at += 128
                 for h in range(2):
                     out[8 + 2 * c + h : 9 + 2 * c + h, :] = ups[h][...]
 
@@ -1100,8 +1142,9 @@
         out[12:13, :128] = jnp.where((lane >= 4) & (lane < 9), moved, row)
 
     ins = [sums_one, sums_two, *bias_grads, *bias_ups, squares_mlp, squares_w]
-    return pl.pallas_call(
+    return call(
         kernel,
+        token,
         grid=(1,),
         in_specs=[SMEM] + [whole(x.shape) for x in ins],
         out_specs=whole((16, width)),
@@ -1112,38 +1155,49 @@
     )(place, *ins)
 
 
-def last_shards(sums, keep_r, recv_r, shard_q):
-    _, rows, columns = keep_r.shape
-    wide = shard_q.shape[1]
-
-    def kernel(sums_ref, keep, *refs):
-        recvs, q, shard, out = refs[:-3], refs[-3], refs[-2], refs[-1]
-        total = keep[0]
-        for ref in recvs:
-            total = total + ref[0].astype(F32)
-        shard[...] = total
+def last_shards(token, sums, wide, narrow, recv_z):
+    rows, columns = wide[0].shape[1:]
+    more = narrow[0].shape[2]
+    inner = 2 * more
+
+    def kernel(sums_ref, *refs):
+        wides, narrows, last = refs[:3], refs[3:6], refs[6:9]
+        shard, out = refs[9:]
+        total = sum(ref[0].astype(F32) for ref in wides)
+        extra = sum(ref[0].astype(F32) for ref in narrows)
+        for ref in last:
+            came = ref[0].astype(F32)
+            total = total + came[:, :columns]
+            extra = extra + came[:, columns:]
+        heads, outer = total[:, :inner], total[:, inner:]
+        shard[:, :inner] = heads
+        shard[:, inner : inner + more] = extra
+        shard[:, inner + more :] = outer
         out[...] = sums_ref[...]
-        inner, outer = q[:, :768], q[:, 768:]
-        square = jnp.sum(total * total) + jnp.sum(inner * inner)
+        square = jnp.sum(heads * heads) + jnp.sum(extra * extra)
         lane = lax.broadcasted_iota(jnp.int32, (1, 128), 1)
         old = sums_ref[12:13, :128]
         new = jnp.where(lane == 0, square, jnp.where(lane == 1, jnp.sum(outer * outer), old))
         out[12:13, :128] = new
 
-    block = pl.BlockSpec((1, rows, columns), lambda i: (0, 0, 0))
-    return pl.pallas_call(
+    block = lambda c: pl.BlockSpec((1, rows, c), lambda i: (0, 0, 0))
+    return call(
         kernel,
+        token,
         grid=(1,),
-        in_specs=[whole(sums.shape), block] + [block] * len(recv_r) + [whole((rows, wide))],
-        out_specs=[whole((rows, columns)), whole(sums.shape)],
+        in_specs=[whole(sums.shape)]
+        + [block(columns)] * 3
+        + [block(more)] * 3
+        + [block(columns + more)] * 3,
+        out_specs=[whole((rows, columns + more)), whole(sums.shape)],
         out_shape=[
-            jax.ShapeDtypeStruct((rows, columns), F32),
+            jax.ShapeDtypeStruct((rows, columns + more), F32),
             jax.ShapeDtypeStruct(sums.shape, F32),
         ],
         compiler_params=params(16),
         cost_estimate=lasting(2),
         name="last_shards",
-    )(sums, keep_r, *recv_r, shard_q)
+    )(sums, *wide, *narrow, *recv_z)
 
 
 def finish(masters, moments, averages, grads, totals):
@@ -1176,211 +1230,223 @@
     core = lax.axis_index("dp")
     chip = lax.axis_index("fsdp")
     table = jnp.asarray(links.masks())
+    core_id = core[None].astype(jnp.int32)
     mine = lax.dynamic_index_in_dim(table, core, 0, False) ^ chip
     partner = lax.dynamic_index_in_dim(table, 1 - core, 0, False) ^ chip
-    core_id = core[None].astype(jnp.int32)
     meta = jnp.concatenate([core_id, mine, partner])
+    mine = jnp.concatenate([mine, core_id])
     place = jnp.concatenate([core_id, chip[None].astype(jnp.int32)])
     part = width // 2
     pairs = part // 128
     cross, flip, along_z = links.cross, links.flip, links.along_z
     half_core = lambda x, axis: lax.dynamic_index_in_dim(x, core, axis, False)
     join = lambda *blocks: jnp.concatenate(blocks, axis=0)
+    beside = lambda *blocks: jnp.concatenate(blocks, axis=2)
 
     def onward(first, last, keep, *recvs):
-        total = keep[first:last]
+        total = keep[first:last].astype(F32)
         for recv in recvs:
             total = total + recv[first:last].astype(F32)
         return total
 
     cut = half_core(w_qkv.reshape(rows, 3, 2, pairs, 128), 2).astype(BF)
     cut = jnp.swapaxes(cut, 1, 2).reshape(rows, pairs * 384)
+    out_cut = half_core(w_out.reshape(rows, 2, part), 1).astype(BF)
     small_cut = jnp.concatenate([w_small[:8], w_small[8:].T.reshape(4, rows)], axis=0)
     small_cut = jnp.pad(small_cut.astype(BF).T, ((0, 0), (0, 116)))
-    pack_one = jnp.concatenate([cut[:, :768], small_cut], axis=1)[None]
-    pack_one, cut, positions, counts, tokens, w_out, w_up, w_down = tie(
-        pack_one, cut, positions, counts, tokens, w_out, w_up, w_down
-    )
-    one_z = along_z([pack_one] * 3)
+    pack_q = jnp.concatenate([cut[:, :768], small_cut, cut[:, 768:], out_cut], axis=1)[None]
+    token = jnp.zeros((8, 128), F32)
+    token, pack_q, w_up, w_down, tokens, positions, counts = tie(
+        token, pack_q, w_up, w_down, tokens, positions, counts
+    )
+    q_z = along_z([pack_q] * 3)
     token_other = cross(tokens)
     place_other = cross(jnp.concatenate([positions, counts[:, None]], axis=1))
-    out_cut = half_core(w_out.reshape(rows, 2, part), 1).astype(BF)
-    pack_two = jnp.concatenate([cut[:, 768:], out_cut], axis=1)[None]
+    column = lambda x: x.astype(F32)[..., None]
+    token, embed = embed_rows(token, [tokens], [column(positions)])
     up_cut = half_core(w_up.reshape(rows, 16, 2, 2, rows), 2).astype(BF)
     down_cut = half_core(w_down.reshape(2, 2, rows, width), 0).astype(BF)
-    pack_a, pack_b = [
-        jnp.concatenate([up_cut[:, :, h].reshape(rows, 16 * rows), down_cut[h]], axis=1)[None]
-        for h in range(2)
-    ]
-    *one_z, pack_two, pack_a, pack_b = tie(*one_z, pack_two, pack_a, pack_b)
-    one_4 = join(pack_one, *one_z)
-
-    column = lambda x: x.astype(F32)[..., None]
-    one_4, pack_two, tokens = tie(one_4, pack_two, tokens)
-    one_b = flip(one_4, 4)
-    two_z = along_z([pack_two] * 3)
-    embed = embed_rows([tokens], [column(positions)])
-    one_b, *two_z, embed = tie(one_b, *two_z, embed)
-    one_8, two_4 = join(one_4, one_b), join(pack_two, *two_z)
-
-    one_8, two_4, pack_a, token_other, cotangent = tie(
-        one_8, two_4, pack_a, token_other, cotangent
-    )
+    ups = [up_cut[:, :, h].reshape(1, rows, 16 * rows) for h in range(2)]
+    downs = [down_cut[h][None] for h in range(2)]
+    pack_b = beside(ups[1], downs[1])
+    token, ups[0], downs[0], pack_b, token_other, place_other, *q_z = tie(
+        token, ups[0], downs[0], pack_b, token_other, place_other, *q_z
+    )
+    q_4 = join(pack_q, *q_z)
+
+    token, q_4, up_a, token_other, place_other = tie(
+        token, q_4, ups[0], token_other, place_other
+    )
+    q_b = flip(q_4, 4)
+    a_zu = along_z([up_a] * 3)
+    token, embed_other = embed_rows(
+        token, [token_other], [column(place_other[:, :length])]
+    )
+    counts_all = jnp.concatenate([counts, place_other[:, length]])
+    token, q_b, cotangent, *a_zu = tie(token, q_b, cotangent, *a_zu)
+    one_8 = join(q_4[:, :, :896], q_b[:, :, :896])
+    two_8 = join(q_4[:, :, 896:], q_b[:, :, 896:])
+
+    token, one_8, two_8, down_a, cotangent = tie(token, one_8, two_8, downs[0], cotangent)
     one_c = flip(one_8, 8)
-    two_b = flip(two_4, 4)
-    a_z = along_z([pack_a] * 3)
+    a_zd = along_z([down_a] * 3)
     cot_other = cross(cotangent)
-    embed_other = embed_rows([token_other], [column(place_other[:, :length])])
-    squares_w = weight_squares(state[:5])
-    one_c, two_b, embed_other, squares_w = tie(one_c, two_b, embed_other, squares_w)
-    counts_all = jnp.concatenate([counts, place_other[:, length]])
-    two_8 = join(two_4, two_b)
-
-    embed_other, two_8, pack_b = tie(embed_other, two_8, pack_b)
-    qkv_one, embeds = [one_8, one_c], [embed, embed_other]
+    token, squares_w = weight_squares(token, state[:5])
+    token, one_c, cot_other, squares_w, *a_zd = tie(token, one_c, cot_other, squares_w, *a_zd)
+    a_4 = beside(join(up_a, *a_zu), join(down_a, *a_zd))
+
+    embeds = [embed, embed_other]
+    token, a_4, two_8, pack_b = tie(token, a_4, two_8, pack_b)
     two_c = flip(two_8, 8)
+    a_b = flip(a_4, 4)
     b_z = along_z([pack_b] * 3)
-    forward = lambda source, small, pieces, pair, at: attend_forward(
-        source, small, mine, core_id, counts_all, pieces, rows, each, 2 * pair, 2, 6, at
-    )
-    small, attn_in, qkv_0, logs_0, mix_own_0, mix_send_0 = forward(embeds, None, qkv_one, 0, 0)
-    two_c, mix_send_0, *a_z, attn_in = tie(two_c, mix_send_0, *a_z, attn_in)
-    a_4 = join(pack_a, *a_z)
-    qkv_two = [two_8, two_c]
-    two_8o, two_co = two_8[:, :, part:], two_c[:, :, part:]
-
-    a_4, attn_in_1, mix_send_0, two_8o, two_co = tie(a_4, attn_in, mix_send_0, two_8o, two_co)
-    a_b = flip(a_4, 4)
-    mix_recv_0 = cross(mix_send_0)
-    out_c, out_d = cross(two_8o), cross(two_co)
-    qkv_1, logs_1, mix_own_1, mix_send_1 = forward([attn_in_1], small, qkv_one, 1, 1)
-    a_b, mix_send_1, *b_z = tie(a_b, mix_send_1, *b_z)
-    a_8, b_4 = join(a_4, a_b), join(pack_b, *b_z)
-
-    a_8, b_4, mix_send_1, attn_in_2 = tie(a_8, b_4, mix_send_1, attn_in)
-    a_c = flip(a_8, 8)
+    token, small, attn_in, qkv_1, logs_1, mix_own_1, mix_send_1 = attend_forward(
+        token, embeds, None, mine, core_id, counts_all, [one_8, one_c], rows, each, 0, 4, 6, 0
+    )
+    token, a_4, a_b, two_c, small, attn_in, qkv_1, logs_1, mix_own_1, mix_send_1, *b_z = tie(
+        token, a_4, a_b, two_c, small, attn_in, qkv_1, logs_1, mix_own_1, mix_send_1, *b_z
+    )
+    a_c1 = flip(a_4, 8)
     mix_recv_1 = cross(mix_send_1)
-    qkv_2, logs_2, mix_own_2, mix_send_2 = forward([attn_in_2], small, qkv_two, 2, 0)
-    mix_send_2, mix_recv_0, mix_recv_1, b_4 = tie(mix_send_2, mix_recv_0, mix_recv_1, b_4)
-
+    out_c, out_d = cross(two_8), cross(two_c)
+    b_4 = join(pack_b, *b_z)
+    token, qkv_2, logs_2, mix_own_2, mix_send_2 = attend_forward(
+        token, [attn_in], small, mine, core_id, counts_all, [two_8, two_c], rows, each, 4, 2, 6, 0
+    )
+    token, a_b, a_c1, b_4, mix_recv_1, out_c, out_d, qkv_2, logs_2, mix_own_2, mix_send_2 = tie(
+        token, a_b, a_c1, b_4, mix_recv_1, out_c, out_d, qkv_2, logs_2, mix_own_2, mix_send_2
+    )
+    a_c2 = flip(a_b, 8)
     mix_recv_2 = cross(mix_send_2)
-    b_b = flip(b_4, 4)
-    mixes = [mix_own_0, mix_own_1, mix_own_2, mix_recv_0, mix_recv_1, mix_recv_2]
-    places = [(0, 0), (0, 128), (0, 256), (1, 0), (1, 128), (1, 256)]
+    mixes = [mix_own_1, mix_own_2, mix_recv_1, mix_recv_2]
+    places = [(0, 0), (0, 256), (1, 0), (1, 256)]
     out_pieces = ([two_8, two_c], [out_c, out_d])
-    resid, mlp_own = project_norm(mixes, places, embed, small, meta, *out_pieces, rows)
-    mlp_own, a_c, b_b = tie(mlp_own, a_c, b_b)
+    token, resid, mlp_own = project_norm(
+        token, mixes, places, embed, small, meta, *out_pieces, rows
+    )
+    token, a_c2, resid, mlp_own = tie(token, a_c2, resid, mlp_own)
     mlp_other = cross(mlp_own)
-    b_8 = join(b_4, b_b)
-
-    mlp_own, mlp_other, b_8 = tie(mlp_own, mlp_other, b_8)
-    b_c = flip(b_8, 8)
-    biases = [lax.dynamic_slice(small, (8 + 2 * core + h, 0), (1, width)) for h in range(2)]
+
+    token, mlp_own, mlp_other, b_4, resid = tie(token, mlp_own, mlp_other, b_4, resid)
+    b_rest = [flip(b_4, p) for p in (4, 8, 12)]
     groups, cots = [mlp_own, mlp_other], [cotangent, cot_other]
-    own_out_a, own_dm_a, sent_out_a, sent_dm_a, bias_up_a, keep_a, send_a = mlp_both(
-        groups, cots, mine, counts_all, biases[0], [a_8, a_c], rows, True
-    )
-    mlp_own, mlp_other, send_a, b_c, sent_dm_a, sent_out_a = tie(
-        mlp_own, mlp_other, send_a, b_c, sent_dm_a, sent_out_a
-    )
-    groups = [mlp_own, mlp_other]
-    a_r3 = flip(send_a, 8)
+    token, *made_a = mlp_both(
+        token, groups, cots, mine, counts_all, small, 8, [a_4, a_b, a_c1, a_c2], rows, True
+    )
+    token, *both = tie(token, *b_rest, *made_a)
+    b_rest, made_a = both[:3], both[3:]
+    own_out_a, own_dm_a, sent_out_a, sent_dm_a, bias_up_a, keep_a, *sends = made_a
+
+    a_r3 = [flip(send, 8) for send in sends]
     recv_dm_a, recv_out_a = cross(sent_dm_a), cross(sent_out_a)
-    own_out_b, own_dm_b, sent_out_b, sent_dm_b, bias_up_b, keep_b, send_b = mlp_both(
-        groups, cots, mine, counts_all, biases[1], [b_8, b_c], rows, True
-    )
-    sent_dm_b, sent_out_b, send_b, a_r3, recv_dm_a, recv_out_a = tie(
-        sent_dm_b, sent_out_b, send_b, a_r3, recv_dm_a, recv_out_a
-    )
-    b_r3 = flip(send_b, 8)
+    token, *made_b = mlp_both(
+        token, groups, cots, mine, counts_all, small, 9, [b_4, *b_rest], rows, True
+    )
+    token, *both = tie(token, *a_r3, recv_dm_a, recv_out_a, *made_b)
+    a_r3, (recv_dm_a, recv_out_a), made_b = both[:2], both[2:4], both[4:]
+    own_out_b, own_dm_b, sent_out_b, sent_dm_b, bias_up_b, keep_b, *sends = made_b
+
     recv_dm_b = cross(sent_dm_b)
-    send_a = onward(4, 8, keep_a, a_r3).astype(BF)
-    recv_dm_b, send_a = tie(recv_dm_b, send_a)
-
+    send_a = (keep_a[4:].astype(F32) + a_r3[1].astype(F32)).astype(BF)
+    token, recv_dm_b, send_a = tie(token, recv_dm_b, send_a)
     a_r2 = flip(send_a, 4)
     dms = [own_dm_a, own_dm_b, recv_dm_a, recv_dm_b]
-    d_mix_own, d_mix_send, proj, d_resid, sums_two = norm_two_back(
-        dms, resid, cotangent, small, meta, counts, *out_pieces, rows, part
-    )
-    d_mix_send, proj, sent_out_b = tie(d_mix_send, proj, sent_out_b)
+    token, d_mix_own, d_mix_send, proj, d_resid, sums_two = norm_two_back(
+        token, dms, resid, cotangent, small, meta, counts, *out_pieces, rows, part
+    )
+    token, a_r2, d_mix_own, d_mix_send, proj, d_resid, sums_two, sent_out_b = tie(
+        token, a_r2, d_mix_own, d_mix_send, proj, d_resid, sums_two, sent_out_b
+    )
+
     d_mix_recv = cross(d_mix_send)
-    keep_o, send_o = out_weight_grad(mixes, places, proj, meta, rows)
-    d_mix_recv, send_o, b_r3, a_r2 = tie(d_mix_recv, send_o, b_r3, a_r2)
-    send_b = onward(4, 8, keep_b, b_r3).astype(BF)
-    sends_a = [onward(k, k + 1, keep_a, a_r3, a_r2).astype(BF) for k in (1, 2, 3)]
-
-    d_mix_recv, send_b, send_o, sent_out_b, *sends_a = tie(
-        d_mix_recv, send_b, send_o, sent_out_b, *sends_a
-    )
-    b_r2 = flip(send_b, 4)
+    recv_out_b = cross(sent_out_b)
+    sends_a = [onward(k, k + 1, keep_a, a_r3[0], a_r2).astype(BF) for k in (1, 2, 3)]
+    token, keep_o, send_o = out_weight_grad(token, mixes, places, proj, meta, rows)
+    token, d_mix_recv, keep_o, send_o, recv_out_b, *both = tie(
+        token, d_mix_recv, keep_o, send_o, recv_out_b, *sends, *sends_a
+    )
+    sends, sends_a = both[:2], both[2:]
+
+    b_r3 = [flip(send, 8) for send in sends]
     a_rz = along_z(sends_a)
     recv_o = cross(send_o)
-    recv_out_b = cross(sent_out_b)
     d_mixes = [d_mix_own, d_mix_recv]
-    back = lambda qkv, logs, pair, ins: attend_back(
-        [ins], qkv, logs, d_mixes, mine, counts_all, rows, True, 0, pair, 1
-    )
-    d_qkv_0, bias_grad_0, keep_0, send_0 = back(qkv_0, logs_0, 0, attn_in)
-    send_0, b_r2, *a_rz, recv_o, recv_out_b = tie(send_0, b_r2, *a_rz, recv_o, recv_out_b)
-    sends_b = [onward(k, k + 1, keep_b, b_r3, b_r2).astype(BF) for k in (1, 2, 3)]
-    shard_a = onward(0, 1, keep_a, a_r3, a_r2, *a_rz)[0]
-
-    send_0, shard_a, attn_in_1, *sends_b = tie(send_0, shard_a, attn_in, *sends_b)
+    back = lambda token, qkv, logs, first, pair: attend_back(
+        token, [attn_in], qkv, logs, d_mixes, mine, counts_all, rows, True, first, pair, 1
+    )
+    token, *made_0 = back(token, qkv_1, logs_1, 0, 0)
+    token, *both = tie(token, *b_r3, *a_rz, recv_o, *made_0)
+    b_r3, a_rz, (recv_o, d_qkv_0, bias_grad_0, keep_0, send_0) = both[:2], both[2:5], both[5:]
+    send_b = (keep_b[4:].astype(F32) + b_r3[1].astype(F32)).astype(BF)
+    total_o = (keep_o.astype(F32) + recv_o.astype(F32)).astype(BF)
+
+    token, total_o, send_b = tie(token, total_o, send_b)
+    b_r2 = flip(send_b, 4)
+    token, *made_1 = back(token, qkv_1, logs_1, 1, 1)
+    token, b_r2, d_qkv_1, bias_grad_1, keep_1, send_1 = tie(token, b_r2, *made_1)
+    sends_b = [onward(k, k + 1, keep_b, b_r3[0], b_r2).astype(BF) for k in (1, 2, 3)]
+    send_q = beside(send_0, send_1, total_o[8:])
+
+    token, send_q, *sends_b = tie(token, send_q, *sends_b)
+    q_r3 = flip(send_q, 8)
     b_rz = along_z(sends_b)
-    other_a = cross(shard_a)
-    d_qkv_1, bias_grad_1, keep_1, send_1 = back(qkv_1, logs_1, 1, attn_in_1)
-    send_1, *b_rz, other_a = tie(send_1, *b_rz, other_a)
-    keep_q = jnp.concatenate([keep_0, keep_1, keep_o[:8] + recv_o[:8].astype(F32)], axis=2)
-    send_o = keep_o[8:] + recv_o[8:].astype(F32)
-    send_q = jnp.concatenate([send_0, send_1, send_o.astype(BF)], axis=2)
-    shard_b = onward(0, 1, keep_b, b_r3, b_r2, *b_rz)[0]
-
-    send_q, shard_b, attn_in_2 = tie(send_q, shard_b, attn_in)
-    q_r3 = flip(send_q, 8)
-    other_b = cross(shard_b)
-    d_qkv_2, bias_grad_2, keep_r, send_r = back(qkv_2, logs_2, 2, attn_in_2)
-    d_qkv_2, send_r, q_r3, other_b = tie(d_qkv_2, send_r, q_r3, other_b)
+    token, *made_2 = back(token, qkv_2, logs_2, 0, 2)
+    token, q_r3, *both = tie(token, q_r3, *b_rz, *made_2)
+    b_rz, (d_qkv_2, bias_grad_2, keep_r, send_r) = both[:3], both[3:]
+    keep_q = beside(keep_0, keep_1, total_o[:8])
     send_q = onward(4, 8, keep_q, q_r3).astype(BF)
 
-    d_qkv_2, send_r, send_q = tie(d_qkv_2, send_r, send_q)
+    token, send_q, send_r = tie(token, send_q, send_r)
     r_r3 = flip(send_r, 8)
     q_r2 = flip(send_q, 4)
-    da_own, da_send = attn_in_grad(
-        [d_qkv_0, d_qkv_1, d_qkv_2], mine, [(qkv_one, 768), (qkv_two, 384)], rows, each, width
-    )
-    da_send, r_r3, q_r2 = tie(da_send, r_r3, q_r2)
+    token, da_own, da_send = attn_in_grad(
+        token, [d_qkv_0, d_qkv_1, d_qkv_2], mine, [([one_8, one_c], 768), ([two_8, two_c], 384)], rows, each, width
+    )
+    token, r_r3, q_r2, da_own, da_send = tie(token, r_r3, q_r2, da_own, da_send)
+
     send_r = onward(4, 8, keep_r, r_r3).astype(BF)
-    sends_q = [onward(k, k + 1, keep_q, q_r3, q_r2).astype(BF) for k in (1, 2, 3)]
-
-    da_send, send_r, *sends_q = tie(da_send, send_r, *sends_q)
+    token, send_r = tie(token, send_r)
+    r_r2 = flip(send_r, 4)
     da_recv = cross(da_send)
-    r_r2 = flip(send_r, 4)
-    q_rz = along_z(sends_q)
-    token_grad, sums_one = norm_one_back([da_own, da_recv], embed, d_resid, small)
-    r_r2, sums_one = tie(r_r2, sums_one)
-    sends_r = [onward(k, k + 1, keep_r, r_r3, r_r2).astype(BF) for k in (1, 2, 3)]
-
-    resid, *sends_r = tie(resid, *sends_r)
-    r_rz = along_z(sends_r)
-    g_up, g_down, squares_mlp = interleave((shard_a, shard_b), (other_a, other_b), place)
-    bias_grads = [bias_grad_0, bias_grad_1, bias_grad_2]
-    sums = gather_sums(
-        place, sums_one, sums_two, bias_grads, (bias_up_a, bias_up_b), squares_mlp, squares_w
-    )
+    token, token_grad, sums_one = norm_one_back(
+        token, [da_own, da_recv], embed, d_resid, small
+    )
+    token, r_r2, token_grad, sums_one = tie(token, r_r2, token_grad, sums_one)
+
+    sends_z = [
+        beside(
+            onward(k, k + 1, keep_q, q_r3, q_r2).astype(BF),
+            onward(k, k + 1, keep_r, r_r3, r_r2).astype(BF),
+        )
+        for k in (1, 2, 3)
+    ]
+    token, resid, keep_a, keep_b, *sends_z = tie(token, resid, keep_a, keep_b, *sends_z)
+    recv_z = along_z(sends_z)
+    shard_m = jnp.concatenate(
+        [
+            onward(0, 1, keep_a, a_r3[0], a_r2, *a_rz)[0],
+            onward(0, 1, keep_b, b_r3[0], b_r2, *b_rz)[0],
+        ],
+        axis=1,
+    )
+    other_m = cross(shard_m)
     block_rows = resid + small[7]
     for value in (own_out_a, own_out_b, recv_out_a, recv_out_b):
         block_rows = block_rows + value.astype(F32)
     block_out = block_rows.astype(BF)
-    *q_rz, block_out, sums = tie(*q_rz, block_out, sums)
-    shard_q = onward(0, 1, keep_q, q_r3, q_r2, *q_rz)[0]
-    *r_rz, shard_q = tie(*r_rz, shard_q)
+    token, g_up, g_down, squares_mlp = interleave(token, shard_m, other_m, place)
+    bias_grads = [bias_grad_0, bias_grad_1, bias_grad_2]
+    token, sums = gather_sums(
+        token, place, sums_one, sums_two, bias_grads, (bias_up_a, bias_up_b), squares_mlp, squares_w
+    )
+    token, block_out, *both = tie(token, block_out, g_up, g_down, sums, *recv_z)
+    g_up, g_down, sums, *recv_z = both
+    token, shard_q, sums = last_shards(
+        token, sums, (keep_q, q_r3, q_r2), (keep_r, r_r3, r_r2), recv_z
+    )
     other_q = cross(shard_q)
-    shard_r, sums = last_shards(sums, keep_r, [r_r3, r_r2, *r_rz], shard_q)
-    other_r = cross(shard_r)
     sums = links.sum_all(sums)
-    results = update_all(
-        state, sums, place, (shard_q, other_q), (shard_r, other_r), g_up, g_down, 3
-    )
+    results = update_all(token, state, sums, place, (shard_q, other_q), g_up, g_down, 3)[1:]
     outs = [x.T if k % 5 == 4 else x for k, x in enumerate(results[:15])]
     return (block_out, token_grad) + tuple(outs) + (results[15][0, :10],)
 
@@ -1400,23 +1466,28 @@
     bias_up = table[:, 8:].reshape(1, -1)
     hidden = bias_up.shape[1]
     order = jnp.zeros((33,), jnp.int32)
-    embed = embed_rows([tokens], [positions.astype(F32)[..., None]])
-    attn_in, qkv, logs, mixed = attend_forward(
-        [embed], vectors, order, order, counts, [wq], width, each, 0, heads, 0, 0
+    token = jnp.zeros((8, 128), F32)
+    token, embed = embed_rows(token, [tokens], [positions.astype(F32)[..., None]])
+    token, attn_in, qkv, logs, mixed = attend_forward(
+        token, [embed], vectors, order, order, counts, [wq], width, each, 0, heads, 0, 0
     )
     places = [(0, 0)]
-    resid, mlp_in = project_norm([mixed], places, embed, vectors, order, [wo[None]], [], width)
+    token, resid, mlp_in = project_norm(
+        token, [mixed], places, embed, vectors, order, [wo[None]], [], width
+    )
     outs, dms, bias_ups, ups, downs = [], [], [], [], []
     parts = 4
     size = hidden // parts
     for h in range(parts):
         cols = slice(h * size, (h + 1) * size)
-        out, dm, bias, g_up, g_down = mlp_both(
+        token, out, dm, bias, g_up, g_down = mlp_both(
+            token,
             [mlp_in],
             [cotangent],
             order,
             counts,
             bias_up[:, cols],
+            0,
             [up[:, cols][None], down[cols][None]],
             width,
             False,
@@ -1426,17 +1497,18 @@
         bias_ups.append(bias)
         ups.append(g_up[0])
         downs.append(g_down[0])
-    d_mix, proj, d_resid, sums_two = norm_two_back(
-        dms, resid, cotangent, vectors, order, counts, [wo[None]], [], width, width
-    )
-    g_out = out_weight_grad([mixed], places, proj, order, width)[0][0]
-    d_qkv, bias_grad, g_qkv = attend_back(
-        [attn_in], qkv, logs, [d_mix], order, counts, width, False, 0, 0, pairs
+    token, d_mix, proj, d_resid, sums_two = norm_two_back(
+        token, dms, resid, cotangent, vectors, order, counts, [wo[None]], [], width, width
+    )
+    token, g_out = out_weight_grad(token, [mixed], places, proj, order, width)
+    g_out = g_out[0]
+    token, d_qkv, bias_grad, g_qkv = attend_back(
+        token, [attn_in], qkv, logs, [d_mix], order, counts, width, False, 0, 0, pairs
     )
     natural = lambda g: jnp.swapaxes(g.reshape(-1, pairs, 3, 128), 1, 2).reshape(-1, 3 * width)
     g_qkv, bias_grad = natural(g_qkv), natural(bias_grad)
-    da = attn_in_grad([d_qkv], order, [([wq], 3 * width)], width, each, width)[0]
-    token_grad, sums_one = norm_one_back([da], embed, d_resid, vectors)
+    token, da = attn_in_grad(token, [d_qkv], order, [([wq], 3 * width)], width, each, width)
+    token, token_grad, sums_one = norm_one_back(token, [da], embed, d_resid, vectors)
     block_rows = resid + vectors[7]
     for value in outs:
         block_rows = block_rows + value

time: 292 us -> 282 us (0.966)
  Pallas kernels: 153 us -> 144 us
  other arithmetic: 19.8 us -> 13.2 us
  waiting for transfers between devices: 31 us -> 37 us
    pallas_call x20 -> x19, Pallas kernels: 153 us -> 144 us  [apply(): token_out, *outs = run(token, *args)]
    ppermute x21 -> x18, waiting for transfers between devices: 3.78 us -> 7.69 us  [cross(): return lax.ppermute(x, AXES, pairs)]
    ppermute x46, starting transfers between devices: 60.7 us -> 64.2 us  [flip(): return lax.ppermute(x, AXES, pairs)]
    unnamed x171 -> x149, local copies, waits for them, and re-layouts: 11.4 us -> 8.53 us
  transfers between devices with their start and end apart: 67 -> 64, of which waited for: 19 -> 17; matrix products, arithmetic and copies ran while one was open for 4% -> 4% of each run, Pallas kernels for 51% -> 50%
where the time goes in v2:
time: 282 us; the launch traced here: 279 us
  Pallas kernels  144 us (51%)
  starting transfers between devices  66.8 us (24%)
  waiting for transfers between devices  37 us (13%)
  local copies, waits for them, and re-layouts  15.3 us (5%)
  other arithmetic  13.2 us (5%)
    pallas_call x19, Pallas kernels, apply(): token_out, *outs = run(token, *args)  144 us
    ppermute x46, starting transfers between devices, flip(): return lax.ppermute(x, AXES, pairs)  64.2 us
    ppermute x46, waiting for transfers between devices, flip(): return lax.ppermute(x, AXES, pairs)  29.3 us
    unnamed x149, local copies, waits for them, and re-layouts  8.53 us
    ppermute x18, waiting for transfers between devices, cross(): return lax.ppermute(x, AXES, pairs)  7.69 us
  transfers between devices with their start and end apart: 64, of which 17 were waited for; matrix products, arithmetic and copies ran while one was open for 4% of the time, Pallas kernels for 50%

profile of v2, /device:TPU:0, one launch (start us, length us, event | category | flops | bytes accessed | tf_op | source)
XLA Modules:
  0.0 279.1 jit_solution(12008906233103179622)
XLA Ops:
  2.7 3.1 %collective-permute-start.2 = (bf16[1,48,1664]{2,1,0:T(8,128)(2,1)S(1)}, bf16[1,48,1664]{2,1,0:T(8,128)(2,1)}, u32[]{:S(2)}, u32[]{:S(2)}) collective-permute-start(bf16[1,48,1664]{2,1,0:T(8,128)(2,1)S(1)} %fusion.6), channel_id=1, source_target_pairs={{0,4},{1,5},{2,6},{3,7},{4,0},{5,1},{6,2},{7,3},{8,12},{9,13},{10,... | collective-permute-start | bytes 479240 | tf_op jit(solution)/shard_map/ppermute | solution.py:97
  5.8 2.6 collective-permute-start.3
  11.3 4.9 %embed_rows.2 = (f32[8,128]{1,0:T(8,128)S(1)}, f32[2,392,768]{2,1,0:T(8,128)S(1)}) custom-call(f32[8,128]{1,0:T(8,128)S(1)} %broadcast_in_dim.21.token_ref, f32[8,768]{1,0:T(8,128)S(1)} %copy-done.21, bf16[2,392,768]{2,1,0:T(8,128)(2,1)} %refs_1_.1, f32[2,392,1]{2,1,0:T(8,128)S(1)} %copy.67.refs_2_), custom_call_target="tpu_custom_call", output_to_operand_aliasing={{0}: (0, {})} | custom-call | flops 4000000000 | bytes 12000000 | tf_op jit(solution)/shard_map/embed_rows/pallas_call | solution.py:57
  18.6 2.1 collective-permute-done.3
  21.9 1.6 collective-permute-start.5
  23.4 2.6 collective-permute-start.6
  27.0 1.5 collective-permute-start.8
  28.7 4.7 %embed_rows.3 = (f32[8,128]{1,0:T(8,128)S(1)}, f32[2,392,768]{2,1,0:T(8,128)S(1)}) custom-call(f32[8,128]{1,0:T(8,128)S(1)} %get-tuple-element.312.token_ref, f32[8,768]{1,0:T(8,128)S(1)} %copy-done.21, bf16[2,392,768]{2,1,0:T(8,128)(2,1)} %collective-permute-done.refs_1_, f32[2,392,1]{2,1,0:T(8,128)S(1)} %copy.70.refs_2_), custom_call_target="tpu_custom_call", output_to_operand_aliasing={{0}: (0, {})} | custom-call | flops 4000000000 | bytes 12000000 | tf_op jit(solution)/shard_map/embed_rows/pallas_call | solution.py:57
  36.0 1.6 collective-permute-start.9
  38.0 1.5 collective-permute-start.11
  39.4 1.5 collective-permute-start.12
  40.9 1.5 collective-permute-start.13
  42.7 5.4 %collective-permute-done.12 = bf16[1,48,768]{2,1,0:T(8,128)(2,1)S(1)} collective-permute-done((bf16[1,48,768]{2,1,0:T(8,128)(2,1)S(1)}, bf16[1,48,768]{2,1,0:T(8,128)(2,1)S(1)}, u32[]{:S(2)}, u32[]{:S(2)}) %collective-permute-start.12) | collective-permute-done | bytes 73760 | tf_op jit(solution)/shard_map/ppermute | solution.py:97
  49.6 1.5 collective-permute-start.17
  51.1 1.5 collective-permute-start.18
  54.7 14.1 %attend_forward.2 = (f32[8,128]{1,0:T(8,128)S(1)}, f32[16,768]{1,0:T(8,128)S(1)}, bf16[4,392,768]{2,1,0:T(8,128)(2,1)S(1)}, bf16[4,392,768]{2,1,0:T(8,128)(2,1)}...) custom-call(f32[8,128]{1,0:T(8,128)S(1)} %get-tuple-element.337.toke, ...), custom_call_target="tpu_custom_call", output_to_operand_aliasing={{0}: (0, {})} | custom-call | flops 8000000000 | bytes 24000000 | tf_op jit(solution)/shard_map/attend_forward/pallas_call | solution.py:57
  70.3 6.8 %attend_forward.3 = (f32[8,128]{1,0:T(8,128)S(1)}, bf16[4,392,384]{2,1,0:T(8,128)(2,1)S(1)}, f32[4,2,392]{2,1,0:T(2,128)S(1)}, bf16[2,392,128]{2,1,0:T(8,128)(2,1)S(1)}, bf16[2,392,128]{2,1,0:T(8,128)(2,1)S(1)}) custom-call(f32[8,128]{1,0:T(8,128)S(1)} %get-tuple-element.351.token_ref, ...), custom_call_target="tpu_custom_call", output_to_operand_aliasing={{0}: (0, {})} | custom-call | flops 8000000000 | bytes 24000000 | tf_op jit(solution)/shard_map/attend_forward/pallas_call | solution.py:57
  80.4 4.3 %project_norm.1 = (f32[8,128]{1,0:T(8,128)S(1)}, f32[2,392,768]{2,1,0:T(8,128)S(1)}, bf16[2,392,768]{2,1,0:T(8,128)(2,1)S(1)}) custom-call(f32[8,128]{1,0:T(8,128)S(1)} %get-tuple-element.366.token_ref, s32[33]{0:T(128)S(1)} %pad_add_fusion.3.refs_0_, ...), custom_call_target="tpu_custom_call", output_to_operand_aliasing={{0}: (0, {})} | custom-call | flops 6000000000 | bytes 18000000 | tf_op jit(solution)/shard_map/project_norm/pallas_call | solution.py:57
  84.7 4.4 %collective-permute-done.24.refs_10_ = bf16[4,48,1536]{2,1,0:T(8,128)(2,1)S(1)} collective-permute-done((bf16[4,48,1536]{2,1,0:T(8,128)(2,1)}, bf16[4,48,1536]{2,1,0:T(8,128)(2,1)S(1)}, u32[]{:S(2)}, u32[]{:S(2)}) %collective-permute-start.24) | collective-permute-done | bytes 589856 | tf_op jit(solution)/shard_map/ppermute | solution.py:97
  89.1 2.9 %collective-permute-done.25.refs_4_ = bf16[2,392,768]{2,1,0:T(8,128)(2,1)S(1)} collective-permute-done((bf16[2,392,768]{2,1,0:T(8,128)(2,1)S(1)}, bf16[2,392,768]{2,1,0:T(8,128)(2,1)S(1)}, u32[]{:S(2)}, u32[]{:S(2)}) %collective-permute-start.25) | collective-permute-done | bytes 1204256 | tf_op jit(solution)/shard_map/ppermute | solution.py:101
  95.0 1.5 collective-permute-start.28
  96.5 22.9 %mlp_both.2 = (f32[8,128]{1,0:T(8,128)}, bf16[2,392,768]{2,1,0:T(8,128)(2,1)}, bf16[2,392,768]{2,1,0:T(8,128)(2,1)}, bf16[2,392,768]{2,1,0:T(8,128)(2,1)}, bf16[...) custom-call(f32[8,128]{1,0:T(8,128)} %copy-done.5, ...), custom_call_target="tpu_custom_call", output_to_operand_aliasing={{0}: (0, {})} | custom-call | flops 23000000512 | bytes 69000000 | tf_op jit(solution)/shard_map/mlp_both/pallas_call | solution.py:57
  119.4 2.8 collective-permute-done.28.refs_10_
  124.7 23.3 %mlp_both.3 = (f32[8,128]{1,0:T(8,128)}, bf16[2,392,768]{2,1,0:T(8,128)(2,1)}, bf16[2,392,768]{2,1,0:T(8,128)(2,1)}, bf16[2,392,768]{2,1,0:T(8,128)(2,1)}, bf16[...) custom-call(f32[8,128]{1,0:T(8,128)} %get-tuple-element.397.token_re, ...), custom_call_target="tpu_custom_call", output_to_operand_aliasing={{0}: (0, {})} | custom-call | flops 23000000512 | bytes 69000000 | tf_op jit(solution)/shard_map/mlp_both/pallas_call | solution.py:57
  148.2 1.5 add_convert_fusion.3
  149.7 1.6 collective-permute-done.33.refs_8_
  153.8 6.6 %norm_two_back.1 = (f32[8,128]{1,0:T(8,128)S(1)}, bf16[2,392,384]{2,1,0:T(8,128)(2,1)S(1)}, bf16[2,392,384]{2,1,0:T(8,128)(2,1)S(1)}, bf16[2,392,768]{2,1,0:T(8,...) custom-call(f32[8,128]{1,0:T(8,128)S(1)} %copy-done.6, ...), custom_call_target="tpu_custom_call", output_to_operand_aliasing={{0}: (0, {})} | custom-call | flops 7000000000 | bytes 21000000 | tf_op jit(solution)/shard_map/norm_two_back/pallas_call | solution.py:57
  161.7 5.1 %out_weight_grad.1 = (f32[8,128]{1,0:T(8,128)S(1)}, bf16[16,48,384]{2,1,0:T(8,128)(2,1)S(1)}, bf16[16,48,384]{2,1,0:T(8,128)(2,1)S(1)}) custom-call(f32[8,128]{1,0:T(8,128)S(1)} %get-tuple-element.432.token_ref, s32[33]{0:T(128)S(1)} %pad_add_fusion.3.refs_0_, bf16[2,392,768]{2,1,0:T(8,128)(2,1)S(1)} %get-tuple-element.433.refs_1_, ...), custom_call_target="tpu_custom_call", output_to_operand_aliasing={{0}: (0, {})} | custom-call | flops 5000000000 | bytes 15000000 | tf_op jit(solution)/shard_map/out_weight_grad/pallas_call | solution.py:57
  166.8 1.5 add_convert_fusion.9
  170.9 2.5 collective-permute-start.40
  174.2 2.5 collective-permute-start.41
  176.7 11.3 %attend_back.3 = (f32[8,128]{1,0:T(8,128)S(1)}, bf16[4,392,384]{2,1,0:T(8,128)(2,1)S(1)}, f32[1,384]{1,0:T(1,128)S(1)}, bf16[8,48,384]{2,1,0:T(8,128)(2,1)S(1)}, bf16[8,48,384]{2,1,0:T(8,128)(2,1)S(1)}) custom-call(f32[8,128]{1,0:T(8,128)S(1)} %get-tuple-element.443.token_ref, s32[17]{0:T(128)S(1)} %copy-done.23, ...), custom_call_target="tpu_custom_call", output_to_operand_aliasing={{0}: (0, {})} | custom-call | flops 12000000000 | bytes 36000000 | tf_op jit(solution)/shard_map/attend_back/pallas_call | solution.py:57
  190.3 11.1 %attend_back.4 = (f32[8,128]{1,0:T(8,128)S(1)}, bf16[4,392,384]{2,1,0:T(8,128)(2,1)S(1)}, f32[1,384]{1,0:T(1,128)S(1)}, bf16[8,48,384]{2,1,0:T(8,128)(2,1)S(1)}, bf16[8,48,384]{2,1,0:T(8,128)(2,1)S(1)}) custom-call(f32[8,128]{1,0:T(8,128)S(1)} %get-tuple-element.464.token_ref, s32[17]{0:T(128)S(1)} %copy-done.23, ...), custom_call_target="tpu_custom_call", output_to_operand_aliasing={{0}: (0, {})} | custom-call | flops 12000000000 | bytes 36000000 | tf_op jit(solution)/shard_map/attend_back/pallas_call | solution.py:57
  203.6 2.1 collective-permute-start.46
  205.7 2.3 collective-permute-start.47
  208.0 11.1 %attend_back.5 = (f32[8,128]{1,0:T(8,128)S(1)}, bf16[4,392,384]{2,1,0:T(8,128)(2,1)S(1)}, f32[1,384]{1,0:T(1,128)S(1)}, bf16[8,48,384]{2,1,0:T(8,128)(2,1)S(1)}, bf16[8,48,384]{2,1,0:T(8,128)(2,1)S(1)}) custom-call(f32[8,128]{1,0:T(8,128)S(1)} %get-tuple-element.477.token_ref, s32[17]{0:T(128)S(1)} %copy-done.23, ...), custom_call_target="tpu_custom_call", output_to_operand_aliasing={{0}: (0, {})} | custom-call | flops 12000000000 | bytes 36000000 | tf_op jit(solution)/shard_map/attend_back/pallas_call | solution.py:57
  223.6 6.9 %attn_in_grad.1 = (f32[8,128]{1,0:T(8,128)S(1)}, f32[2,392,768]{2,1,0:T(8,128)S(1)}, bf16[2,392,768]{2,1,0:T(8,128)(2,1)S(1)}) custom-call(f32[8,128]{1,0:T(8,128)S(1)} %get-tuple-element.494.token_ref, s32[17]{0:T(128)S(1)} %copy-done.23, bf16[4,392,384]{2,1,0:T(8,128)(2,1)S(1)} %copy-done.37, ...), custom_call_target="tpu_custom_call", output_to_operand_aliasing={{0}: (0, {})} | custom-call | flops 7000000000 | bytes 21000000 | tf_op jit(solution)/shard_map/attn_in_grad/pallas_call | solution.py:57
  232.1 1.4 collective-permute-done.50.refs_4_
  233.5 3.2 %norm_one_back.1 = (f32[8,128]{1,0:T(8,128)S(1)}, f32[2,392,768]{2,1,0:T(8,128)}, f32[8,768]{1,0:T(8,128)S(1)}) custom-call(f32[8,128]{1,0:T(8,128)S(1)} %get-tuple-element.506.token_ref, f32[16,768]{1,0:T(8,128)S(1)} %copy-done.8, f32[2,392,768]{2,1,0:T(8,128)S(1)} %copy-done.28, f32[2,392,768]{2,1,0:T(8,128)S(1)} %copy-done.30, ...), custom_call_target="tpu_custom_call", output_to_operand_aliasing={{0}: (0, {})} | custom-call | flops 4000000000 | bytes 12000000 | tf_op jit(solution)/shard_map/norm_one_back/pallas_call | solution.py:57
  239.9 1.9 collective-permute-start.54
  241.8 2.5 collective-permute-start.55
  244.3 3.2 %add_convert_fusion = bf16[2,392,768]{2,1,0:T(8,128)(2,1)} fusion(bf16[2,392,768]{2,1,0:T(8,128)(2,1)S(1)} %copy-done.53, bf16[2,392,768]{2,1,0:T(8,128)(2,1)} %collective-permute-done.32, bf16[2,392,768]{2,1,0:T(8,128)(2,1)S(1)} %copy-done.51, bf16[2,392,768]{2,1,0:T(8,128)(2,1)S(1)} %copy-done.50, f32[2,392,768]{2,1,0:T(8,128)S(1)} %get-tuple-element.537.refs_3_, ...), kind=kLoop, calls=%fused_computation | loop fusion | flops 6021120 | bytes 8432640 | tf_op jit(solution)/shard_map/convert_element_type | solution.py:1436
  249.6 4.3 %collective-permute-done.54.refs_8_ = bf16[1,48,1536]{2,1,0:T(8,128)(2,1)S(1)} collective-permute-done((bf16[1,48,1536]{2,1,0:T(8,128)(2,1)S(1)}, bf16[1,48,1536]{2,1,0:T(8,128)(2,1)S(1)}, u32[]{:S(2)}, u32[]{:S(2)}) %collective-permute-start.54) | collective-permute-done | bytes 147488 | tf_op jit(solution)/shard_map/ppermute | solution.py:97
  255.5 3.2 %collective-permute-start.57 = (f32[16,768]{1,0:T(8,128)S(1)}, f32[16,768]{1,0:T(8,128)S(1)}, u32[]{:S(2)}, u32[]{:S(2)}) collective-permute-start(f32[16,768]{1,0:T(8,128)S(1)} %add.226), channel_id=1, source_target_pairs={{0,4},{1,5},{2,6},{3,7},{4,0},{5,1},{6,2},{7,3},{8,12},{9,13},{10,... | collective-permute-start | bytes 147464 | tf_op jit(solution)/shard_map/ppermute | solution.py:97
  258.8 2.4 collective-permute-start.59
  261.2 4.3 %collective-permute-done.58 = f32[16,768]{1,0:T(8,128)S(1)} collective-permute-done((f32[16,768]{1,0:T(8,128)S(1)}, f32[16,768]{1,0:T(8,128)S(1)}, u32[]{:S(2)}, u32[]{:S(2)}) %collective-permute-start.58) | collective-permute-done | bytes 49184 | tf_op jit(solution)/shard_map/ppermute | solution.py:97
  270.9 2.0 collective-permute-done.62
  273.0 5.3 %update_all.1 = (f32[8,128]{1,0:T(8,128)S(1)}, f32[48,2304]{1,0:T(8,128)}, f32[48,768]{1,0:T(8,128)}, f32[48,3072]{1,0:T(8,128)}, f32[192,768]{1,0:T(8,128)}, /*...) custom-call(f32[8,128]{1,0:T(8,128)S(1)} %get-tuple-element.555.toke, ...), custom_call_target="tpu_custom_call", output_to_operand_aliasing={{0}: (0, {})} | custom-call | flops 6000000000 | bytes 18000000 | tf_op jit(solution)/shard_map/update_all/pallas_call | solution.py:57
  (316 shorter events, 56.6 us)
Async XLA Ops:
  2.7 15.8 %collective-permute-start.2 = (bf16[1,48,1664]{2,1,0:T(8,128)(2,1)S(1)}, bf16[1,48,1664]{2,1,0:T(8,128)(2,1)}, u32[]{:S(2)}, u32[]{:S(2)}) collective-permute-start(bf16[1,48,1664]{2,1,0:T(8,128)(2,1)S(1)} %fusion.6), channel_id=1, source_target_pairs={{0,4},{1,5},{2,6},{3,7},{4,0},{5,1},{6,2},{7,3},{8,12},{9,13},{10,... | collective-permute-start | bytes 479240 | tf_op jit(solution)/shard_map/ppermute | solution.py:97
  5.8 14.9 %collective-permute-start.3 = (bf16[1,48,1664]{2,1,0:T(8,128)(2,1)S(1)}, bf16[1,48,1664]{2,1,0:T(8,128)(2,1)}, u32[]{:S(2)}, u32[]{:S(2)}) collective-permute-start(bf16[1,48,1664]{2,1,0:T(8,128)(2,1)S(1)} %fusion.6), channel_id=1, source_target_pairs={{0,8},{1,9},{2,10},{3,11},{4,12},{5,13},{6,14},{7,15},{8,0},{9,1},... | collective-permute-start | bytes 479240 | tf_op jit(solution)/shard_map/ppermute | solution.py:97
  8.4 12.3 %collective-permute-start.4 = (bf16[1,48,1664]{2,1,0:T(8,128)(2,1)S(1)}, bf16[1,48,1664]{2,1,0:T(8,128)(2,1)}, u32[]{:S(2)}, u32[]{:S(2)}) collective-permute-start(bf16[1,48,1664]{2,1,0:T(8,128)(2,1)S(1)} %fusion.6), channel_id=1, source_target_pairs={{0,12},{1,13},{2,14},{3,15},{4,8},{5,9},{6,10},{7,11},{8,4},{9,5},... | collective-permute-start | bytes 479240 | tf_op jit(solution)/shard_map/ppermute | solution.py:97
  8.6 10.0 %collective-permute-start.1 = (s32[2,393]{1,0:T(2,128)S(1)}, s32[2,393]{1,0:T(2,128)S(1)}, u32[]{:S(2)}, u32[]{:S(2)}) collective-permute-start(s32[2,393]{1,0:T(2,128)S(1)} %pad_add_fusion), channel_id=1, source_target_pairs={{0,16},{1,17},{2,18},{3,19},{4,20},{5,21},{6,22},{7,23},{8,24},{9,... | collective-permute-start | bytes 9440 | tf_op jit(solution)/shard_map/ppermute | solution.py:101
  8.6 12.1 %collective-permute-start = (bf16[2,392,768]{2,1,0:T(8,128)(2,1)}, bf16[2,392,768]{2,1,0:T(8,128)(2,1)}, u32[]{:S(2)}, u32[]{:S(2)}) collective-permute-start(bf16[2,392,768]{2,1,0:T(8,128)(2,1)} %refs_1_.1), channel_id=1, source_target_pairs={{0,16},{1,17},{2,18},{3,19},{4,20},{5,21},{6,22},{7,23},{8,24},{9,... | collective-permute-start | bytes 3612680 | tf_op jit(solution)/shard_map/ppermute | solution.py:101
  21.9 11.7 %collective-permute-start.5 = (bf16[4,48,1664]{2,1,0:T(8,128)(2,1)S(1)}, bf16[4,48,1664]{2,1,0:T(8,128)(2,1)}, u32[]{:S(2)}, u32[]{:S(2)}) collective-permute-start(bf16[4,48,1664]{2,1,0:T(8,128)(2,1)S(1)} %pad_maximum_fusion.3), channel_id=1, source_target_pairs={{0,1},{1,0},{2,3},{3,2},{4,5},{5,4},{6,7},{7,6},{8,9},{9,8},{10,11... | collective-permute-start | bytes 1916936 | tf_op jit(solution)/shard_map/ppermute | solution.py:97
  23.4 10.1 %collective-permute-start.6 = (bf16[1,48,768]{2,1,0:T(8,128)(2,1)S(1)}, bf16[1,48,768]{2,1,0:T(8,128)(2,1)S(1)}, u32[]{:S(2)}, u32[]{:S(2)}) collective-permute-start(bf16[1,48,768]{2,1,0:T(8,128)(2,1)S(1)} %reshape_squeeze.6), channel_id=1, source_target_pairs={{0,4},{1,5},{2,6},{3,7},{4,0},{5,1},{6,2},{7,3},{8,12},{9,13},{10,... | collective-permute-start | bytes 221192 | tf_op jit(solution)/shard_map/ppermute | solution.py:97
  26.0 7.5 %collective-permute-start.7 = (bf16[1,48,768]{2,1,0:T(8,128)(2,1)S(1)}, bf16[1,48,768]{2,1,0:T(8,128)(2,1)S(1)}, u32[]{:S(2)}, u32[]{:S(2)}) collective-permute-start(bf16[1,48,768]{2,1,0:T(8,128)(2,1)S(1)} %reshape_squeeze.6), channel_id=1, source_target_pairs={{0,8},{1,9},{2,10},{3,11},{4,12},{5,13},{6,14},{7,15},{8,0},{9,1},... | collective-permute-start | bytes 221192 | tf_op jit(solution)/shard_map/ppermute | solution.py:97
  35.9 12.2 %collective-permute-start.10 = (bf16[2,392,768]{2,1,0:T(8,128)(2,1)}, bf16[2,392,768]{2,1,0:T(8,128)(2,1)}, u32[]{:S(2)}, u32[]{:S(2)}) collective-permute-start(bf16[2,392,768]{2,1,0:T(8,128)(2,1)} %refs_4_), channel_id=1, source_target_pairs={{0,16},{1,17},{2,18},{3,19},{4,20},{5,21},{6,22},{7,23},{8,24},{9,... | collective-permute-start | bytes 3612680 | tf_op jit(solution)/shard_map/ppermute | solution.py:101
  36.0 12.1 %collective-permute-start.9 = (bf16[8,48,896]{2,1,0:T(8,128)(2,1)S(1)}, bf16[8,48,896]{2,1,0:T(8,128)(2,1)}, u32[]{:S(2)}, u32[]{:S(2)}) collective-permute-start(bf16[8,48,896]{2,1,0:T(8,128)(2,1)S(1)} %pad_maximum_fusion.2.refs_5_.refs_4_), channel_id=1, source_target_pairs={{0,2},{1,3},{2,0},{3,1},{4,6},{5,7},{6,4},{7,5},{8,10},{9,11},{10,... | collective-permute-start | bytes 2064392 | tf_op jit(solution)/shard_map/ppermute | solution.py:97
  39.4 8.6 %collective-permute-start.12 = (bf16[1,48,768]{2,1,0:T(8,128)(2,1)S(1)}, bf16[1,48,768]{2,1,0:T(8,128)(2,1)S(1)}, u32[]{:S(2)}, u32[]{:S(2)}) collective-permute-start(bf16[1,48,768]{2,1,0:T(8,128)(2,1)S(1)} %get-tuple-element.327), channel_id=1, source_target_pairs={{0,8},{1,9},{2,10},{3,11},{4,12},{5,13},{6,14},{7,15},{8,0},{9,1},... | collective-permute-start | bytes 221192 | tf_op jit(solution)/shard_map/ppermute | solution.py:97
  40.9 7.2 %collective-permute-start.13 = (bf16[1,48,768]{2,1,0:T(8,128)(2,1)S(1)}, bf16[1,48,768]{2,1,0:T(8,128)(2,1)S(1)}, u32[]{:S(2)}, u32[]{:S(2)}) collective-permute-start(bf16[1,48,768]{2,1,0:T(8,128)(2,1)S(1)} %get-tuple-element.327), channel_id=1, source_target_pairs={{0,12},{1,13},{2,14},{3,15},{4,8},{5,9},{6,10},{7,11},{8,4},{9,5},... | collective-permute-start | bytes 221192 | tf_op jit(solution)/shard_map/ppermute | solution.py:97
  48.2 20.6 %collective-permute-start.16 = (bf16[1,48,1536]{2,1,0:T(8,128)(2,1)S(1)}, bf16[1,48,1536]{2,1,0:T(8,128)(2,1)S(1)}, u32[]{:S(2)}, u32[]{:S(2)}) collective-permute-start(bf16[1,48,1536]{2,1,0:T(8,128)(2,1)S(1)} %copy-done.58), channel_id=1, source_target_pairs={{0,4},{1,5},{2,6},{3,7},{4,0},{5,1},{6,2},{7,3},{8,12},{9,13},{10,... | collective-permute-start | bytes 442376 | tf_op jit(solution)/shard_map/ppermute | solution.py:97
  49.6 19.3 %collective-permute-start.17 = (bf16[1,48,1536]{2,1,0:T(8,128)(2,1)S(1)}, bf16[1,48,1536]{2,1,0:T(8,128)(2,1)S(1)}, u32[]{:S(2)}, u32[]{:S(2)}) collective-permute-start(bf16[1,48,1536]{2,1,0:T(8,128)(2,1)S(1)} %copy-done.58), channel_id=1, source_target_pairs={{0,8},{1,9},{2,10},{3,11},{4,12},{5,13},{6,14},{7,15},{8,0},{9,1},... | collective-permute-start | bytes 442376 | tf_op jit(solution)/shard_map/ppermute | solution.py:97
  51.1 17.8 %collective-permute-start.18 = (bf16[1,48,1536]{2,1,0:T(8,128)(2,1)S(1)}, bf16[1,48,1536]{2,1,0:T(8,128)(2,1)S(1)}, u32[]{:S(2)}, u32[]{:S(2)}) collective-permute-start(bf16[1,48,1536]{2,1,0:T(8,128)(2,1)S(1)} %copy-done.58), channel_id=1, source_target_pairs={{0,12},{1,13},{2,14},{3,15},{4,8},{5,9},{6,10},{7,11},{8,4},{9,5},... | collective-permute-start | bytes 442376 | tf_op jit(solution)/shard_map/ppermute | solution.py:97
  52.6 16.3 %collective-permute-start.14 = (bf16[4,48,1536]{2,1,0:T(8,128)(2,1)S(1)}, bf16[4,48,1536]{2,1,0:T(8,128)(2,1)}, u32[]{:S(2)}, u32[]{:S(2)}) collective-permute-start(bf16[4,48,1536]{2,1,0:T(8,128)(2,1)S(1)} %maximum_maximum_fusion.refs_7_), channel_id=1, source_target_pairs={{0,1},{1,0},{2,3},{3,2},{4,5},{5,4},{6,7},{7,6},{8,9},{9,8},{10,11... | collective-permute-start | bytes 1769480 | tf_op jit(solution)/shard_map/ppermute | solution.py:97
  53.4 15.5 %collective-permute-start.15 = (bf16[8,48,768]{2,1,0:T(8,128)(2,1)S(1)}, bf16[8,48,768]{2,1,0:T(8,128)(2,1)S(1)}, u32[]{:S(2)}, u32[]{:S(2)}) collective-permute-start(bf16[8,48,768]{2,1,0:T(8,128)(2,1)S(1)} %pad_maximum_fusion.4.refs_5_.refs_7_.refs_9_.refs_6_), channel_id=1, source_target_pairs={{0,2},{1,3},{2,0},{3,1},{4,6},{5,7},{6,4},{7,5},{8,10},{9,11},{10,... | collective-permute-start | bytes 1769480 | tf_op jit(solution)/shard_map/ppermute | solution.py:97
  68.8 9.3 %collective-permute-start.21 = (bf16[8,48,768]{2,1,0:T(8,128)(2,1)S(1)}, bf16[8,48,768]{2,1,0:T(8,128)(2,1)S(1)}, u32[]{:S(2)}, u32[]{:S(2)}) collective-permute-start(bf16[8,48,768]{2,1,0:T(8,128)(2,1)S(1)} %pad_maximum_fusion.4.refs_5_.refs_7_.refs_9_.refs_6_), channel_id=1, source_target_pairs={{0,16},{1,17},{2,18},{3,19},{4,20},{5,21},{6,22},{7,23},{8,24},{9,... | collective-permute-start | bytes 1769480 | tf_op jit(solution)/shard_map/ppermute | solution.py:101
  69.0 9.9 %collective-permute-start.19 = (bf16[4,48,1536]{2,1,0:T(8,128)(2,1)S(1)}, bf16[4,48,1536]{2,1,0:T(8,128)(2,1)S(1)}, u32[]{:S(2)}, u32[]{:S(2)}) collective-permute-start(bf16[4,48,1536]{2,1,0:T(8,128)(2,1)S(1)} %maximum_maximum_fusion.refs_7_), channel_id=1, source_target_pairs={{0,2},{1,3},{2,0},{3,1},{4,6},{5,7},{6,4},{7,5},{8,10},{9,11},{10,... | collective-permute-start | bytes 1769480 | tf_op jit(solution)/shard_map/ppermute | solution.py:97
  69.8 9.1 %collective-permute-start.22 = (bf16[8,48,768]{2,1,0:T(8,128)(2,1)S(1)}, bf16[8,48,768]{2,1,0:T(8,128)(2,1)S(1)}, u32[]{:S(2)}, u32[]{:S(2)}) collective-permute-start(bf16[8,48,768]{2,1,0:T(8,128)(2,1)S(1)} %collective-permute-done.15.refs_6_.refs_8_.refs_10_.refs_7_), channel_id=1, source_target_pairs={{0,16},{1,17},{2,18},{3,19},{4,20},{5,21},{6,22},{7,23},{8,24},{9,... | collective-permute-start | bytes 1769480 | tf_op jit(solution)/shard_map/ppermute | solution.py:101
  70.2 8.0 %collective-permute-start.20 = (bf16[2,392,256]{2,1,0:T(8,128)(2,1)S(1)}, bf16[2,392,256]{2,1,0:T(8,128)(2,1)S(1)}, u32[]{:S(2)}, u32[]{:S(2)}) collective-permute-start(bf16[2,392,256]{2,1,0:T(8,128)(2,1)S(1)} %get-tuple-element.361), channel_id=1, source_target_pairs={{0,16},{1,17},{2,18},{3,19},{4,20},{5,21},{6,22},{7,23},{8,24},{9,... | collective-permute-start | bytes 1204232 | tf_op jit(solution)/shard_map/ppermute | solution.py:101
  78.9 10.2 %collective-permute-start.24 = (bf16[4,48,1536]{2,1,0:T(8,128)(2,1)}, bf16[4,48,1536]{2,1,0:T(8,128)(2,1)S(1)}, u32[]{:S(2)}, u32[]{:S(2)}) collective-permute-start(bf16[4,48,1536]{2,1,0:T(8,128)(2,1)} %collective-permute-done.14.refs_8_), channel_id=1, source_target_pairs={{0,2},{1,3},{2,0},{3,1},{4,6},{5,7},{6,4},{7,5},{8,10},{9,11},{10,... | collective-permute-start | bytes 1769480 | tf_op jit(solution)/shard_map/ppermute | solution.py:97
  93.0 26.4 %collective-permute-start.26 = (bf16[4,48,1536]{2,1,0:T(8,128)(2,1)}, bf16[4,48,1536]{2,1,0:T(8,128)(2,1)}, u32[]{:S(2)}, u32[]{:S(2)}) collective-permute-start(bf16[4,48,1536]{2,1,0:T(8,128)(2,1)} %pad_maximum_fusion.5.refs_7_), channel_id=1, source_target_pairs={{0,1},{1,0},{2,3},{3,2},{4,5},{5,4},{6,7},{7,6},{8,9},{9,8},{10,11... | collective-permute-start | bytes 1769480 | tf_op jit(solution)/shard_map/ppermute | solution.py:97
  94.0 25.4 %collective-permute-start.27 = (bf16[4,48,1536]{2,1,0:T(8,128)(2,1)}, bf16[4,48,1536]{2,1,0:T(8,128)(2,1)}, u32[]{:S(2)}, u32[]{:S(2)}) collective-permute-start(bf16[4,48,1536]{2,1,0:T(8,128)(2,1)} %pad_maximum_fusion.5.refs_7_), channel_id=1, source_target_pairs={{0,2},{1,3},{2,0},{3,1},{4,6},{5,7},{6,4},{7,5},{8,10},{9,11},{10,... | collective-permute-start | bytes 1769480 | tf_op jit(solution)/shard_map/ppermute | solution.py:97
  95.0 27.1 %collective-permute-start.28 = (bf16[4,48,1536]{2,1,0:T(8,128)(2,1)}, bf16[4,48,1536]{2,1,0:T(8,128)(2,1)}, u32[]{:S(2)}, u32[]{:S(2)}) collective-permute-start(bf16[4,48,1536]{2,1,0:T(8,128)(2,1)} %pad_maximum_fusion.5.refs_7_), channel_id=1, source_target_pairs={{0,3},{1,2},{2,1},{3,0},{4,7},{5,6},{6,5},{7,4},{8,11},{9,10},{10,... | collective-permute-start | bytes 1769480 | tf_op jit(solution)/shard_map/ppermute | solution.py:97
  122.2 25.9 %collective-permute-start.31 = (bf16[2,392,768]{2,1,0:T(8,128)(2,1)}, bf16[2,392,768]{2,1,0:T(8,128)(2,1)}, u32[]{:S(2)}, u32[]{:S(2)}) collective-permute-start(bf16[2,392,768]{2,1,0:T(8,128)(2,1)} %get-tuple-element.404), channel_id=1, source_target_pairs={{0,16},{1,17},{2,18},{3,19},{4,20},{5,21},{6,22},{7,23},{8,24},{9,... | collective-permute-start | bytes 3612680 | tf_op jit(solution)/shard_map/ppermute | solution.py:101
  122.3 25.8 %collective-permute-start.32 = (bf16[2,392,768]{2,1,0:T(8,128)(2,1)}, bf16[2,392,768]{2,1,0:T(8,128)(2,1)}, u32[]{:S(2)}, u32[]{:S(2)}) collective-permute-start(bf16[2,392,768]{2,1,0:T(8,128)(2,1)} %get-tuple-element.405), channel_id=1, source_target_pairs={{0,16},{1,17},{2,18},{3,19},{4,20},{5,21},{6,22},{7,23},{8,24},{9,... | collective-permute-start | bytes 3612680 | tf_op jit(solution)/shard_map/ppermute | solution.py:101
  122.7 25.4 %collective-permute-start.29 = (bf16[4,48,1536]{2,1,0:T(8,128)(2,1)}, bf16[4,48,1536]{2,1,0:T(8,128)(2,1)}, u32[]{:S(2)}, u32[]{:S(2)}) collective-permute-start(bf16[4,48,1536]{2,1,0:T(8,128)(2,1)} %get-tuple-element.402), channel_id=1, source_target_pairs={{0,2},{1,3},{2,0},{3,1},{4,6},{5,7},{6,4},{7,5},{8,10},{9,11},{10,... | collective-permute-start | bytes 1769480 | tf_op jit(solution)/shard_map/ppermute | solution.py:97
  123.8 24.3 %collective-permute-start.30 = (bf16[4,48,1536]{2,1,0:T(8,128)(2,1)}, bf16[4,48,1536]{2,1,0:T(8,128)(2,1)}, u32[]{:S(2)}, u32[]{:S(2)}) collective-permute-start(bf16[4,48,1536]{2,1,0:T(8,128)(2,1)} %get-tuple-element.403), channel_id=1, source_target_pairs={{0,2},{1,3},{2,0},{3,1},{4,6},{5,7},{6,4},{7,5},{8,10},{9,11},{10,... | collective-permute-start | bytes 1769480 | tf_op jit(solution)/shard_map/ppermute | solution.py:97
  151.2 9.9 %collective-permute-start.34 = (bf16[4,48,1536]{2,1,0:T(8,128)(2,1)S(1)}, bf16[4,48,1536]{2,1,0:T(8,128)(2,1)S(1)}, u32[]{:S(2)}, u32[]{:S(2)}) collective-permute-start(bf16[4,48,1536]{2,1,0:T(8,128)(2,1)S(1)} %add_convert_fusion.3), channel_id=1, source_target_pairs={{0,1},{1,0},{2,3},{3,2},{4,5},{5,4},{6,7},{7,6},{8,9},{9,8},{10,11... | collective-permute-start | bytes 1769480 | tf_op jit(solution)/shard_map/ppermute | solution.py:97
  161.1 7.2 %collective-permute-start.36 = (bf16[2,392,768]{2,1,0:T(8,128)(2,1)S(1)}, bf16[2,392,768]{2,1,0:T(8,128)(2,1)S(1)}, u32[]{:S(2)}, u32[]{:S(2)}) collective-permute-start(bf16[2,392,768]{2,1,0:T(8,128)(2,1)S(1)} %copy-done.68), channel_id=1, source_target_pairs={{0,16},{1,17},{2,18},{3,19},{4,20},{5,21},{6,22},{7,23},{8,24},{9,... | collective-permute-start | bytes 3612680 | tf_op jit(solution)/shard_map/ppermute | solution.py:101
  168.9 19.2 %collective-permute-start.37 = (bf16[4,48,1536]{2,1,0:T(8,128)(2,1)}, bf16[4,48,1536]{2,1,0:T(8,128)(2,1)S(1)}, u32[]{:S(2)}, u32[]{:S(2)}) collective-permute-start(bf16[4,48,1536]{2,1,0:T(8,128)(2,1)} %get-tuple-element.449), channel_id=1, source_target_pairs={{0,2},{1,3},{2,0},{3,1},{4,6},{5,7},{6,4},{7,5},{8,10},{9,11},{10,... | collective-permute-start | bytes 1769480 | tf_op jit(solution)/shard_map/ppermute | solution.py:97
  170.1 18.0 %collective-permute-start.38 = (bf16[4,48,1536]{2,1,0:T(8,128)(2,1)S(1)}, bf16[4,48,1536]{2,1,0:T(8,128)(2,1)S(1)}, u32[]{:S(2)}, u32[]{:S(2)}) collective-permute-start(bf16[4,48,1536]{2,1,0:T(8,128)(2,1)S(1)} %copy-done.70), channel_id=1, source_target_pairs={{0,2},{1,3},{2,0},{3,1},{4,6},{5,7},{6,4},{7,5},{8,10},{9,11},{10,... | collective-permute-start | bytes 1769480 | tf_op jit(solution)/shard_map/ppermute | solution.py:97
  170.9 17.2 %collective-permute-start.42 = (bf16[16,48,384]{2,1,0:T(8,128)(2,1)S(1)}, bf16[16,48,384]{2,1,0:T(8,128)(2,1)S(1)}, u32[]{:S(2)}, u32[]{:S(2)}) collective-permute-start(bf16[16,48,384]{2,1,0:T(8,128)(2,1)S(1)} %get-tuple-element.454), channel_id=1, source_target_pairs={{0,16},{1,17},{2,18},{3,19},{4,20},{5,21},{6,22},{7,23},{8,24},{9,... | collective-permute-start | bytes 1769480 | tf_op jit(solution)/shard_map/ppermute | solution.py:101
  170.9 17.1 %collective-permute-start.40 = (bf16[1,48,1536]{2,1,0:T(8,128)(2,1)S(1)}, bf16[1,48,1536]{2,1,0:T(8,128)(2,1)S(1)}, u32[]{:S(2)}, u32[]{:S(2)}) collective-permute-start(bf16[1,48,1536]{2,1,0:T(8,128)(2,1)S(1)} %get-tuple-element.452), channel_id=1, source_target_pairs={{0,8},{1,9},{2,10},{3,11},{4,12},{5,13},{6,14},{7,15},{8,0},{9,1},... | collective-permute-start | bytes 442376 | tf_op jit(solution)/shard_map/ppermute | solution.py:97
  174.2 13.9 %collective-permute-start.41 = (bf16[1,48,1536]{2,1,0:T(8,128)(2,1)S(1)}, bf16[1,48,1536]{2,1,0:T(8,128)(2,1)S(1)}, u32[]{:S(2)}, u32[]{:S(2)}) collective-permute-start(bf16[1,48,1536]{2,1,0:T(8,128)(2,1)S(1)} %get-tuple-element.453), channel_id=1, source_target_pairs={{0,12},{1,13},{2,14},{3,15},{4,8},{5,9},{6,10},{7,11},{8,4},{9,5},... | collective-permute-start | bytes 442376 | tf_op jit(solution)/shard_map/ppermute | solution.py:97
  189.1 12.5 %collective-permute-start.43 = (bf16[4,48,1536]{2,1,0:T(8,128)(2,1)S(1)}, bf16[4,48,1536]{2,1,0:T(8,128)(2,1)S(1)}, u32[]{:S(2)}, u32[]{:S(2)}) collective-permute-start(bf16[4,48,1536]{2,1,0:T(8,128)(2,1)S(1)} %add_convert_fusion.1), channel_id=1, source_target_pairs={{0,1},{1,0},{2,3},{3,2},{4,5},{5,4},{6,7},{7,6},{8,9},{9,8},{10,11... | collective-permute-start | bytes 1769480 | tf_op jit(solution)/shard_map/ppermute | solution.py:97
  202.7 17.6 %collective-permute-start.44 = (bf16[8,48,1152]{2,1,0:T(8,128)(2,1)S(1)}, bf16[8,48,1152]{2,1,0:T(8,128)(2,1)S(1)}, u32[]{:S(2)}, u32[]{:S(2)}) collective-permute-start(bf16[8,48,1152]{2,1,0:T(8,128)(2,1)S(1)} %pad_maximum_fusion), channel_id=1, source_target_pairs={{0,2},{1,3},{2,0},{3,1},{4,6},{5,7},{6,4},{7,5},{8,10},{9,11},{10,... | collective-permute-start | bytes 2654216 | tf_op jit(solution)/shard_map/ppermute | solution.py:97
  203.6 16.6 %collective-permute-start.45 = (bf16[1,48,1536]{2,1,0:T(8,128)(2,1)S(1)}, bf16[1,48,1536]{2,1,0:T(8,128)(2,1)S(1)}, u32[]{:S(2)}, u32[]{:S(2)}) collective-permute-start(bf16[1,48,1536]{2,1,0:T(8,128)(2,1)S(1)} %get-tuple-element.482), channel_id=1, source_target_pairs={{0,4},{1,5},{2,6},{3,7},{4,0},{5,1},{6,2},{7,3},{8,12},{9,13},{10,... | collective-permute-start | bytes 442376 | tf_op jit(solution)/shard_map/ppermute | solution.py:97
  203.6 16.6 %collective-permute-start.46 = (bf16[1,48,1536]{2,1,0:T(8,128)(2,1)S(1)}, bf16[1,48,1536]{2,1,0:T(8,128)(2,1)S(1)}, u32[]{:S(2)}, u32[]{:S(2)}) collective-permute-start(bf16[1,48,1536]{2,1,0:T(8,128)(2,1)S(1)} %get-tuple-element.483), channel_id=1, source_target_pairs={{0,8},{1,9},{2,10},{3,11},{4,12},{5,13},{6,14},{7,15},{8,0},{9,1},... | collective-permute-start | bytes 442376 | tf_op jit(solution)/shard_map/ppermute | solution.py:97
  205.7 14.5 %collective-permute-start.47 = (bf16[1,48,1536]{2,1,0:T(8,128)(2,1)S(1)}, bf16[1,48,1536]{2,1,0:T(8,128)(2,1)S(1)}, u32[]{:S(2)}, u32[]{:S(2)}) collective-permute-start(bf16[1,48,1536]{2,1,0:T(8,128)(2,1)S(1)} %get-tuple-element.484), channel_id=1, source_target_pairs={{0,12},{1,13},{2,14},{3,15},{4,8},{5,9},{6,10},{7,11},{8,4},{9,5},... | collective-permute-start | bytes 442376 | tf_op jit(solution)/shard_map/ppermute | solution.py:97
  220.4 10.1 %collective-permute-start.49 = (bf16[4,48,1152]{2,1,0:T(8,128)(2,1)S(1)}, bf16[4,48,1152]{2,1,0:T(8,128)(2,1)S(1)}, u32[]{:S(2)}, u32[]{:S(2)}) collective-permute-start(bf16[4,48,1152]{2,1,0:T(8,128)(2,1)S(1)} %add_convert_fusion.4), channel_id=1, source_target_pairs={{0,1},{1,0},{2,3},{3,2},{4,5},{5,4},{6,7},{7,6},{8,9},{9,8},{10,11... | collective-permute-start | bytes 1327112 | tf_op jit(solution)/shard_map/ppermute | solution.py:97
  221.3 9.2 %collective-permute-start.48 = (bf16[8,48,384]{2,1,0:T(8,128)(2,1)S(1)}, bf16[8,48,384]{2,1,0:T(8,128)(2,1)S(1)}, u32[]{:S(2)}, u32[]{:S(2)}) collective-permute-start(bf16[8,48,384]{2,1,0:T(8,128)(2,1)S(1)} %get-tuple-element.499), channel_id=1, source_target_pairs={{0,2},{1,3},{2,0},{3,1},{4,6},{5,7},{6,4},{7,5},{8,10},{9,11},{10,... | collective-permute-start | bytes 884744 | tf_op jit(solution)/shard_map/ppermute | solution.py:97
  239.5 8.0 %collective-permute-start.52 = (f32[48,3072]{1,0:T(8,128)S(1)}, f32[48,3072]{1,0:T(8,128)S(1)}, u32[]{:S(2)}, u32[]{:S(2)}) collective-permute-start(f32[48,3072]{1,0:T(8,128)S(1)} %pad_maximum_fusion.6.refs_1_), channel_id=1, source_target_pairs={{0,16},{1,17},{2,18},{3,19},{4,20},{5,21},{6,22},{7,23},{8,24},{9,... | collective-permute-start | bytes 1769480 | tf_op jit(solution)/shard_map/ppermute | solution.py:101
  239.8 9.8 %collective-permute-start.53 = (bf16[1,48,1536]{2,1,0:T(8,128)(2,1)S(1)}, bf16[1,48,1536]{2,1,0:T(8,128)(2,1)S(1)}, u32[]{:S(2)}, u32[]{:S(2)}) collective-permute-start(bf16[1,48,1536]{2,1,0:T(8,128)(2,1)S(1)} %get-tuple-element.545), channel_id=1, source_target_pairs={{0,4},{1,5},{2,6},{3,7},{4,0},{5,1},{6,2},{7,3},{8,12},{9,13},{10,... | collective-permute-start | bytes 442376 | tf_op jit(solution)/shard_map/ppermute | solution.py:97
  239.9 14.0 %collective-permute-start.54 = (bf16[1,48,1536]{2,1,0:T(8,128)(2,1)S(1)}, bf16[1,48,1536]{2,1,0:T(8,128)(2,1)S(1)}, u32[]{:S(2)}, u32[]{:S(2)}) collective-permute-start(bf16[1,48,1536]{2,1,0:T(8,128)(2,1)S(1)} %get-tuple-element.546), channel_id=1, source_target_pairs={{0,8},{1,9},{2,10},{3,11},{4,12},{5,13},{6,14},{7,15},{8,0},{9,1},... | collective-permute-start | bytes 442376 | tf_op jit(solution)/shard_map/ppermute | solution.py:97
  241.8 12.1 %collective-permute-start.55 = (bf16[1,48,1536]{2,1,0:T(8,128)(2,1)S(1)}, bf16[1,48,1536]{2,1,0:T(8,128)(2,1)S(1)}, u32[]{:S(2)}, u32[]{:S(2)}) collective-permute-start(bf16[1,48,1536]{2,1,0:T(8,128)(2,1)S(1)} %pad_maximum_fusion.10), channel_id=1, source_target_pairs={{0,12},{1,13},{2,14},{3,15},{4,8},{5,9},{6,10},{7,11},{8,4},{9,5},... | collective-permute-start | bytes 442376 | tf_op jit(solution)/shard_map/ppermute | solution.py:97
  261.2 11.7 %collective-permute-start.63 = (f32[48,1536]{1,0:T(8,128)S(1)}, f32[48,1536]{1,0:T(8,128)S(1)}, u32[]{:S(2)}, u32[]{:S(2)}) collective-permute-start(f32[48,1536]{1,0:T(8,128)S(1)} %get-tuple-element.557.refs_2_), channel_id=1, source_target_pairs={{0,16},{1,17},{2,18},{3,19},{4,20},{5,21},{6,22},{7,23},{8,24},{9,... | collective-permute-start | bytes 884744 | tf_op jit(solution)/shard_map/ppermute | solution.py:101
  (89 other events, 756.6 us)

commit v3 on v2

--- a/solution.py
+++ b/solution.py
@@ -105,7 +105,7 @@
 
     def sum_all(self, x):
         x = x + self.cross(x)
-        for step in (1, 4):
+        for step in (4, 1):
             one, two, three = [self.flip(x, step * p) for p in (1, 2, 3)]
             x = (x + one) + (two + three)
         return x

time: 282 us -> 282 us (level)
  transfers between devices with their start and end apart: 64 -> 64, of which waited for: 17 -> 18; matrix products, arithmetic and copies ran while one was open for 4% -> 4% of each run, Pallas kernels for 50% -> 50%
where the time goes in v3:
time: 282 us; the launch traced here: 278 us
  Pallas kernels  144 us (51%)
  starting transfers between devices  66.8 us (24%)
  waiting for transfers between devices  36.3 us (13%)
  local copies, waits for them, and re-layouts  15.3 us (5%)
  other arithmetic  13.2 us (5%)
    pallas_call x19, Pallas kernels, apply(): token_out, *outs = run(token, *args)  144 us
    ppermute x46, starting transfers between devices, flip(): return lax.ppermute(x, AXES, pairs)  64.2 us
    ppermute x46, waiting for transfers between devices, flip(): return lax.ppermute(x, AXES, pairs)  28.6 us
    unnamed x149, local copies, waits for them, and re-layouts  8.53 us
    ppermute x18, waiting for transfers between devices, cross(): return lax.ppermute(x, AXES, pairs)  7.69 us
  transfers between devices with their start and end apart: 64, of which 18 were waited for; matrix products, arithmetic and copies ran while one was open for 4% of the time, Pallas kernels for 50%

profile of v3, /device:TPU:0, one launch (start us, length us, event | category | flops | bytes accessed | tf_op | source)
XLA Modules:
  0.0 278.3 jit_solution(7037509994696895717)
XLA Ops:
  2.7 3.1 %collective-permute-start.2 = (bf16[1,48,1664]{2,1,0:T(8,128)(2,1)S(1)}, bf16[1,48,1664]{2,1,0:T(8,128)(2,1)}, u32[]{:S(2)}, u32[]{:S(2)}) collective-permute-start(bf16[1,48,1664]{2,1,0:T(8,128)(2,1)S(1)} %fusion.6), channel_id=1, source_target_pairs={{0,4},{1,5},{2,6},{3,7},{4,0},{5,1},{6,2},{7,3},{8,12},{9,13},{10,... | collective-permute-start | bytes 479240 | tf_op jit(solution)/shard_map/ppermute | solution.py:97
  5.8 2.6 collective-permute-start.3
  11.3 4.9 %embed_rows.2 = (f32[8,128]{1,0:T(8,128)S(1)}, f32[2,392,768]{2,1,0:T(8,128)S(1)}) custom-call(f32[8,128]{1,0:T(8,128)S(1)} %broadcast_in_dim.21.token_ref, f32[8,768]{1,0:T(8,128)S(1)} %copy-done.21, bf16[2,392,768]{2,1,0:T(8,128)(2,1)} %refs_1_.1, f32[2,392,1]{2,1,0:T(8,128)S(1)} %copy.67.refs_2_), custom_call_target="tpu_custom_call", output_to_operand_aliasing={{0}: (0, {})} | custom-call | flops 4000000000 | bytes 12000000 | tf_op jit(solution)/shard_map/embed_rows/pallas_call | solution.py:57
  18.6 2.1 collective-permute-done.3
  21.9 1.6 collective-permute-start.5
  23.4 2.6 collective-permute-start.6
  27.0 1.5 collective-permute-start.8
  28.7 4.7 %embed_rows.3 = (f32[8,128]{1,0:T(8,128)S(1)}, f32[2,392,768]{2,1,0:T(8,128)S(1)}) custom-call(f32[8,128]{1,0:T(8,128)S(1)} %get-tuple-element.312.token_ref, f32[8,768]{1,0:T(8,128)S(1)} %copy-done.21, bf16[2,392,768]{2,1,0:T(8,128)(2,1)} %collective-permute-done.refs_1_, f32[2,392,1]{2,1,0:T(8,128)S(1)} %copy.70.refs_2_), custom_call_target="tpu_custom_call", output_to_operand_aliasing={{0}: (0, {})} | custom-call | flops 4000000000 | bytes 12000000 | tf_op jit(solution)/shard_map/embed_rows/pallas_call | solution.py:57
  36.0 1.6 collective-permute-start.9
  38.0 1.5 collective-permute-start.11
  39.4 1.5 collective-permute-start.12
  40.9 1.5 collective-permute-start.13
  42.7 5.4 %collective-permute-done.12 = bf16[1,48,768]{2,1,0:T(8,128)(2,1)S(1)} collective-permute-done((bf16[1,48,768]{2,1,0:T(8,128)(2,1)S(1)}, bf16[1,48,768]{2,1,0:T(8,128)(2,1)S(1)}, u32[]{:S(2)}, u32[]{:S(2)}) %collective-permute-start.12) | collective-permute-done | bytes 73760 | tf_op jit(solution)/shard_map/ppermute | solution.py:97
  49.6 1.5 collective-permute-start.17
  51.1 1.5 collective-permute-start.18
  54.7 14.1 %attend_forward.2 = (f32[8,128]{1,0:T(8,128)S(1)}, f32[16,768]{1,0:T(8,128)S(1)}, bf16[4,392,768]{2,1,0:T(8,128)(2,1)S(1)}, bf16[4,392,768]{2,1,0:T(8,128)(2,1)}...) custom-call(f32[8,128]{1,0:T(8,128)S(1)} %get-tuple-element.337.toke, ...), custom_call_target="tpu_custom_call", output_to_operand_aliasing={{0}: (0, {})} | custom-call | flops 8000000000 | bytes 24000000 | tf_op jit(solution)/shard_map/attend_forward/pallas_call | solution.py:57
  70.3 6.8 %attend_forward.3 = (f32[8,128]{1,0:T(8,128)S(1)}, bf16[4,392,384]{2,1,0:T(8,128)(2,1)S(1)}, f32[4,2,392]{2,1,0:T(2,128)S(1)}, bf16[2,392,128]{2,1,0:T(8,128)(2,1)S(1)}, bf16[2,392,128]{2,1,0:T(8,128)(2,1)S(1)}) custom-call(f32[8,128]{1,0:T(8,128)S(1)} %get-tuple-element.351.token_ref, ...), custom_call_target="tpu_custom_call", output_to_operand_aliasing={{0}: (0, {})} | custom-call | flops 8000000000 | bytes 24000000 | tf_op jit(solution)/shard_map/attend_forward/pallas_call | solution.py:57
  80.4 4.3 %project_norm.1 = (f32[8,128]{1,0:T(8,128)S(1)}, f32[2,392,768]{2,1,0:T(8,128)S(1)}, bf16[2,392,768]{2,1,0:T(8,128)(2,1)S(1)}) custom-call(f32[8,128]{1,0:T(8,128)S(1)} %get-tuple-element.366.token_ref, s32[33]{0:T(128)S(1)} %pad_add_fusion.3.refs_0_, ...), custom_call_target="tpu_custom_call", output_to_operand_aliasing={{0}: (0, {})} | custom-call | flops 6000000000 | bytes 18000000 | tf_op jit(solution)/shard_map/project_norm/pallas_call | solution.py:57
  84.7 4.4 %collective-permute-done.24.refs_10_ = bf16[4,48,1536]{2,1,0:T(8,128)(2,1)S(1)} collective-permute-done((bf16[4,48,1536]{2,1,0:T(8,128)(2,1)}, bf16[4,48,1536]{2,1,0:T(8,128)(2,1)S(1)}, u32[]{:S(2)}, u32[]{:S(2)}) %collective-permute-start.24) | collective-permute-done | bytes 589856 | tf_op jit(solution)/shard_map/ppermute | solution.py:97
  89.1 2.9 %collective-permute-done.25.refs_4_ = bf16[2,392,768]{2,1,0:T(8,128)(2,1)S(1)} collective-permute-done((bf16[2,392,768]{2,1,0:T(8,128)(2,1)S(1)}, bf16[2,392,768]{2,1,0:T(8,128)(2,1)S(1)}, u32[]{:S(2)}, u32[]{:S(2)}) %collective-permute-start.25) | collective-permute-done | bytes 1204256 | tf_op jit(solution)/shard_map/ppermute | solution.py:101
  95.0 1.5 collective-permute-start.28
  96.5 22.9 %mlp_both.2 = (f32[8,128]{1,0:T(8,128)}, bf16[2,392,768]{2,1,0:T(8,128)(2,1)}, bf16[2,392,768]{2,1,0:T(8,128)(2,1)}, bf16[2,392,768]{2,1,0:T(8,128)(2,1)}, bf16[...) custom-call(f32[8,128]{1,0:T(8,128)} %copy-done.5, ...), custom_call_target="tpu_custom_call", output_to_operand_aliasing={{0}: (0, {})} | custom-call | flops 23000000512 | bytes 69000000 | tf_op jit(solution)/shard_map/mlp_both/pallas_call | solution.py:57
  119.4 2.8 collective-permute-done.28.refs_10_
  124.7 23.3 %mlp_both.3 = (f32[8,128]{1,0:T(8,128)}, bf16[2,392,768]{2,1,0:T(8,128)(2,1)}, bf16[2,392,768]{2,1,0:T(8,128)(2,1)}, bf16[2,392,768]{2,1,0:T(8,128)(2,1)}, bf16[...) custom-call(f32[8,128]{1,0:T(8,128)} %get-tuple-element.397.token_re, ...), custom_call_target="tpu_custom_call", output_to_operand_aliasing={{0}: (0, {})} | custom-call | flops 23000000512 | bytes 69000000 | tf_op jit(solution)/shard_map/mlp_both/pallas_call | solution.py:57
  148.2 1.5 add_convert_fusion.3
  149.7 1.6 collective-permute-done.33.refs_8_
  153.8 6.6 %norm_two_back.1 = (f32[8,128]{1,0:T(8,128)S(1)}, bf16[2,392,384]{2,1,0:T(8,128)(2,1)S(1)}, bf16[2,392,384]{2,1,0:T(8,128)(2,1)S(1)}, bf16[2,392,768]{2,1,0:T(8,...) custom-call(f32[8,128]{1,0:T(8,128)S(1)} %copy-done.6, ...), custom_call_target="tpu_custom_call", output_to_operand_aliasing={{0}: (0, {})} | custom-call | flops 7000000000 | bytes 21000000 | tf_op jit(solution)/shard_map/norm_two_back/pallas_call | solution.py:57
  161.7 5.1 %out_weight_grad.1 = (f32[8,128]{1,0:T(8,128)S(1)}, bf16[16,48,384]{2,1,0:T(8,128)(2,1)S(1)}, bf16[16,48,384]{2,1,0:T(8,128)(2,1)S(1)}) custom-call(f32[8,128]{1,0:T(8,128)S(1)} %get-tuple-element.432.token_ref, s32[33]{0:T(128)S(1)} %pad_add_fusion.3.refs_0_, bf16[2,392,768]{2,1,0:T(8,128)(2,1)S(1)} %get-tuple-element.433.refs_1_, ...), custom_call_target="tpu_custom_call", output_to_operand_aliasing={{0}: (0, {})} | custom-call | flops 5000000000 | bytes 15000000 | tf_op jit(solution)/shard_map/out_weight_grad/pallas_call | solution.py:57
  166.8 1.5 add_convert_fusion.9
  170.9 2.5 collective-permute-start.40
  174.2 2.5 collective-permute-start.41
  176.7 11.3 %attend_back.3 = (f32[8,128]{1,0:T(8,128)S(1)}, bf16[4,392,384]{2,1,0:T(8,128)(2,1)S(1)}, f32[1,384]{1,0:T(1,128)S(1)}, bf16[8,48,384]{2,1,0:T(8,128)(2,1)S(1)}, bf16[8,48,384]{2,1,0:T(8,128)(2,1)S(1)}) custom-call(f32[8,128]{1,0:T(8,128)S(1)} %get-tuple-element.443.token_ref, s32[17]{0:T(128)S(1)} %copy-done.23, ...), custom_call_target="tpu_custom_call", output_to_operand_aliasing={{0}: (0, {})} | custom-call | flops 12000000000 | bytes 36000000 | tf_op jit(solution)/shard_map/attend_back/pallas_call | solution.py:57
  190.3 11.1 %attend_back.4 = (f32[8,128]{1,0:T(8,128)S(1)}, bf16[4,392,384]{2,1,0:T(8,128)(2,1)S(1)}, f32[1,384]{1,0:T(1,128)S(1)}, bf16[8,48,384]{2,1,0:T(8,128)(2,1)S(1)}, bf16[8,48,384]{2,1,0:T(8,128)(2,1)S(1)}) custom-call(f32[8,128]{1,0:T(8,128)S(1)} %get-tuple-element.464.token_ref, s32[17]{0:T(128)S(1)} %copy-done.23, ...), custom_call_target="tpu_custom_call", output_to_operand_aliasing={{0}: (0, {})} | custom-call | flops 12000000000 | bytes 36000000 | tf_op jit(solution)/shard_map/attend_back/pallas_call | solution.py:57
  203.6 2.1 collective-permute-start.46
  205.7 2.3 collective-permute-start.47
  208.0 11.1 %attend_back.5 = (f32[8,128]{1,0:T(8,128)S(1)}, bf16[4,392,384]{2,1,0:T(8,128)(2,1)S(1)}, f32[1,384]{1,0:T(1,128)S(1)}, bf16[8,48,384]{2,1,0:T(8,128)(2,1)S(1)}, bf16[8,48,384]{2,1,0:T(8,128)(2,1)S(1)}) custom-call(f32[8,128]{1,0:T(8,128)S(1)} %get-tuple-element.477.token_ref, s32[17]{0:T(128)S(1)} %copy-done.23, ...), custom_call_target="tpu_custom_call", output_to_operand_aliasing={{0}: (0, {})} | custom-call | flops 12000000000 | bytes 36000000 | tf_op jit(solution)/shard_map/attend_back/pallas_call | solution.py:57
  223.6 6.9 %attn_in_grad.1 = (f32[8,128]{1,0:T(8,128)S(1)}, f32[2,392,768]{2,1,0:T(8,128)S(1)}, bf16[2,392,768]{2,1,0:T(8,128)(2,1)S(1)}) custom-call(f32[8,128]{1,0:T(8,128)S(1)} %get-tuple-element.494.token_ref, s32[17]{0:T(128)S(1)} %copy-done.23, bf16[4,392,384]{2,1,0:T(8,128)(2,1)S(1)} %copy-done.37, ...), custom_call_target="tpu_custom_call", output_to_operand_aliasing={{0}: (0, {})} | custom-call | flops 7000000000 | bytes 21000000 | tf_op jit(solution)/shard_map/attn_in_grad/pallas_call | solution.py:57
  232.1 1.4 collective-permute-done.50.refs_4_
  233.5 3.2 %norm_one_back.1 = (f32[8,128]{1,0:T(8,128)S(1)}, f32[2,392,768]{2,1,0:T(8,128)}, f32[8,768]{1,0:T(8,128)S(1)}) custom-call(f32[8,128]{1,0:T(8,128)S(1)} %get-tuple-element.506.token_ref, f32[16,768]{1,0:T(8,128)S(1)} %copy-done.8, f32[2,392,768]{2,1,0:T(8,128)S(1)} %copy-done.28, f32[2,392,768]{2,1,0:T(8,128)S(1)} %copy-done.30, ...), custom_call_target="tpu_custom_call", output_to_operand_aliasing={{0}: (0, {})} | custom-call | flops 4000000000 | bytes 12000000 | tf_op jit(solution)/shard_map/norm_one_back/pallas_call | solution.py:57
  239.9 1.9 collective-permute-start.54
  241.8 2.5 collective-permute-start.55
  244.3 3.2 %add_convert_fusion = bf16[2,392,768]{2,1,0:T(8,128)(2,1)} fusion(bf16[2,392,768]{2,1,0:T(8,128)(2,1)S(1)} %copy-done.53, bf16[2,392,768]{2,1,0:T(8,128)(2,1)} %collective-permute-done.32, bf16[2,392,768]{2,1,0:T(8,128)(2,1)S(1)} %copy-done.51, bf16[2,392,768]{2,1,0:T(8,128)(2,1)S(1)} %copy-done.50, f32[2,392,768]{2,1,0:T(8,128)S(1)} %get-tuple-element.537.refs_3_, ...), kind=kLoop, calls=%fused_computation | loop fusion | flops 6021120 | bytes 8432640 | tf_op jit(solution)/shard_map/convert_element_type | solution.py:1436
  249.6 4.3 %collective-permute-done.54.refs_8_ = bf16[1,48,1536]{2,1,0:T(8,128)(2,1)S(1)} collective-permute-done((bf16[1,48,1536]{2,1,0:T(8,128)(2,1)S(1)}, bf16[1,48,1536]{2,1,0:T(8,128)(2,1)S(1)}, u32[]{:S(2)}, u32[]{:S(2)}) %collective-permute-start.54) | collective-permute-done | bytes 147488 | tf_op jit(solution)/shard_map/ppermute | solution.py:97
  260.9 1.9 collective-permute-done.59
  262.8 3.2 %collective-permute-start.60 = (f32[16,768]{1,0:T(8,128)S(1)}, f32[16,768]{1,0:T(8,128)S(1)}, u32[]{:S(2)}, u32[]{:S(2)}) collective-permute-start(f32[16,768]{1,0:T(8,128)S(1)} %add_add_fusion.1), channel_id=1, source_target_pairs={{0,4},{1,5},{2,6},{3,7},{4,0},{5,1},{6,2},{7,3},{8,12},{9,13},{10,... | collective-permute-start | bytes 147464 | tf_op jit(solution)/shard_map/ppermute | solution.py:97
  266.2 2.3 collective-permute-start.62
  268.5 2.6 collective-permute-done.61
  272.3 5.3 %update_all.1 = (f32[8,128]{1,0:T(8,128)S(1)}, f32[48,2304]{1,0:T(8,128)}, f32[48,768]{1,0:T(8,128)}, f32[48,3072]{1,0:T(8,128)}, f32[192,768]{1,0:T(8,128)}, /*...) custom-call(f32[8,128]{1,0:T(8,128)S(1)} %get-tuple-element.555.toke, ...), custom_call_target="tpu_custom_call", output_to_operand_aliasing={{0}: (0, {})} | custom-call | flops 6000000000 | bytes 18000000 | tf_op jit(solution)/shard_map/update_all/pallas_call | solution.py:57
  (316 shorter events, 57.8 us)
Async XLA Ops:
  2.7 15.8 %collective-permute-start.2 = (bf16[1,48,1664]{2,1,0:T(8,128)(2,1)S(1)}, bf16[1,48,1664]{2,1,0:T(8,128)(2,1)}, u32[]{:S(2)}, u32[]{:S(2)}) collective-permute-start(bf16[1,48,1664]{2,1,0:T(8,128)(2,1)S(1)} %fusion.6), channel_id=1, source_target_pairs={{0,4},{1,5},{2,6},{3,7},{4,0},{5,1},{6,2},{7,3},{8,12},{9,13},{10,... | collective-permute-start | bytes 479240 | tf_op jit(solution)/shard_map/ppermute | solution.py:97
  5.8 14.9 %collective-permute-start.3 = (bf16[1,48,1664]{2,1,0:T(8,128)(2,1)S(1)}, bf16[1,48,1664]{2,1,0:T(8,128)(2,1)}, u32[]{:S(2)}, u32[]{:S(2)}) collective-permute-start(bf16[1,48,1664]{2,1,0:T(8,128)(2,1)S(1)} %fusion.6), channel_id=1, source_target_pairs={{0,8},{1,9},{2,10},{3,11},{4,12},{5,13},{6,14},{7,15},{8,0},{9,1},... | collective-permute-start | bytes 479240 | tf_op jit(solution)/shard_map/ppermute | solution.py:97
  8.4 12.3 %collective-permute-start.4 = (bf16[1,48,1664]{2,1,0:T(8,128)(2,1)S(1)}, bf16[1,48,1664]{2,1,0:T(8,128)(2,1)}, u32[]{:S(2)}, u32[]{:S(2)}) collective-permute-start(bf16[1,48,1664]{2,1,0:T(8,128)(2,1)S(1)} %fusion.6), channel_id=1, source_target_pairs={{0,12},{1,13},{2,14},{3,15},{4,8},{5,9},{6,10},{7,11},{8,4},{9,5},... | collective-permute-start | bytes 479240 | tf_op jit(solution)/shard_map/ppermute | solution.py:97
  8.6 10.0 %collective-permute-start.1 = (s32[2,393]{1,0:T(2,128)S(1)}, s32[2,393]{1,0:T(2,128)S(1)}, u32[]{:S(2)}, u32[]{:S(2)}) collective-permute-start(s32[2,393]{1,0:T(2,128)S(1)} %pad_add_fusion), channel_id=1, source_target_pairs={{0,16},{1,17},{2,18},{3,19},{4,20},{5,21},{6,22},{7,23},{8,24},{9,... | collective-permute-start | bytes 9440 | tf_op jit(solution)/shard_map/ppermute | solution.py:101
  8.6 12.1 %collective-permute-start = (bf16[2,392,768]{2,1,0:T(8,128)(2,1)}, bf16[2,392,768]{2,1,0:T(8,128)(2,1)}, u32[]{:S(2)}, u32[]{:S(2)}) collective-permute-start(bf16[2,392,768]{2,1,0:T(8,128)(2,1)} %refs_1_.1), channel_id=1, source_target_pairs={{0,16},{1,17},{2,18},{3,19},{4,20},{5,21},{6,22},{7,23},{8,24},{9,... | collective-permute-start | bytes 3612680 | tf_op jit(solution)/shard_map/ppermute | solution.py:101
  21.9 11.7 %collective-permute-start.5 = (bf16[4,48,1664]{2,1,0:T(8,128)(2,1)S(1)}, bf16[4,48,1664]{2,1,0:T(8,128)(2,1)}, u32[]{:S(2)}, u32[]{:S(2)}) collective-permute-start(bf16[4,48,1664]{2,1,0:T(8,128)(2,1)S(1)} %pad_maximum_fusion.3), channel_id=1, source_target_pairs={{0,1},{1,0},{2,3},{3,2},{4,5},{5,4},{6,7},{7,6},{8,9},{9,8},{10,11... | collective-permute-start | bytes 1916936 | tf_op jit(solution)/shard_map/ppermute | solution.py:97
  23.4 10.1 %collective-permute-start.6 = (bf16[1,48,768]{2,1,0:T(8,128)(2,1)S(1)}, bf16[1,48,768]{2,1,0:T(8,128)(2,1)S(1)}, u32[]{:S(2)}, u32[]{:S(2)}) collective-permute-start(bf16[1,48,768]{2,1,0:T(8,128)(2,1)S(1)} %reshape_squeeze.6), channel_id=1, source_target_pairs={{0,4},{1,5},{2,6},{3,7},{4,0},{5,1},{6,2},{7,3},{8,12},{9,13},{10,... | collective-permute-start | bytes 221192 | tf_op jit(solution)/shard_map/ppermute | solution.py:97
  26.0 7.5 %collective-permute-start.7 = (bf16[1,48,768]{2,1,0:T(8,128)(2,1)S(1)}, bf16[1,48,768]{2,1,0:T(8,128)(2,1)S(1)}, u32[]{:S(2)}, u32[]{:S(2)}) collective-permute-start(bf16[1,48,768]{2,1,0:T(8,128)(2,1)S(1)} %reshape_squeeze.6), channel_id=1, source_target_pairs={{0,8},{1,9},{2,10},{3,11},{4,12},{5,13},{6,14},{7,15},{8,0},{9,1},... | collective-permute-start | bytes 221192 | tf_op jit(solution)/shard_map/ppermute | solution.py:97
  35.9 12.2 %collective-permute-start.10 = (bf16[2,392,768]{2,1,0:T(8,128)(2,1)}, bf16[2,392,768]{2,1,0:T(8,128)(2,1)}, u32[]{:S(2)}, u32[]{:S(2)}) collective-permute-start(bf16[2,392,768]{2,1,0:T(8,128)(2,1)} %refs_4_), channel_id=1, source_target_pairs={{0,16},{1,17},{2,18},{3,19},{4,20},{5,21},{6,22},{7,23},{8,24},{9,... | collective-permute-start | bytes 3612680 | tf_op jit(solution)/shard_map/ppermute | solution.py:101
  36.0 12.1 %collective-permute-start.9 = (bf16[8,48,896]{2,1,0:T(8,128)(2,1)S(1)}, bf16[8,48,896]{2,1,0:T(8,128)(2,1)}, u32[]{:S(2)}, u32[]{:S(2)}) collective-permute-start(bf16[8,48,896]{2,1,0:T(8,128)(2,1)S(1)} %pad_maximum_fusion.2.refs_5_.refs_4_), channel_id=1, source_target_pairs={{0,2},{1,3},{2,0},{3,1},{4,6},{5,7},{6,4},{7,5},{8,10},{9,11},{10,... | collective-permute-start | bytes 2064392 | tf_op jit(solution)/shard_map/ppermute | solution.py:97
  39.4 8.6 %collective-permute-start.12 = (bf16[1,48,768]{2,1,0:T(8,128)(2,1)S(1)}, bf16[1,48,768]{2,1,0:T(8,128)(2,1)S(1)}, u32[]{:S(2)}, u32[]{:S(2)}) collective-permute-start(bf16[1,48,768]{2,1,0:T(8,128)(2,1)S(1)} %get-tuple-element.327), channel_id=1, source_target_pairs={{0,8},{1,9},{2,10},{3,11},{4,12},{5,13},{6,14},{7,15},{8,0},{9,1},... | collective-permute-start | bytes 221192 | tf_op jit(solution)/shard_map/ppermute | solution.py:97
  40.9 7.2 %collective-permute-start.13 = (bf16[1,48,768]{2,1,0:T(8,128)(2,1)S(1)}, bf16[1,48,768]{2,1,0:T(8,128)(2,1)S(1)}, u32[]{:S(2)}, u32[]{:S(2)}) collective-permute-start(bf16[1,48,768]{2,1,0:T(8,128)(2,1)S(1)} %get-tuple-element.327), channel_id=1, source_target_pairs={{0,12},{1,13},{2,14},{3,15},{4,8},{5,9},{6,10},{7,11},{8,4},{9,5},... | collective-permute-start | bytes 221192 | tf_op jit(solution)/shard_map/ppermute | solution.py:97
  48.2 20.6 %collective-permute-start.16 = (bf16[1,48,1536]{2,1,0:T(8,128)(2,1)S(1)}, bf16[1,48,1536]{2,1,0:T(8,128)(2,1)S(1)}, u32[]{:S(2)}, u32[]{:S(2)}) collective-permute-start(bf16[1,48,1536]{2,1,0:T(8,128)(2,1)S(1)} %copy-done.58), channel_id=1, source_target_pairs={{0,4},{1,5},{2,6},{3,7},{4,0},{5,1},{6,2},{7,3},{8,12},{9,13},{10,... | collective-permute-start | bytes 442376 | tf_op jit(solution)/shard_map/ppermute | solution.py:97
  49.6 19.3 %collective-permute-start.17 = (bf16[1,48,1536]{2,1,0:T(8,128)(2,1)S(1)}, bf16[1,48,1536]{2,1,0:T(8,128)(2,1)S(1)}, u32[]{:S(2)}, u32[]{:S(2)}) collective-permute-start(bf16[1,48,1536]{2,1,0:T(8,128)(2,1)S(1)} %copy-done.58), channel_id=1, source_target_pairs={{0,8},{1,9},{2,10},{3,11},{4,12},{5,13},{6,14},{7,15},{8,0},{9,1},... | collective-permute-start | bytes 442376 | tf_op jit(solution)/shard_map/ppermute | solution.py:97
  51.1 17.8 %collective-permute-start.18 = (bf16[1,48,1536]{2,1,0:T(8,128)(2,1)S(1)}, bf16[1,48,1536]{2,1,0:T(8,128)(2,1)S(1)}, u32[]{:S(2)}, u32[]{:S(2)}) collective-permute-start(bf16[1,48,1536]{2,1,0:T(8,128)(2,1)S(1)} %copy-done.58), channel_id=1, source_target_pairs={{0,12},{1,13},{2,14},{3,15},{4,8},{5,9},{6,10},{7,11},{8,4},{9,5},... | collective-permute-start | bytes 442376 | tf_op jit(solution)/shard_map/ppermute | solution.py:97
  52.6 16.3 %collective-permute-start.14 = (bf16[4,48,1536]{2,1,0:T(8,128)(2,1)S(1)}, bf16[4,48,1536]{2,1,0:T(8,128)(2,1)}, u32[]{:S(2)}, u32[]{:S(2)}) collective-permute-start(bf16[4,48,1536]{2,1,0:T(8,128)(2,1)S(1)} %maximum_maximum_fusion.refs_7_), channel_id=1, source_target_pairs={{0,1},{1,0},{2,3},{3,2},{4,5},{5,4},{6,7},{7,6},{8,9},{9,8},{10,11... | collective-permute-start | bytes 1769480 | tf_op jit(solution)/shard_map/ppermute | solution.py:97
  53.4 15.5 %collective-permute-start.15 = (bf16[8,48,768]{2,1,0:T(8,128)(2,1)S(1)}, bf16[8,48,768]{2,1,0:T(8,128)(2,1)S(1)}, u32[]{:S(2)}, u32[]{:S(2)}) collective-permute-start(bf16[8,48,768]{2,1,0:T(8,128)(2,1)S(1)} %pad_maximum_fusion.4.refs_5_.refs_7_.refs_9_.refs_6_), channel_id=1, source_target_pairs={{0,2},{1,3},{2,0},{3,1},{4,6},{5,7},{6,4},{7,5},{8,10},{9,11},{10,... | collective-permute-start | bytes 1769480 | tf_op jit(solution)/shard_map/ppermute | solution.py:97
  68.8 9.3 %collective-permute-start.21 = (bf16[8,48,768]{2,1,0:T(8,128)(2,1)S(1)}, bf16[8,48,768]{2,1,0:T(8,128)(2,1)S(1)}, u32[]{:S(2)}, u32[]{:S(2)}) collective-permute-start(bf16[8,48,768]{2,1,0:T(8,128)(2,1)S(1)} %pad_maximum_fusion.4.refs_5_.refs_7_.refs_9_.refs_6_), channel_id=1, source_target_pairs={{0,16},{1,17},{2,18},{3,19},{4,20},{5,21},{6,22},{7,23},{8,24},{9,... | collective-permute-start | bytes 1769480 | tf_op jit(solution)/shard_map/ppermute | solution.py:101
  69.0 9.9 %collective-permute-start.19 = (bf16[4,48,1536]{2,1,0:T(8,128)(2,1)S(1)}, bf16[4,48,1536]{2,1,0:T(8,128)(2,1)S(1)}, u32[]{:S(2)}, u32[]{:S(2)}) collective-permute-start(bf16[4,48,1536]{2,1,0:T(8,128)(2,1)S(1)} %maximum_maximum_fusion.refs_7_), channel_id=1, source_target_pairs={{0,2},{1,3},{2,0},{3,1},{4,6},{5,7},{6,4},{7,5},{8,10},{9,11},{10,... | collective-permute-start | bytes 1769480 | tf_op jit(solution)/shard_map/ppermute | solution.py:97
  69.8 9.1 %collective-permute-start.22 = (bf16[8,48,768]{2,1,0:T(8,128)(2,1)S(1)}, bf16[8,48,768]{2,1,0:T(8,128)(2,1)S(1)}, u32[]{:S(2)}, u32[]{:S(2)}) collective-permute-start(bf16[8,48,768]{2,1,0:T(8,128)(2,1)S(1)} %collective-permute-done.15.refs_6_.refs_8_.refs_10_.refs_7_), channel_id=1, source_target_pairs={{0,16},{1,17},{2,18},{3,19},{4,20},{5,21},{6,22},{7,23},{8,24},{9,... | collective-permute-start | bytes 1769480 | tf_op jit(solution)/shard_map/ppermute | solution.py:101
  70.2 8.0 %collective-permute-start.20 = (bf16[2,392,256]{2,1,0:T(8,128)(2,1)S(1)}, bf16[2,392,256]{2,1,0:T(8,128)(2,1)S(1)}, u32[]{:S(2)}, u32[]{:S(2)}) collective-permute-start(bf16[2,392,256]{2,1,0:T(8,128)(2,1)S(1)} %get-tuple-element.361), channel_id=1, source_target_pairs={{0,16},{1,17},{2,18},{3,19},{4,20},{5,21},{6,22},{7,23},{8,24},{9,... | collective-permute-start | bytes 1204232 | tf_op jit(solution)/shard_map/ppermute | solution.py:101
  78.9 10.2 %collective-permute-start.24 = (bf16[4,48,1536]{2,1,0:T(8,128)(2,1)}, bf16[4,48,1536]{2,1,0:T(8,128)(2,1)S(1)}, u32[]{:S(2)}, u32[]{:S(2)}) collective-permute-start(bf16[4,48,1536]{2,1,0:T(8,128)(2,1)} %collective-permute-done.14.refs_8_), channel_id=1, source_target_pairs={{0,2},{1,3},{2,0},{3,1},{4,6},{5,7},{6,4},{7,5},{8,10},{9,11},{10,... | collective-permute-start | bytes 1769480 | tf_op jit(solution)/shard_map/ppermute | solution.py:97
  93.0 26.4 %collective-permute-start.26 = (bf16[4,48,1536]{2,1,0:T(8,128)(2,1)}, bf16[4,48,1536]{2,1,0:T(8,128)(2,1)}, u32[]{:S(2)}, u32[]{:S(2)}) collective-permute-start(bf16[4,48,1536]{2,1,0:T(8,128)(2,1)} %pad_maximum_fusion.5.refs_7_), channel_id=1, source_target_pairs={{0,1},{1,0},{2,3},{3,2},{4,5},{5,4},{6,7},{7,6},{8,9},{9,8},{10,11... | collective-permute-start | bytes 1769480 | tf_op jit(solution)/shard_map/ppermute | solution.py:97
  94.0 25.4 %collective-permute-start.27 = (bf16[4,48,1536]{2,1,0:T(8,128)(2,1)}, bf16[4,48,1536]{2,1,0:T(8,128)(2,1)}, u32[]{:S(2)}, u32[]{:S(2)}) collective-permute-start(bf16[4,48,1536]{2,1,0:T(8,128)(2,1)} %pad_maximum_fusion.5.refs_7_), channel_id=1, source_target_pairs={{0,2},{1,3},{2,0},{3,1},{4,6},{5,7},{6,4},{7,5},{8,10},{9,11},{10,... | collective-permute-start | bytes 1769480 | tf_op jit(solution)/shard_map/ppermute | solution.py:97
  95.0 27.1 %collective-permute-start.28 = (bf16[4,48,1536]{2,1,0:T(8,128)(2,1)}, bf16[4,48,1536]{2,1,0:T(8,128)(2,1)}, u32[]{:S(2)}, u32[]{:S(2)}) collective-permute-start(bf16[4,48,1536]{2,1,0:T(8,128)(2,1)} %pad_maximum_fusion.5.refs_7_), channel_id=1, source_target_pairs={{0,3},{1,2},{2,1},{3,0},{4,7},{5,6},{6,5},{7,4},{8,11},{9,10},{10,... | collective-permute-start | bytes 1769480 | tf_op jit(solution)/shard_map/ppermute | solution.py:97
  122.2 25.9 %collective-permute-start.31 = (bf16[2,392,768]{2,1,0:T(8,128)(2,1)}, bf16[2,392,768]{2,1,0:T(8,128)(2,1)}, u32[]{:S(2)}, u32[]{:S(2)}) collective-permute-start(bf16[2,392,768]{2,1,0:T(8,128)(2,1)} %get-tuple-element.404), channel_id=1, source_target_pairs={{0,16},{1,17},{2,18},{3,19},{4,20},{5,21},{6,22},{7,23},{8,24},{9,... | collective-permute-start | bytes 3612680 | tf_op jit(solution)/shard_map/ppermute | solution.py:101
  122.3 25.8 %collective-permute-start.32 = (bf16[2,392,768]{2,1,0:T(8,128)(2,1)}, bf16[2,392,768]{2,1,0:T(8,128)(2,1)}, u32[]{:S(2)}, u32[]{:S(2)}) collective-permute-start(bf16[2,392,768]{2,1,0:T(8,128)(2,1)} %get-tuple-element.405), channel_id=1, source_target_pairs={{0,16},{1,17},{2,18},{3,19},{4,20},{5,21},{6,22},{7,23},{8,24},{9,... | collective-permute-start | bytes 3612680 | tf_op jit(solution)/shard_map/ppermute | solution.py:101
  122.7 25.4 %collective-permute-start.29 = (bf16[4,48,1536]{2,1,0:T(8,128)(2,1)}, bf16[4,48,1536]{2,1,0:T(8,128)(2,1)}, u32[]{:S(2)}, u32[]{:S(2)}) collective-permute-start(bf16[4,48,1536]{2,1,0:T(8,128)(2,1)} %get-tuple-element.402), channel_id=1, source_target_pairs={{0,2},{1,3},{2,0},{3,1},{4,6},{5,7},{6,4},{7,5},{8,10},{9,11},{10,... | collective-permute-start | bytes 1769480 | tf_op jit(solution)/shard_map/ppermute | solution.py:97
  123.8 24.3 %collective-permute-start.30 = (bf16[4,48,1536]{2,1,0:T(8,128)(2,1)}, bf16[4,48,1536]{2,1,0:T(8,128)(2,1)}, u32[]{:S(2)}, u32[]{:S(2)}) collective-permute-start(bf16[4,48,1536]{2,1,0:T(8,128)(2,1)} %get-tuple-element.403), channel_id=1, source_target_pairs={{0,2},{1,3},{2,0},{3,1},{4,6},{5,7},{6,4},{7,5},{8,10},{9,11},{10,... | collective-permute-start | bytes 1769480 | tf_op jit(solution)/shard_map/ppermute | solution.py:97
  151.2 9.9 %collective-permute-start.34 = (bf16[4,48,1536]{2,1,0:T(8,128)(2,1)S(1)}, bf16[4,48,1536]{2,1,0:T(8,128)(2,1)S(1)}, u32[]{:S(2)}, u32[]{:S(2)}) collective-permute-start(bf16[4,48,1536]{2,1,0:T(8,128)(2,1)S(1)} %add_convert_fusion.3), channel_id=1, source_target_pairs={{0,1},{1,0},{2,3},{3,2},{4,5},{5,4},{6,7},{7,6},{8,9},{9,8},{10,11... | collective-permute-start | bytes 1769480 | tf_op jit(solution)/shard_map/ppermute | solution.py:97
  161.1 7.2 %collective-permute-start.36 = (bf16[2,392,768]{2,1,0:T(8,128)(2,1)S(1)}, bf16[2,392,768]{2,1,0:T(8,128)(2,1)S(1)}, u32[]{:S(2)}, u32[]{:S(2)}) collective-permute-start(bf16[2,392,768]{2,1,0:T(8,128)(2,1)S(1)} %copy-done.68), channel_id=1, source_target_pairs={{0,16},{1,17},{2,18},{3,19},{4,20},{5,21},{6,22},{7,23},{8,24},{9,... | collective-permute-start | bytes 3612680 | tf_op jit(solution)/shard_map/ppermute | solution.py:101
  168.9 19.2 %collective-permute-start.37 = (bf16[4,48,1536]{2,1,0:T(8,128)(2,1)}, bf16[4,48,1536]{2,1,0:T(8,128)(2,1)S(1)}, u32[]{:S(2)}, u32[]{:S(2)}) collective-permute-start(bf16[4,48,1536]{2,1,0:T(8,128)(2,1)} %get-tuple-element.449), channel_id=1, source_target_pairs={{0,2},{1,3},{2,0},{3,1},{4,6},{5,7},{6,4},{7,5},{8,10},{9,11},{10,... | collective-permute-start | bytes 1769480 | tf_op jit(solution)/shard_map/ppermute | solution.py:97
  170.1 18.0 %collective-permute-start.38 = (bf16[4,48,1536]{2,1,0:T(8,128)(2,1)S(1)}, bf16[4,48,1536]{2,1,0:T(8,128)(2,1)S(1)}, u32[]{:S(2)}, u32[]{:S(2)}) collective-permute-start(bf16[4,48,1536]{2,1,0:T(8,128)(2,1)S(1)} %copy-done.70), channel_id=1, source_target_pairs={{0,2},{1,3},{2,0},{3,1},{4,6},{5,7},{6,4},{7,5},{8,10},{9,11},{10,... | collective-permute-start | bytes 1769480 | tf_op jit(solution)/shard_map/ppermute | solution.py:97
  170.9 17.2 %collective-permute-start.42 = (bf16[16,48,384]{2,1,0:T(8,128)(2,1)S(1)}, bf16[16,48,384]{2,1,0:T(8,128)(2,1)S(1)}, u32[]{:S(2)}, u32[]{:S(2)}) collective-permute-start(bf16[16,48,384]{2,1,0:T(8,128)(2,1)S(1)} %get-tuple-element.454), channel_id=1, source_target_pairs={{0,16},{1,17},{2,18},{3,19},{4,20},{5,21},{6,22},{7,23},{8,24},{9,... | collective-permute-start | bytes 1769480 | tf_op jit(solution)/shard_map/ppermute | solution.py:101
  170.9 17.1 %collective-permute-start.40 = (bf16[1,48,1536]{2,1,0:T(8,128)(2,1)S(1)}, bf16[1,48,1536]{2,1,0:T(8,128)(2,1)S(1)}, u32[]{:S(2)}, u32[]{:S(2)}) collective-permute-start(bf16[1,48,1536]{2,1,0:T(8,128)(2,1)S(1)} %get-tuple-element.452), channel_id=1, source_target_pairs={{0,8},{1,9},{2,10},{3,11},{4,12},{5,13},{6,14},{7,15},{8,0},{9,1},... | collective-permute-start | bytes 442376 | tf_op jit(solution)/shard_map/ppermute | solution.py:97
  174.2 13.9 %collective-permute-start.41 = (bf16[1,48,1536]{2,1,0:T(8,128)(2,1)S(1)}, bf16[1,48,1536]{2,1,0:T(8,128)(2,1)S(1)}, u32[]{:S(2)}, u32[]{:S(2)}) collective-permute-start(bf16[1,48,1536]{2,1,0:T(8,128)(2,1)S(1)} %get-tuple-element.453), channel_id=1, source_target_pairs={{0,12},{1,13},{2,14},{3,15},{4,8},{5,9},{6,10},{7,11},{8,4},{9,5},... | collective-permute-start | bytes 442376 | tf_op jit(solution)/shard_map/ppermute | solution.py:97
  189.1 12.5 %collective-permute-start.43 = (bf16[4,48,1536]{2,1,0:T(8,128)(2,1)S(1)}, bf16[4,48,1536]{2,1,0:T(8,128)(2,1)S(1)}, u32[]{:S(2)}, u32[]{:S(2)}) collective-permute-start(bf16[4,48,1536]{2,1,0:T(8,128)(2,1)S(1)} %add_convert_fusion.1), channel_id=1, source_target_pairs={{0,1},{1,0},{2,3},{3,2},{4,5},{5,4},{6,7},{7,6},{8,9},{9,8},{10,11... | collective-permute-start | bytes 1769480 | tf_op jit(solution)/shard_map/ppermute | solution.py:97
  202.7 17.6 %collective-permute-start.44 = (bf16[8,48,1152]{2,1,0:T(8,128)(2,1)S(1)}, bf16[8,48,1152]{2,1,0:T(8,128)(2,1)S(1)}, u32[]{:S(2)}, u32[]{:S(2)}) collective-permute-start(bf16[8,48,1152]{2,1,0:T(8,128)(2,1)S(1)} %pad_maximum_fusion), channel_id=1, source_target_pairs={{0,2},{1,3},{2,0},{3,1},{4,6},{5,7},{6,4},{7,5},{8,10},{9,11},{10,... | collective-permute-start | bytes 2654216 | tf_op jit(solution)/shard_map/ppermute | solution.py:97
  203.6 16.6 %collective-permute-start.45 = (bf16[1,48,1536]{2,1,0:T(8,128)(2,1)S(1)}, bf16[1,48,1536]{2,1,0:T(8,128)(2,1)S(1)}, u32[]{:S(2)}, u32[]{:S(2)}) collective-permute-start(bf16[1,48,1536]{2,1,0:T(8,128)(2,1)S(1)} %get-tuple-element.482), channel_id=1, source_target_pairs={{0,4},{1,5},{2,6},{3,7},{4,0},{5,1},{6,2},{7,3},{8,12},{9,13},{10,... | collective-permute-start | bytes 442376 | tf_op jit(solution)/shard_map/ppermute | solution.py:97
  203.6 16.6 %collective-permute-start.46 = (bf16[1,48,1536]{2,1,0:T(8,128)(2,1)S(1)}, bf16[1,48,1536]{2,1,0:T(8,128)(2,1)S(1)}, u32[]{:S(2)}, u32[]{:S(2)}) collective-permute-start(bf16[1,48,1536]{2,1,0:T(8,128)(2,1)S(1)} %get-tuple-element.483), channel_id=1, source_target_pairs={{0,8},{1,9},{2,10},{3,11},{4,12},{5,13},{6,14},{7,15},{8,0},{9,1},... | collective-permute-start | bytes 442376 | tf_op jit(solution)/shard_map/ppermute | solution.py:97
  205.7 14.5 %collective-permute-start.47 = (bf16[1,48,1536]{2,1,0:T(8,128)(2,1)S(1)}, bf16[1,48,1536]{2,1,0:T(8,128)(2,1)S(1)}, u32[]{:S(2)}, u32[]{:S(2)}) collective-permute-start(bf16[1,48,1536]{2,1,0:T(8,128)(2,1)S(1)} %get-tuple-element.484), channel_id=1, source_target_pairs={{0,12},{1,13},{2,14},{3,15},{4,8},{5,9},{6,10},{7,11},{8,4},{9,5},... | collective-permute-start | bytes 442376 | tf_op jit(solution)/shard_map/ppermute | solution.py:97
  220.4 10.1 %collective-permute-start.49 = (bf16[4,48,1152]{2,1,0:T(8,128)(2,1)S(1)}, bf16[4,48,1152]{2,1,0:T(8,128)(2,1)S(1)}, u32[]{:S(2)}, u32[]{:S(2)}) collective-permute-start(bf16[4,48,1152]{2,1,0:T(8,128)(2,1)S(1)} %add_convert_fusion.4), channel_id=1, source_target_pairs={{0,1},{1,0},{2,3},{3,2},{4,5},{5,4},{6,7},{7,6},{8,9},{9,8},{10,11... | collective-permute-start | bytes 1327112 | tf_op jit(solution)/shard_map/ppermute | solution.py:97
  221.3 9.2 %collective-permute-start.48 = (bf16[8,48,384]{2,1,0:T(8,128)(2,1)S(1)}, bf16[8,48,384]{2,1,0:T(8,128)(2,1)S(1)}, u32[]{:S(2)}, u32[]{:S(2)}) collective-permute-start(bf16[8,48,384]{2,1,0:T(8,128)(2,1)S(1)} %get-tuple-element.499), channel_id=1, source_target_pairs={{0,2},{1,3},{2,0},{3,1},{4,6},{5,7},{6,4},{7,5},{8,10},{9,11},{10,... | collective-permute-start | bytes 884744 | tf_op jit(solution)/shard_map/ppermute | solution.py:97
  239.5 8.0 %collective-permute-start.52 = (f32[48,3072]{1,0:T(8,128)S(1)}, f32[48,3072]{1,0:T(8,128)S(1)}, u32[]{:S(2)}, u32[]{:S(2)}) collective-permute-start(f32[48,3072]{1,0:T(8,128)S(1)} %pad_maximum_fusion.6.refs_1_), channel_id=1, source_target_pairs={{0,16},{1,17},{2,18},{3,19},{4,20},{5,21},{6,22},{7,23},{8,24},{9,... | collective-permute-start | bytes 1769480 | tf_op jit(solution)/shard_map/ppermute | solution.py:101
  239.8 9.8 %collective-permute-start.53 = (bf16[1,48,1536]{2,1,0:T(8,128)(2,1)S(1)}, bf16[1,48,1536]{2,1,0:T(8,128)(2,1)S(1)}, u32[]{:S(2)}, u32[]{:S(2)}) collective-permute-start(bf16[1,48,1536]{2,1,0:T(8,128)(2,1)S(1)} %get-tuple-element.545), channel_id=1, source_target_pairs={{0,4},{1,5},{2,6},{3,7},{4,0},{5,1},{6,2},{7,3},{8,12},{9,13},{10,... | collective-permute-start | bytes 442376 | tf_op jit(solution)/shard_map/ppermute | solution.py:97
  239.9 14.0 %collective-permute-start.54 = (bf16[1,48,1536]{2,1,0:T(8,128)(2,1)S(1)}, bf16[1,48,1536]{2,1,0:T(8,128)(2,1)S(1)}, u32[]{:S(2)}, u32[]{:S(2)}) collective-permute-start(bf16[1,48,1536]{2,1,0:T(8,128)(2,1)S(1)} %get-tuple-element.546), channel_id=1, source_target_pairs={{0,8},{1,9},{2,10},{3,11},{4,12},{5,13},{6,14},{7,15},{8,0},{9,1},... | collective-permute-start | bytes 442376 | tf_op jit(solution)/shard_map/ppermute | solution.py:97
  241.8 12.1 %collective-permute-start.55 = (bf16[1,48,1536]{2,1,0:T(8,128)(2,1)S(1)}, bf16[1,48,1536]{2,1,0:T(8,128)(2,1)S(1)}, u32[]{:S(2)}, u32[]{:S(2)}) collective-permute-start(bf16[1,48,1536]{2,1,0:T(8,128)(2,1)S(1)} %pad_maximum_fusion.10), channel_id=1, source_target_pairs={{0,12},{1,13},{2,14},{3,15},{4,8},{5,9},{6,10},{7,11},{8,4},{9,5},... | collective-permute-start | bytes 442376 | tf_op jit(solution)/shard_map/ppermute | solution.py:97
  259.1 13.1 %collective-permute-start.63 = (f32[48,1536]{1,0:T(8,128)S(1)}, f32[48,1536]{1,0:T(8,128)S(1)}, u32[]{:S(2)}, u32[]{:S(2)}) collective-permute-start(f32[48,1536]{1,0:T(8,128)S(1)} %get-tuple-element.557.refs_2_), channel_id=1, source_target_pairs={{0,16},{1,17},{2,18},{3,19},{4,20},{5,21},{6,22},{7,23},{8,24},{9,... | collective-permute-start | bytes 884744 | tf_op jit(solution)/shard_map/ppermute | solution.py:101
  (89 other events, 748.3 us)
